TPU v7x, 256 devices: a whole 4x4x8 slice. The times are simulated.
256 devices in a mesh: dp: 32 (over y, x, core), tensor: 8 (over z).
Axes of the slice: x: 4, y: 4, z: 8, core: 2. Of those that a mesh axis runs over, the one named last changes fastest.
Arguments:
- grads: bfloat16 [32, 1024, 12288], P('dp', None, 'tensor'), may hold values from -6 to 6
- errors: bfloat16 [32, 1024, 12288], P('dp', None, 'tensor'), may hold values from -4 to 4
- q_prev: float32 [12288, 64], P('tensor'), may hold values from -6 to 6
Outputs:
- update: bfloat16 [1024, 12288], P('dp', 'tensor')
- q_new: float32 [12288, 64], P('tensor')
- new_errors: bfloat16 [32, 1024, 12288], P('dp', None, 'tensor')
All inputs are finite; a program needn't handle non-finite values.
Results may differ from a plain program's by a relative error of at most 0.012.
Values may be sent and summed in bfloat16 or wider, within the bound.
No kernel may reach another device: no remote copies, remote signals or barrier semaphores. Data moves between devices by JAX's collectives and lax.ppermute only.
A program may use at most 64 MiB of HBM per device.

v0:
```python
import jax
import jax.numpy as jnp
from jax import lax
from jax.sharding import PartitionSpec as P


def orthonormal(left_sum, factor):
    return jax.scipy.linalg.solve_triangular(factor, left_sum.T, lower=True).T.astype(jnp.bfloat16)


def per_device(grads, errors, q_prev):
    replicas = lax.axis_size("dp")
    merged = (grads[0].astype(jnp.float32) + errors[0].astype(jnp.float32)).astype(jnp.bfloat16)
    prior_cast = q_prev.astype(jnp.bfloat16)
    partial_left = jnp.dot(merged, prior_cast, preferred_element_type=jnp.float32)
    left_sum = lax.psum(partial_left, ("dp", "tensor")) / replicas
    gram_matrix = jnp.dot(left_sum.T, left_sum, precision=lax.Precision.HIGHEST)
    ortho_left = orthonormal(left_sum, jnp.linalg.cholesky(gram_matrix))
    partial_right = lax.dot_general(
        merged, ortho_left, (((0,), (0,)), ((), ())), preferred_element_type=jnp.float32
    )
    q_new = lax.psum(partial_right, "dp") / replicas
    full_update = jnp.dot(
        ortho_left, q_new.astype(jnp.bfloat16).T, preferred_element_type=jnp.float32
    )
    new_errors = (merged.astype(jnp.float32) - full_update).astype(jnp.bfloat16)[None]
    row_count = full_update.shape[0] // replicas
    row_start = lax.axis_index("dp") * row_count
    update = lax.dynamic_slice_in_dim(full_update, row_start, row_count, 0).astype(jnp.bfloat16)
    return (update, q_new, new_errors)


def solution(mesh):
    placed = (P("dp", None, "tensor"), P("dp", None, "tensor"), P("tensor", None))
    return jax.shard_map(
        per_device,
        mesh=mesh,
        in_specs=placed,
        out_specs=(P("dp", "tensor"), P("tensor", None), P("dp", None, "tensor")),
        check_vma=False,
    )
```

profile of v0, /device:TPU:1, one launch (start us, length us, event | category | flops | bytes accessed | tf_op | source)
XLA Modules:
  0.0 411.8 jit_solution(10880885257899631858)
XLA Ops:
  7.2 0.0 copy-start
  7.2 0.0 all-reduce.3.cloned.1.call-start
  7.2 4.8 %fusion.7 = f32[1024,64]{0,1:T(8,128)} fusion(f32[1536,64]{0,1:T(8,128)} %param.5, bf16[1,1024,1536]{2,1,0:T(8,128)(2,1)} %param.4, bf16[1,1024,1536]{2,1,0:T(8,128)(2,1)} %param.3), kind=kOutput, calls=%fused_computation.12 | convolution fusion | flops 207716352 | bytes 6946816 | tf_op jit(solution)/shard_map/dot_general | solution.py:15
  12.0 0.0 all-reduce.3.cloned.1.call-update
  12.0 0.0 all-reduce.5.cloned.1.call-start
  12.1 254.6 %all-reduce.3.cloned.1.call-done = f32[1024,64]{0,1:T(8,128)} async-done(((f32[1024,64]{0,1:T(8,128)}), f32[1024,64]{0,1:T(8,128)}) %all-reduce.3.cloned.1.call-update) | async-done | bytes 262160 | tf_op jit(solution)/shard_map/psum | solution.py:16
  266.6 1.4 fusion.3
  268.0 0.1 copy.6
  268.1 5.8 %cholesky.16 = f32[64,64]{1,0:T(8,128)S(1)} custom-call(f32[64,64]{1,0:T(8,128)S(1)} %fusion.13), custom_call_target="Cholesky" | custom-call | tf_op jit(solution)/shard_map/jit(cholesky)/cholesky | solution.py:18
  274.0 0.6 compare_reduce_fusion
  274.7 0.7 fusion.11
  275.3 4.9 %custom-call.7 = f32[1,64,64]{1,2,0:T(8,128)S(1)} custom-call(f32[1,64,64]{2,1,0:T(8,128)S(1)} %fusion.11), custom_call_target="InvertDiagBlocksLowerTriangular" | custom-call | tf_op jit(solution)/shard_map/jit(_solve_triangular)/triangular_solve | solution.py:8
  280.2 1.4 convolution_convert_fusion
  281.6 0.0 copy-done
  281.6 3.6 fusion.16
  285.2 0.0 all-reduce.5.cloned.1.call-update
  285.2 112.9 %all-reduce.5.cloned.1.call-done = f32[1536,64]{0,1:T(8,128)} async-done(((f32[1536,64]{0,1:T(8,128)}), f32[1536,64]{0,1:T(8,128)}) %all-reduce.5.cloned.1.call-update) | async-done | bytes 393232 | tf_op jit(solution)/shard_map/psum | solution.py:22
  398.2 1.0 broadcast_multiply_fusion
  399.2 0.0 copy-start.2
  399.2 0.0 copy-start.1
  399.2 1.0 fusion.5
  400.2 0.0 copy-done.2
  400.2 1.0 copy-done.1
  401.2 3.1 fusion.1
  404.4 0.7 dynamic-slice_convert_fusion
  (2 shorter events, 0.0 us)
Async XLA Ops:
  7.2 274.4 %copy-start = (bf16[1,1024,1536]{2,1,0:T(8,128)(2,1)S(1)}, bf16[1,1024,1536]{2,1,0:T(8,128)(2,1)}, u32[]{:S(2)}) copy-start(bf16[1,1024,1536]{2,1,0:T(8,128)(2,1)} %param.4) | copy-start | bytes 9437188
  7.2 259.5 %all-reduce.3.cloned.1.call-start = ((), (), s32[]{:S(2)}) async-start(), calls=%async_computation | async-start | bytes 524288 | tf_op jit(solution)/shard_map/psum | solution.py:16
  12.0 386.1 %all-reduce.5.cloned.1.call-start = ((), (), s32[]{:S(2)}) async-start(), calls=%async_computation.1 | async-start | bytes 786432 | tf_op jit(solution)/shard_map/psum | solution.py:22
  399.2 1.0 copy-start.2
  399.2 2.0 copy-start.1
Sparse Core Ops, SparseCore 0:
  14.0 252.5 all-reduce.2
  285.4 112.7 all-reduce.4
where the time goes:
time: 412 us
  waiting for transfers between devices  368 us (89%)
  other arithmetic  16.2 us (4%)
  between operations  14.1 us (3%)
  matrix products  12.1 us (3%)
    psum x1, waiting for transfers between devices, per_device(): left_sum = lax.psum(partial_left, ('dp', 'tensor')) / replicas  255 us
    psum x1, waiting for transfers between devices, per_device(): q_new = lax.psum(partial_right, 'dp') / replicas  113 us
  transfers between devices with their start and end apart: 2, of which 2 were waited for; matrix products, arithmetic and copies ran while one was open for 0% of the time, Pallas kernels for 0%

commit v1 on v0

v1 whole, which is shorter than its diff:
```python
import jax
import jax.numpy as jnp
from jax import lax
from jax.sharding import Mesh, PartitionSpec as P

YX = ("y", "x")


def swap_cores(value):
    return lax.ppermute(value, "core", [(0, 1), (1, 0)])


def exchange(value, axes):
    return lax.all_to_all(value, axes, 0, 0)


def spread(value, copies):
    return jnp.broadcast_to(value[None], (copies,) + value.shape)


def per_device(grads, errors, q_prev):
    core = lax.axis_index("core")
    pairs = lax.axis_size("y") * lax.axis_size("x")
    depth = lax.axis_size("z")
    replicas = 2 * pairs
    merged = (grads[0].astype(jnp.float32) + errors[0].astype(jnp.float32)).astype(jnp.bfloat16)
    prior_cast = q_prev.astype(jnp.bfloat16)
    rows, columns = merged.shape
    rank = prior_cast.shape[1]

    def halves(total):
        total = total.reshape(2, -1, *total.shape[1:])
        keep = lax.dynamic_index_in_dim(total, core, 0, keepdims=False)
        give = lax.dynamic_index_in_dim(total, 1 - core, 0, keepdims=False)
        return keep + swap_cores(give)

    def joined(half):
        other = swap_cores(half)
        return jnp.where(core == 0, jnp.concatenate([half, other]), jnp.concatenate([other, half]))

    partial_left = lax.dot_general(
        prior_cast, merged, (((0,), (1,)), ((), ())), preferred_element_type=jnp.float32
    )
    tiles = partial_left.reshape(rank // 16, 16, rows // 128, 128).transpose(0, 2, 1, 3)
    tiles = tiles.reshape(-1, 16, 128)
    mine = jnp.sum(exchange(halves(tiles), YX), axis=0)
    mine = jnp.sum(exchange(spread(mine, depth), "z"), axis=0) / replicas
    left = joined(exchange(spread(mine, pairs), YX))
    left = left.reshape(rank // 16, rows // 128, 16, 128).transpose(0, 2, 1, 3).reshape(rank, rows)

    gram_matrix = lax.dot_general(
        left, left, (((1,), (1,)), ((), ())), precision=lax.Precision.HIGHEST
    )
    factor = jnp.linalg.cholesky(gram_matrix)
    ortho = jax.scipy.linalg.solve_triangular(factor, left, lower=True).astype(jnp.bfloat16)

    partial_right = jnp.dot(ortho, merged, preferred_element_type=jnp.float32)
    wide = rank * columns // (8 * replicas)
    tiles = partial_right.reshape(rank // 8, 8, columns // wide, wide).transpose(0, 2, 1, 3)
    tiles = tiles.reshape(-1, 8, wide)
    mine = jnp.sum(exchange(halves(tiles), YX), axis=0) / replicas
    right = joined(exchange(spread(mine, pairs), YX))
    right = right.reshape(rank // 8, columns // wide, 8, wide).transpose(0, 2, 1, 3)
    right = right.reshape(rank, columns)

    full_update = lax.dot_general(
        ortho, right.astype(jnp.bfloat16), (((0,), (0,)), ((), ())),
        preferred_element_type=jnp.float32,
    )
    new_errors = (merged.astype(jnp.float32) - full_update).astype(jnp.bfloat16)[None]
    row_count = rows // replicas
    row_start = lax.axis_index(("y", "x", "core")) * row_count
    update = lax.dynamic_slice_in_dim(full_update, row_start, row_count, 0).astype(jnp.bfloat16)
    return update, right.T, new_errors


def solution(mesh):
    chips = Mesh(mesh.devices.reshape(4, 4, 2, 8), ("y", "x", "core", "z"))
    dp = ("y", "x", "core")
    placed = (P(dp, None, "z"), P(dp, None, "z"), P("z", None))
    return jax.shard_map(
        per_device,
        mesh=chips,
        in_specs=placed,
        out_specs=(P(dp, "z"), P("z", None), P(dp, None, "z")),
        check_vma=False,
    )
```

time: 412 us -> 111 us (0.27)
  waiting for transfers between devices: 368 us -> 3.83 us
  blocking collectives: 0 us -> 57.2 us
  between operations: 14.1 us -> 0.82 us
  starting transfers between devices: 0.08 us -> 10.4 us
  local copies, waits for them, and re-layouts: 1.75 us -> 7.3 us
  other arithmetic: 16.2 us -> 21.4 us
    psum x2 -> x0, waiting for transfers between devices: 367 us -> none  [the longest x1 255 us: per_device(): left_sum = lax.psum(partial_left, ('dp', 'tensor')) / replicas]
    all_to_all x0 -> x5, blocking collectives: none -> 57.2 us  [exchange(): return lax.all_to_all(value, axes, 0, 0)]
    ppermute x0 -> x4, starting transfers between devices: none -> 10.4 us  [swap_cores(): return lax.ppermute(value, 'core', [(0, 1), (1, 0)])]
    dot_general x1 -> x2, local copies, waits for them, and re-layouts: 0.07 us -> 4.72 us  [the longest x1 4.64 us: per_device(): partial_right = jnp.dot(ortho, merged, preferred_element_type=jnp.float32)]
    dot_general x0 -> x1, other arithmetic: none -> 4.39 us  [per_device(): partial_right = jnp.dot(ortho, merged, preferred_element_type=jnp.float32)]
  transfers between devices with their start and end apart: 2 -> 4, of which waited for: 2 -> 3; matrix products, arithmetic and copies ran while one was open for 0% -> 8% of each run, Pallas kernels for 0% -> 0%
where the time goes in v1:
time: 111 us; the launch traced here: 110 us
  blocking collectives  57.2 us (52%)
  other arithmetic  21.4 us (19%)
  starting transfers between devices  10.4 us (9%)
  matrix products  9.57 us (9%)
  local copies, waits for them, and re-layouts  7.3 us (7%)
  waiting for transfers between devices  3.83 us (3%)
    all_to_all x5, blocking collectives, exchange(): return lax.all_to_all(value, axes, 0, 0)  57.2 us
    ppermute x4, starting transfers between devices, swap_cores(): return lax.ppermute(value, 'core', [(0, 1), (1, 0)])  10.4 us
    another operation x3, other arithmetic, per_device(): factor = jnp.linalg.cholesky(gram_matrix)  6.52 us
    another operation x2, other arithmetic, per_device(): jax.scipy.linalg.solve_triangular(factor, left, lower=True)  6.18 us
    dot_general x1, local copies, waits for them, and re-layouts, per_device(): partial_right = jnp.dot(ortho, merged, preferred_element_type=jnp.float32)  4.64 us
    dot_general x1, other arithmetic, per_device(): partial_right = jnp.dot(ortho, merged, preferred_element_type=jnp.float32)  4.39 us
    dot_general x1, matrix products, per_device(): lax.dot_general(prior_cast, merged, (((0,), (1,)), ((), ())), preferred_e...  4.06 us
    ppermute x4, waiting for transfers between devices, swap_cores(): return lax.ppermute(value, 'core', [(0, 1), (1, 0)])  3.83 us
  transfers between devices with their start and end apart: 4, of which 3 were waited for; matrix products, arithmetic and copies ran while one was open for 8% of the time, Pallas kernels for 0%

profile of v1, /device:TPU:1, one launch (start us, length us, event | category | flops | bytes accessed | tf_op | source)
XLA Modules:
  0.0 110.5 jit_solution(2153766597447414260)
XLA Ops:
  0.6 0.0 copy-start
  0.6 4.1 %fusion.3 = f32[8,8,8,128]{3,1,2,0:T(8,128)S(1)} fusion(f32[1536,64]{0,1:T(8,128)} %param.5, bf16[1,1024,1536]{2,1,0:T(8,128)(2,1)} %param.4, bf16[1,1024,1536]{2,1,0:T(8,128)(2,1)} %param.3), kind=kOutput, calls=%fused_computation.5 | convolution fusion | flops 207716352 | bytes 6946816 | tf_op jit(solution)/shard_map/dot_general | solution.py:41
  4.8 0.7 dynamic-slice_bitcast_fusion.1
  5.5 3.2 %collective-permute-start = (f32[16,16,128]{2,1,0:T(8,128)}, f32[16,16,128]{2,1,0:T(8,128)S(1)}, u32[]{:S(2)}, u32[]{:S(2)}) collective-permute-start(f32[16,16,128]{2,1,0:T(8,128)} %dynamic-slice_bitcast_fusion.1), channel_id=1, source_target_pairs={{0,8},{8,0},{1,9},{9,1},{2,10},{10,2},{3,11},{11,3},{4,12},{12,4},... | collective-permute-start | bytes 393224 | tf_op jit(solution)/shard_map/ppermute | solution.py:10
  8.7 1.2 %collective-permute-done = f32[16,16,128]{2,1,0:T(8,128)S(1)} collective-permute-done((f32[16,16,128]{2,1,0:T(8,128)}, f32[16,16,128]{2,1,0:T(8,128)S(1)}, u32[]{:S(2)}, u32[]{:S(2)}) %collective-permute-start) | collective-permute-done | bytes 131104 | tf_op jit(solution)/shard_map/ppermute | solution.py:10
  10.0 11.7 %all_to_all.25 = f32[16,16,128]{2,1,0:T(8,128)S(1)} all-to-all(f32[16,16,128]{2,1,0:T(8,128)S(1)} %bitcast_add_fusion.1), channel_id=1, replica_groups=mesh['y'=4,'x'=4,'core'=2,'z'=8] {'y','x'}, dimensions={0} | all-to-all | bytes 262144 | tf_op jit(solution)/shard_map/all_to_all | solution.py:14
  21.7 15.2 %all_to_all.26 = f32[8,16,128]{2,1,0:T(8,128)S(1)} all-to-all(f32[8,16,128]{2,1,0:T(8,128)S(1)} %broadcast_in_dim.10), channel_id=1, replica_groups=mesh['y'=4,'x'=4,'core'=2,'z'=8] {'z'}, dimensions={0} | all-to-all | bytes 131072 | tf_op jit(solution)/shard_map/all_to_all | solution.py:14
  36.9 10.0 %all_to_all.27 = f32[16,16,128]{2,1,0:T(8,128)S(1)} all-to-all(f32[16,16,128]{2,1,0:T(8,128)S(1)} %broadcast_in_dim.11), channel_id=1, replica_groups=mesh['y'=4,'x'=4,'core'=2,'z'=8] {'y','x'}, dimensions={0} | all-to-all | bytes 262144 | tf_op jit(solution)/shard_map/all_to_all | solution.py:14
  46.9 4.3 %collective-permute-start.1 = (f32[16,16,128]{2,1,0:T(8,128)S(1)}, f32[16,16,128]{2,1,0:T(8,128)S(1)}, u32[]{:S(2)}, u32[]{:S(2)}) collective-permute-start(f32[16,16,128]{2,1,0:T(8,128)S(1)} %all_to_all.27), channel_id=1, source_target_pairs={{0,8},{8,0},{1,9},{9,1},{2,10},{10,2},{3,11},{11,3},{4,12},{12,4},... | collective-permute-start | bytes 393224 | tf_op jit(solution)/shard_map/ppermute | solution.py:10
  51.2 0.0 copy-done
  51.2 4.4 %fusion.19 = bf16[1536,1024]{0,1:T(8,128)(2,1)} fusion(bf16[1,1024,1536]{2,1,0:T(8,128)(2,1)S(1)} %copy-done, bf16[1,1024,1536]{2,1,0:T(8,128)(2,1)} %param.3), kind=kLoop, calls=%fused_computation.35 | loop fusion | flops 6291456 | bytes 9437184 | tf_op jit(solution)/shard_map/dot_general | solution.py:57
  55.6 4.6 %copy.20 = bf16[1536,1024]{1,0:T(8,128)(2,1)} copy(bf16[1536,1024]{0,1:T(8,128)(2,1)} %fusion.19) | data formatting | bytes 6291456 | tf_op jit(solution)/shard_map/dot_general | solution.py:57
  60.2 0.0 collective-permute-done.1
  60.3 0.1 copy.16
  60.3 0.4 fusion.7
  60.7 0.1 copy.17
  60.8 5.8 %cholesky.16 = f32[64,64]{1,0:T(8,128)S(1)} custom-call(f32[64,64]{1,0:T(8,128)S(1)} %fusion.18), custom_call_target="Cholesky" | custom-call | tf_op jit(solution)/shard_map/jit(cholesky)/cholesky | solution.py:54
  66.7 0.6 compare_reduce_fusion
  67.3 0.7 fusion.16
  68.0 5.5 %custom-call.7 = f32[1,64,64]{1,2,0:T(8,128)} custom-call(f32[1,64,64]{2,1,0:T(8,128)S(1)} %fusion.16), custom_call_target="InvertDiagBlocksLowerTriangular" | custom-call | tf_op jit(solution)/shard_map/jit(_solve_triangular)/triangular_solve | solution.py:55
  73.5 1.2 %convolution_convert_fusion = bf16[64,1024]{1,0:T(8,128)(2,1)S(1)} fusion(f32[8,8,8,128]{3,2,1,0:T(8,128)S(1)} %bitcast.70, f32[1,64,64]{1,2,0:T(8,128)} %custom-call.7), kind=kOutput, calls=%fused_computation.6 | convolution fusion | flops 50397184 | bytes 409600 | tf_op jit(solution)/shard_map/jit(_solve_triangular)/triangular_solve | solution.py:55
  74.7 3.0 %fusion.14 = f32[8,8,4,384]{3,1,2,0:T(8,128)S(1)} fusion(bf16[4,384,1024,1]{2,1,0,3:T(8,128)(2,1)} %bitcast.68, bf16[64,1024]{1,0:T(8,128)(2,1)S(1)} %convolution_convert_fusion), kind=kOutput, calls=%fused_computation.20 | convolution fusion | flops 201326592 | bytes 3670016 | tf_op jit(solution)/shard_map/dot_general | solution.py:57
  77.7 0.1 collective-permute-start.2
  77.8 1.4 %collective-permute-done.2 = f32[16,8,384]{2,1,0:T(8,128)S(1)} collective-permute-done((f32[16,8,384]{2,1,0:T(8,128)S(1)}, f32[16,8,384]{2,1,0:T(8,128)S(1)}, u32[]{:S(2)}, u32[]{:S(2)}) %collective-permute-start.2) | collective-permute-done | bytes 196640 | tf_op jit(solution)/shard_map/ppermute | solution.py:10
  79.3 10.5 %all_to_all.28 = f32[16,8,384]{2,1,0:T(8,128)S(1)} all-to-all(f32[16,8,384]{2,1,0:T(8,128)S(1)} %bitcast_add_fusion), channel_id=1, replica_groups=mesh['y'=4,'x'=4,'core'=2,'z'=8] {'y','x'}, dimensions={0} | all-to-all | bytes 393216 | tf_op jit(solution)/shard_map/all_to_all | solution.py:14
  89.8 9.8 %all_to_all.29 = f32[16,8,384]{2,1,0:T(8,128)S(1)} all-to-all(f32[16,8,384]{2,1,0:T(8,128)S(1)} %broadcast_in_dim.12), channel_id=1, replica_groups=mesh['y'=4,'x'=4,'core'=2,'z'=8] {'y','x'}, dimensions={0} | all-to-all | bytes 393216 | tf_op jit(solution)/shard_map/all_to_all | solution.py:14
  99.6 2.8 %collective-permute-start.3 = (f32[16,8,384]{2,1,0:T(8,128)S(1)}, f32[16,8,384]{2,1,0:T(8,128)}, u32[]{:S(2)}, u32[]{:S(2)}) collective-permute-start(f32[16,8,384]{2,1,0:T(8,128)S(1)} %all_to_all.29), channel_id=1, source_target_pairs={{0,8},{8,0},{1,9},{9,1},{2,10},{10,2},{3,11},{11,3},{4,12},{12,4},... | collective-permute-start | bytes 589832 | tf_op jit(solution)/shard_map/ppermute | solution.py:10
  102.4 1.2 %collective-permute-done.3 = f32[16,8,384]{2,1,0:T(8,128)} collective-permute-done((f32[16,8,384]{2,1,0:T(8,128)S(1)}, f32[16,8,384]{2,1,0:T(8,128)}, u32[]{:S(2)}, u32[]{:S(2)}) %collective-permute-start.3) | collective-permute-done | bytes 196640 | tf_op jit(solution)/shard_map/ppermute | solution.py:10
  103.6 1.1 maximum_select_fusion
  104.6 0.0 copy-start.2
  104.6 0.0 copy-start.1
  104.7 1.0 fusion.11
  105.7 0.0 copy-done.2
  105.7 1.0 copy-done.1
  106.7 3.1 %fusion = bf16[1,1024,1536]{2,1,0:T(8,128)(2,1)} fusion(f32[1024,1536]{1,0:T(8,128)S(1)} %fusion.11, bf16[1,1024,1536]{2,1,0:T(8,128)(2,1)S(1)} %copy-done, bf16[1,1024,1536]{2,1,0:T(8,128)(2,1)S(1)} %copy-done.1), kind=kLoop, calls=%fused_computation.2 | loop fusion | flops 11010048 | bytes 15728640 | tf_op jit(solution)/shard_map/broadcast_in_dim | solution.py:70
  109.8 0.7 dynamic-slice_convert_fusion
  (16 shorter events, 0.3 us)
Async XLA Ops:
  0.6 50.6 %copy-start = (bf16[1,1024,1536]{2,1,0:T(8,128)(2,1)S(1)}, bf16[1,1024,1536]{2,1,0:T(8,128)(2,1)}, u32[]{:S(2)}) copy-start(bf16[1,1024,1536]{2,1,0:T(8,128)(2,1)} %param.4) | copy-start | bytes 9437188
  5.5 4.4 %collective-permute-start = (f32[16,16,128]{2,1,0:T(8,128)}, f32[16,16,128]{2,1,0:T(8,128)S(1)}, u32[]{:S(2)}, u32[]{:S(2)}) collective-permute-start(f32[16,16,128]{2,1,0:T(8,128)} %dynamic-slice_bitcast_fusion.1), channel_id=1, source_target_pairs={{0,8},{8,0},{1,9},{9,1},{2,10},{10,2},{3,11},{11,3},{4,12},{12,4},... | collective-permute-start | bytes 393224 | tf_op jit(solution)/shard_map/ppermute | solution.py:10
  46.9 13.3 %collective-permute-start.1 = (f32[16,16,128]{2,1,0:T(8,128)S(1)}, f32[16,16,128]{2,1,0:T(8,128)S(1)}, u32[]{:S(2)}, u32[]{:S(2)}) collective-permute-start(f32[16,16,128]{2,1,0:T(8,128)S(1)} %all_to_all.27), channel_id=1, source_target_pairs={{0,8},{8,0},{1,9},{9,1},{2,10},{10,2},{3,11},{11,3},{4,12},{12,4},... | collective-permute-start | bytes 393224 | tf_op jit(solution)/shard_map/ppermute | solution.py:10
  77.7 1.5 %collective-permute-start.2 = (f32[16,8,384]{2,1,0:T(8,128)S(1)}, f32[16,8,384]{2,1,0:T(8,128)S(1)}, u32[]{:S(2)}, u32[]{:S(2)}) collective-permute-start(f32[16,8,384]{2,1,0:T(8,128)S(1)} %dynamic-slice_bitcast_fusion), channel_id=1, source_target_pairs={{0,8},{8,0},{1,9},{9,1},{2,10},{10,2},{3,11},{11,3},{4,12},{12,4},... | collective-permute-start | bytes 589832 | tf_op jit(solution)/shard_map/ppermute | solution.py:10
  99.6 4.0 %collective-permute-start.3 = (f32[16,8,384]{2,1,0:T(8,128)S(1)}, f32[16,8,384]{2,1,0:T(8,128)}, u32[]{:S(2)}, u32[]{:S(2)}) collective-permute-start(f32[16,8,384]{2,1,0:T(8,128)S(1)} %all_to_all.29), channel_id=1, source_target_pairs={{0,8},{8,0},{1,9},{9,1},{2,10},{10,2},{3,11},{11,3},{4,12},{12,4},... | collective-permute-start | bytes 589832 | tf_op jit(solution)/shard_map/ppermute | solution.py:10
  104.6 1.0 copy-start.2
  104.6 2.0 %copy-start.1 = (bf16[1,1024,1536]{2,1,0:T(8,128)(2,1)S(1)}, bf16[1,1024,1536]{2,1,0:T(8,128)(2,1)}, u32[]{:S(2)}) copy-start(bf16[1,1024,1536]{2,1,0:T(8,128)(2,1)} %param.3) | copy-start | bytes 9437188

commit v2 on v0

v2 whole, which is shorter than its diff:
```python
import jax
import jax.numpy as jnp
from jax import lax
from jax.experimental import pallas as pl
from jax.experimental.pallas import tpu as pltpu
from jax.sharding import Mesh, PartitionSpec as P

YX = ("y", "x")
VMEM_LIMIT = 48 * 1024 * 1024
WHOLE = pl.BlockSpec(memory_space=pltpu.VMEM)
SCALAR = pl.BlockSpec(memory_space=pltpu.SMEM)
BLOCK_ROWS = 256


def own_first(core, low, high):
    return jnp.where(core == 0, low, high), jnp.where(core == 0, high, low)


def merge_kernel(core_ref, grads_ref, errors_ref, prior_ref, merged_ref, keep_ref, give_ref):
    step = pl.program_id(0)
    merged = (grads_ref[...].astype(jnp.float32) + errors_ref[...].astype(jnp.float32)).astype(
        jnp.bfloat16
    )
    merged_ref[...] = merged
    left = lax.dot_general(
        prior_ref[...].astype(jnp.bfloat16), merged, (((1,), (1,)), ((), ())),
        preferred_element_type=jnp.float32,
    )
    rank, rows = left.shape
    keep, give = own_first(core_ref[0], left[: rank // 2], left[rank // 2 :])
    lanes = rows // 128
    across = keep_ref.shape[0] // (rank // 32)
    for down in range(rank // 32):
        for lane in range(lanes):
            place = down * across + step * lanes + lane
            tile = (slice(16 * down, 16 * down + 16), slice(128 * lane, 128 * lane + 128))
            keep_ref[place] = keep[tile]
            give_ref[place] = give[tile]


def merge(core, grads, errors, prior):
    rows, columns = grads.shape
    rank = prior.shape[0]
    tiles = jax.ShapeDtypeStruct((rows // 128 * (rank // 32), 16, 128), jnp.float32)
    block = pl.BlockSpec((BLOCK_ROWS, columns), lambda i: (i, 0))
    fixed = pl.BlockSpec(tiles.shape, lambda i: (0, 0, 0))
    return pl.pallas_call(
        merge_kernel,
        grid=(rows // BLOCK_ROWS,),
        in_specs=[SCALAR, block, block, pl.BlockSpec(prior.shape, lambda i: (0, 0))],
        out_specs=[block, fixed, fixed],
        out_shape=[jax.ShapeDtypeStruct(grads.shape, jnp.bfloat16), tiles, tiles],
        compiler_params=pltpu.CompilerParams(vmem_limit_bytes=VMEM_LIMIT),
        cost_estimate=pl.CostEstimate(
            flops=2 * rows * columns * rank, bytes_accessed=6 * rows * columns, transcendentals=0
        ),
    )(core, grads, errors, prior)


def inverse_factor(gram):
    rank = gram.shape[0]
    row = lax.broadcasted_iota(jnp.int32, (rank, rank), 0)
    column = lax.broadcasted_iota(jnp.int32, (rank, rank), 1)
    state = jnp.concatenate([gram, jnp.where(row == column, 1.0, 0.0)], axis=1)
    groups = [state[8 * g : 8 * g + 8] for g in range(rank // 8)]
    below = lax.broadcasted_iota(jnp.int32, (8, 2 * rank), 0)
    for k in range(rank):
        own, place = k // 8, k % 8
        pivot_row = groups[own][place : place + 1]
        scale = lax.rsqrt(pivot_row[:, k : k + 1])
        pivot_row = pivot_row * scale
        for g in range(own, rank // 8):
            step = (groups[g][:, k : k + 1] * scale) * pivot_row
            if g > own:
                groups[g] = groups[g] - step
            else:
                groups[g] = jnp.where(
                    below > place, groups[g] - step, jnp.where(below == place, pivot_row, groups[g])
                )
    return jnp.concatenate(groups)[:, rank:]


def ortho_kernel(core_ref, half_ref, other_ref, merged_ref, ortho_ref, keep_ref, give_ref,
                 held_ref, left_ref, sem):
    fetch = pltpu.make_async_copy(merged_ref, held_ref, sem)
    fetch.start()
    core = core_ref[0]
    rank, rows = left_ref.shape
    across = rows // 128
    for place in range(half_ref.shape[0]):
        low, high = own_first(core, half_ref[place], other_ref[place])
        down = 16 * (place // across)
        lane = pl.ds(128 * (place % across), 128)
        left_ref[pl.ds(down, 16), lane] = low
        left_ref[pl.ds(rank // 2 + down, 16), lane] = high
    left = left_ref[...]
    gram = lax.dot_general(
        left, left, (((1,), (1,)), ((), ())), precision=lax.Precision.HIGHEST,
        preferred_element_type=jnp.float32,
    )
    ortho = jnp.dot(
        inverse_factor(gram), left, precision=lax.Precision.HIGHEST,
        preferred_element_type=jnp.float32,
    ).astype(jnp.bfloat16)
    ortho_ref[...] = ortho
    fetch.wait()
    wide = keep_ref.shape[2]
    count = held_ref.shape[1] // wide
    for lane in range(count):
        right = jnp.dot(
            ortho, held_ref[:, wide * lane : wide * lane + wide],
            preferred_element_type=jnp.float32,
        )
        keep, give = own_first(core, right[: rank // 2], right[rank // 2 :])
        for down in range(rank // 16):
            keep_ref[down * count + lane] = keep[8 * down : 8 * down + 8]
            give_ref[down * count + lane] = give[8 * down : 8 * down + 8]


def orthonormal(core, half, other, merged, parts):
    rows, columns = merged.shape
    rank = half.size * 2 // rows
    wide = rank * columns // (8 * parts)
    tiles = jax.ShapeDtypeStruct((parts // 2, 8, wide), jnp.float32)
    return pl.pallas_call(
        ortho_kernel,
        in_specs=[SCALAR, WHOLE, WHOLE, pl.BlockSpec(memory_space=pl.ANY)],
        out_specs=[WHOLE, WHOLE, WHOLE],
        out_shape=[jax.ShapeDtypeStruct((rank, rows), jnp.bfloat16), tiles, tiles],
        scratch_shapes=[
            pltpu.VMEM((rows, columns), jnp.bfloat16),
            pltpu.VMEM((rank, rows), jnp.float32),
            pltpu.SemaphoreType.DMA,
        ],
        compiler_params=pltpu.CompilerParams(vmem_limit_bytes=VMEM_LIMIT),
        cost_estimate=pl.CostEstimate(
            flops=2 * rows * columns * rank, bytes_accessed=2 * rows * columns, transcendentals=0
        ),
    )(core, half, other, merged)


def finish_kernel(core_ref, half_ref, other_ref, ortho_ref, own_ref, merged_ref,
                  update_ref, right_ref, errors_ref, cast_ref):
    rank = ortho_ref.shape[1]

    @pl.when(pl.program_id(0) == 0)
    def _():
        core = core_ref[0]
        wide = half_ref.shape[2]
        count = right_ref.shape[1] // wide
        for lane in range(count):
            pairs = [
                own_first(core, half_ref[down * count + lane], other_ref[down * count + lane])
                for down in range(rank // 16)
            ]
            right = jnp.concatenate([low for low, _ in pairs] + [high for _, high in pairs])
            cast_ref[:, wide * lane : wide * lane + wide] = right.astype(jnp.bfloat16)
            right_ref[:, wide * lane : wide * lane + wide] = right
        update_ref[...] = jnp.dot(
            own_ref[...], cast_ref[...], preferred_element_type=jnp.float32
        ).astype(jnp.bfloat16)

    full_update = jnp.dot(ortho_ref[...], cast_ref[...], preferred_element_type=jnp.float32)
    errors_ref[...] = (merged_ref[...].astype(jnp.float32) - full_update).astype(jnp.bfloat16)


def finish(core, half, other, ortho, own, merged):
    rows, columns = merged.shape
    rank = ortho.shape[1]
    block = pl.BlockSpec((BLOCK_ROWS, columns), lambda i: (i, 0))
    tiles = pl.BlockSpec(half.shape, lambda i: (0, 0, 0))

    def fixed(shape):
        return pl.BlockSpec(shape, lambda i: (0, 0))

    return pl.pallas_call(
        finish_kernel,
        grid=(rows // BLOCK_ROWS,),
        in_specs=[
            SCALAR, tiles, tiles, pl.BlockSpec((BLOCK_ROWS, rank), lambda i: (i, 0)),
            fixed(own.shape), block,
        ],
        out_specs=[fixed((own.shape[0], columns)), fixed((rank, columns)), block],
        out_shape=[
            jax.ShapeDtypeStruct((own.shape[0], columns), jnp.bfloat16),
            jax.ShapeDtypeStruct((rank, columns), jnp.float32),
            jax.ShapeDtypeStruct(merged.shape, jnp.bfloat16),
        ],
        scratch_shapes=[pltpu.VMEM((rank, columns), jnp.bfloat16)],
        compiler_params=pltpu.CompilerParams(vmem_limit_bytes=VMEM_LIMIT),
        cost_estimate=pl.CostEstimate(
            flops=2 * rows * columns * rank, bytes_accessed=4 * rows * columns, transcendentals=0
        ),
    )(core, half, other, ortho, own, merged)


def swap_cores(value):
    return lax.ppermute(value, "core", [(0, 1), (1, 0)])


def exchange(value, axes):
    return lax.all_to_all(value, axes, 0, 0)


def spread(value, copies):
    return jnp.broadcast_to(value[None], (copies,) + value.shape)


def per_device(grads, errors, q_prev):
    core = lax.axis_index("core").astype(jnp.int32).reshape(1)
    pairs = lax.axis_size("y") * lax.axis_size("x")
    depth = lax.axis_size("z")
    replicas = 2 * pairs

    merged, keep, give = merge(core, grads[0], errors[0], q_prev.T)
    mine = jnp.sum(exchange(keep + swap_cores(give), YX), axis=0)
    mine = jnp.sum(exchange(spread(mine, depth), "z"), axis=0) / replicas
    half = exchange(spread(mine, pairs), YX)

    ortho, keep, give = orthonormal(core, half, swap_cores(half), merged, replicas)
    mine = jnp.sum(exchange(keep + swap_cores(give), YX), axis=0) / replicas
    half = exchange(spread(mine, pairs), YX)

    ortho = ortho.T
    row_count = grads.shape[1] // replicas
    row_start = lax.axis_index(("y", "x", "core")) * row_count
    own = lax.dynamic_slice_in_dim(ortho, row_start, row_count, 0)
    update, right, new_errors = finish(core, half, swap_cores(half), ortho, own, merged)
    return update, right.T, new_errors[None]


def solution(mesh):
    chips = Mesh(mesh.devices.reshape(4, 4, 2, 8), ("y", "x", "core", "z"))
    dp = ("y", "x", "core")
    placed = (P(dp, None, "z"), P(dp, None, "z"), P("z", None))
    return jax.shard_map(
        per_device,
        mesh=chips,
        in_specs=placed,
        out_specs=(P(dp, "z"), P("z", None), P(dp, None, "z")),
        check_vma=False,
    )
```

time: 412 us -> 90.4 us (0.22)
  waiting for transfers between devices: 368 us -> 4.27 us
  blocking collectives: 0 us -> 57.4 us
  other arithmetic: 16.2 us -> 0.1 us
  Pallas kernels: 0 us -> 15.4 us
  between operations: 14.1 us -> 0.74 us
  matrix products: 12.1 us -> 0 us
  starting transfers between devices: 0.08 us -> 11 us
    psum x2 -> x0, waiting for transfers between devices: 367 us -> none  [the longest x1 255 us: per_device(): left_sum = lax.psum(partial_left, ('dp', 'tensor')) / replicas]
    all_to_all x0 -> x5, blocking collectives: none -> 57.4 us  [exchange(): return lax.all_to_all(value, axes, 0, 0)]
    pallas_call x0 -> x3, Pallas kernels: none -> 15.4 us  [the longest x1 7.25 us: orthonormal(): pl.pallas_call(ortho_kernel, in_specs=[SCALAR, WHOLE, WHOLE, pl.BlockSpec...]
    another operation x5 -> x0, other arithmetic: 12.1 us -> none  [the longest x3 6.52 us: per_device(): ortho_left = orthonormal(left_sum, jnp.linalg.cholesky(gram_matrix))]
    ppermute x0 -> x4, starting transfers between devices: none -> 11 us  [swap_cores(): return lax.ppermute(value, 'core', [(0, 1), (1, 0)])]
    dot_general x4 -> x0, matrix products: 10.8 us -> none  [the longest x1 4.77 us: per_device(): jnp.dot(merged, prior_cast, preferred_element_type=jnp.float32)]
    ppermute x0 -> x4, waiting for transfers between devices: none -> 4.27 us  [swap_cores(): return lax.ppermute(value, 'core', [(0, 1), (1, 0)])]
  transfers between devices with their start and end apart: 2 -> 4, of which waited for: 2 -> 4; matrix products, arithmetic and copies ran while one was open for 0% -> 0% of each run, Pallas kernels for 0% -> 0%
where the time goes in v2:
time: 90.4 us; the launch traced here: 90 us
  blocking collectives  57.4 us (63%)
  Pallas kernels  15.4 us (17%)
  starting transfers between devices  11 us (12%)
  waiting for transfers between devices  4.27 us (5%)
  local copies, waits for them, and re-layouts  1.2 us (1%)
    all_to_all x5, blocking collectives, exchange(): return lax.all_to_all(value, axes, 0, 0)  57.4 us
    ppermute x4, starting transfers between devices, swap_cores(): return lax.ppermute(value, 'core', [(0, 1), (1, 0)])  11 us
    pallas_call x1, Pallas kernels, orthonormal(): pl.pallas_call(ortho_kernel, in_specs=[SCALAR, WHOLE, WHOLE, pl.BlockSpec...  7.25 us
    ppermute x4, waiting for transfers between devices, swap_cores(): return lax.ppermute(value, 'core', [(0, 1), (1, 0)])  4.27 us
    pallas_call x1, Pallas kernels, merge(): pl.pallas_call(merge_kernel, grid=(rows // BLOCK_ROWS,), in_specs=[SCALAR...  4.08 us
    pallas_call x1, Pallas kernels, finish(): pl.pallas_call(finish_kernel, grid=(rows // BLOCK_ROWS,), in_specs=[SCALA...  4.08 us
  transfers between devices with their start and end apart: 4, of which 4 were waited for; matrix products, arithmetic and copies ran while one was open for 0% of the time, Pallas kernels for 0%

profile of v2, /device:TPU:1, one launch (start us, length us, event | category | flops | bytes accessed | tf_op | source)
XLA Modules:
  0.0 90.0 jit_solution(2157741374437070514)
XLA Ops:
  0.6 0.0 copy-start
  0.6 1.0 %copy-done = f32[1536,64]{0,1:T(8,128)S(1)} copy-done((f32[1536,64]{0,1:T(8,128)S(1)}, f32[1536,64]{0,1:T(8,128)}, u32[]{:S(2)}) %copy-start) | copy-done | bytes 393240
  1.6 4.1 %shard_map.58 = (bf16[1024,1536]{1,0:T(8,128)(2,1)S(1)}, f32[16,16,128]{2,1,0:T(8,128)S(1)}, f32[16,16,128]{2,1,0:T(8,128)S(1)}) custom-call(s32[1]{0:T(128)} %bitcast.core_ref, bf16[1024,1536]{1,0:T(8,128)(2,1)} %bitcast.11, bf16[1024,1536]{1,0:T(8,128)(2,1)} %bitcast.12, f32[64,1536]{1,0:T(8,128)S(1)} %bitcast.10), custom_call_target="tpu_custom_call" | custom-call | flops 201326592 | bytes 9437184 | tf_op jit(solution)/shard_map/pallas_call | solution.py:47
  5.7 3.3 %collective-permute-start = (f32[16,16,128]{2,1,0:T(8,128)S(1)}, f32[16,16,128]{2,1,0:T(8,128)S(1)}, u32[]{:S(2)}, u32[]{:S(2)}) collective-permute-start(f32[16,16,128]{2,1,0:T(8,128)S(1)} %get-tuple-element.13), channel_id=1, source_target_pairs={{0,8},{8,0},{1,9},{9,1},{2,10},{10,2},{3,11},{11,3},{4,12},{12,4},... | collective-permute-start | bytes 393224 | tf_op jit(solution)/shard_map/ppermute | solution.py:198
  9.1 1.0 %collective-permute-done = f32[16,16,128]{2,1,0:T(8,128)S(1)} collective-permute-done((f32[16,16,128]{2,1,0:T(8,128)S(1)}, f32[16,16,128]{2,1,0:T(8,128)S(1)}, u32[]{:S(2)}, u32[]{:S(2)}) %collective-permute-start) | collective-permute-done | bytes 131104 | tf_op jit(solution)/shard_map/ppermute | solution.py:198
  10.1 11.7 %all_to_all.25 = f32[16,16,128]{2,1,0:T(8,128)S(1)} all-to-all(f32[16,16,128]{2,1,0:T(8,128)S(1)} %add.15), channel_id=1, replica_groups=mesh['y'=4,'x'=4,'core'=2,'z'=8] {'y','x'}, dimensions={0} | all-to-all | bytes 262144 | tf_op jit(solution)/shard_map/all_to_all | solution.py:202
  21.8 15.2 %all_to_all.26 = f32[8,16,128]{2,1,0:T(8,128)S(1)} all-to-all(f32[8,16,128]{2,1,0:T(8,128)S(1)} %broadcast_in_dim.8), channel_id=1, replica_groups=mesh['y'=4,'x'=4,'core'=2,'z'=8] {'z'}, dimensions={0} | all-to-all | bytes 131072 | tf_op jit(solution)/shard_map/all_to_all | solution.py:202
  37.0 10.0 %all_to_all.27.half_ref = f32[16,16,128]{2,1,0:T(8,128)S(1)} all-to-all(f32[16,16,128]{2,1,0:T(8,128)S(1)} %broadcast_in_dim.9), channel_id=1, replica_groups=mesh['y'=4,'x'=4,'core'=2,'z'=8] {'y','x'}, dimensions={0} | all-to-all | bytes 262144 | tf_op jit(solution)/shard_map/all_to_all | solution.py:202
  47.0 4.3 %collective-permute-start.1 = (f32[16,16,128]{2,1,0:T(8,128)S(1)}, f32[16,16,128]{2,1,0:T(8,128)S(1)}, u32[]{:S(2)}, u32[]{:S(2)}) collective-permute-start(f32[16,16,128]{2,1,0:T(8,128)S(1)} %all_to_all.27.half_ref), channel_id=1, source_target_pairs={{0,8},{8,0},{1,9},{9,1},{2,10},{10,2},{3,11},{11,3},{4,12},{12,4},... | collective-permute-start | bytes 393224 | tf_op jit(solution)/shard_map/ppermute | solution.py:198
  51.3 1.0 %collective-permute-done.1.other_ref = f32[16,16,128]{2,1,0:T(8,128)S(1)} collective-permute-done((f32[16,16,128]{2,1,0:T(8,128)S(1)}, f32[16,16,128]{2,1,0:T(8,128)S(1)}, u32[]{:S(2)}, u32[]{:S(2)}) %collective-permute-start.1) | collective-permute-done | bytes 131104 | tf_op jit(solution)/shard_map/ppermute | solution.py:198
  52.3 7.2 %shard_map.59 = (bf16[64,1024]{1,0:T(8,128)(2,1)S(1)}, f32[16,8,384]{2,1,0:T(8,128)S(1)}, f32[16,8,384]{2,1,0:T(8,128)S(1)}) custom-call(s32[1]{0:T(128)} %bitcast.core_ref, f32[16,16,128]{2,1,0:T(8,128)S(1)} %all_to_all.27.half_ref, f32[16,16,128]{2,1,0:T(8,128)S(1)} %collective-permute-done.1.other_ref, bf16[1024,1536]{1,0:T(8,128)(2,1)S(1)} %get-tuple-element.14.merged_ref), custom_call_target="tpu_custom_call" | custom-call | flops 201326592 | bytes 3145728 | tf_op jit(solution)/shard_map/pallas_call | solution.py:125
  59.5 0.4 collective-permute-start.2
  60.0 1.1 %collective-permute-done.2 = f32[16,8,384]{2,1,0:T(8,128)S(1)} collective-permute-done((f32[16,8,384]{2,1,0:T(8,128)S(1)}, f32[16,8,384]{2,1,0:T(8,128)S(1)}, u32[]{:S(2)}, u32[]{:S(2)}) %collective-permute-start.2) | collective-permute-done | bytes 196640 | tf_op jit(solution)/shard_map/ppermute | solution.py:198
  61.1 10.0 %all_to_all.28 = f32[16,8,384]{2,1,0:T(8,128)S(1)} all-to-all(f32[16,8,384]{2,1,0:T(8,128)S(1)} %add.16), channel_id=1, replica_groups=mesh['y'=4,'x'=4,'core'=2,'z'=8] {'y','x'}, dimensions={0} | all-to-all | bytes 393216 | tf_op jit(solution)/shard_map/all_to_all | solution.py:202
  71.1 10.5 %all_to_all.29.half_ref = f32[16,8,384]{2,1,0:T(8,128)} all-to-all(f32[16,8,384]{2,1,0:T(8,128)S(1)} %broadcast_in_dim.10), channel_id=1, replica_groups=mesh['y'=4,'x'=4,'core'=2,'z'=8] {'y','x'}, dimensions={0} | all-to-all | bytes 393216 | tf_op jit(solution)/shard_map/all_to_all | solution.py:202
  81.6 2.9 %collective-permute-start.3 = (f32[16,8,384]{2,1,0:T(8,128)}, f32[16,8,384]{2,1,0:T(8,128)}, u32[]{:S(2)}, u32[]{:S(2)}) collective-permute-start(f32[16,8,384]{2,1,0:T(8,128)} %all_to_all.29.half_ref), channel_id=1, source_target_pairs={{0,8},{8,0},{1,9},{9,1},{2,10},{10,2},{3,11},{11,3},{4,12},{12,4},... | collective-permute-start | bytes 589832 | tf_op jit(solution)/shard_map/ppermute | solution.py:198
  84.5 0.2 copy.8
  84.7 1.2 %collective-permute-done.3.other_ref = f32[16,8,384]{2,1,0:T(8,128)} collective-permute-done((f32[16,8,384]{2,1,0:T(8,128)}, f32[16,8,384]{2,1,0:T(8,128)}, u32[]{:S(2)}, u32[]{:S(2)}) %collective-permute-start.3) | collective-permute-done | bytes 196640 | tf_op jit(solution)/shard_map/ppermute | solution.py:198
  86.0 4.1 %shard_map.60 = (bf16[32,1536]{1,0:T(8,128)(2,1)}, f32[64,1536]{1,0:T(8,128)}, bf16[1024,1536]{1,0:T(8,128)(2,1)}) custom-call(s32[1]{0:T(128)} %bitcast.core_ref, f32[16,8,384]{2,1,0:T(8,128)} %all_to_all.29.half_ref, f32[16,8,384]{2,1,0:T(8,128)} %collective-permute-done.3.other_ref, bf16[1024,64]{1,0:T(8,128)(2,1)S(1)} %bitcast.9, ...), custom_call_target="tpu_custom_call" | custom-call | flops 201326592 | bytes 6291456 | tf_op jit(solution)/shard_map/pallas_call | solution.py:176
  (11 shorter events, 0.1 us)
Async XLA Ops:
  0.6 1.0 %copy-start = (f32[1536,64]{0,1:T(8,128)S(1)}, f32[1536,64]{0,1:T(8,128)}, u32[]{:S(2)}) copy-start(f32[1536,64]{0,1:T(8,128)} %param.5) | copy-start | bytes 1179652
  5.7 4.3 %collective-permute-start = (f32[16,16,128]{2,1,0:T(8,128)S(1)}, f32[16,16,128]{2,1,0:T(8,128)S(1)}, u32[]{:S(2)}, u32[]{:S(2)}) collective-permute-start(f32[16,16,128]{2,1,0:T(8,128)S(1)} %get-tuple-element.13), channel_id=1, source_target_pairs={{0,8},{8,0},{1,9},{9,1},{2,10},{10,2},{3,11},{11,3},{4,12},{12,4},... | collective-permute-start | bytes 393224 | tf_op jit(solution)/shard_map/ppermute | solution.py:198
  47.0 5.2 %collective-permute-start.1 = (f32[16,16,128]{2,1,0:T(8,128)S(1)}, f32[16,16,128]{2,1,0:T(8,128)S(1)}, u32[]{:S(2)}, u32[]{:S(2)}) collective-permute-start(f32[16,16,128]{2,1,0:T(8,128)S(1)} %all_to_all.27.half_ref), channel_id=1, source_target_pairs={{0,8},{8,0},{1,9},{9,1},{2,10},{10,2},{3,11},{11,3},{4,12},{12,4},... | collective-permute-start | bytes 393224 | tf_op jit(solution)/shard_map/ppermute | solution.py:198
  59.5 1.5 %collective-permute-start.2 = (f32[16,8,384]{2,1,0:T(8,128)S(1)}, f32[16,8,384]{2,1,0:T(8,128)S(1)}, u32[]{:S(2)}, u32[]{:S(2)}) collective-permute-start(f32[16,8,384]{2,1,0:T(8,128)S(1)} %get-tuple-element.16), channel_id=1, source_target_pairs={{0,8},{8,0},{1,9},{9,1},{2,10},{10,2},{3,11},{11,3},{4,12},{12,4},... | collective-permute-start | bytes 589832 | tf_op jit(solution)/shard_map/ppermute | solution.py:198
  81.6 4.3 %collective-permute-start.3 = (f32[16,8,384]{2,1,0:T(8,128)}, f32[16,8,384]{2,1,0:T(8,128)}, u32[]{:S(2)}, u32[]{:S(2)}) collective-permute-start(f32[16,8,384]{2,1,0:T(8,128)} %all_to_all.29.half_ref), channel_id=1, source_target_pairs={{0,8},{8,0},{1,9},{9,1},{2,10},{10,2},{3,11},{11,3},{4,12},{12,4},... | collective-permute-start | bytes 589832 | tf_op jit(solution)/shard_map/ppermute | solution.py:198

commit v3 on v2

v3 whole, which is shorter than its diff:
```python
import jax
import jax.numpy as jnp
from jax import lax
from jax.experimental import pallas as pl
from jax.experimental.pallas import tpu as pltpu
from jax.sharding import Mesh, PartitionSpec as P

YX = ("y", "x")
VMEM_LIMIT = 32 * 1024 * 1024
WHOLE = pl.BlockSpec(memory_space=pltpu.VMEM)
SCALAR = pl.BlockSpec(memory_space=pltpu.SMEM)
IN_HBM = pl.BlockSpec(memory_space=pltpu.HBM)
CHUNK = 128
GROUP = 8


def own_first(core, low, high):
    return jnp.where(core == 0, low, high), jnp.where(core == 0, high, low)


def merge_kernel(core_ref, grads_ref, errors_ref, prior_ref, merged_ref, keep_ref, give_ref,
                 grads_held, errors_held, sems):
    core = core_ref[0]
    rank = prior_ref.shape[0]
    rows = merged_ref.shape[0]
    chunks = rows // CHUNK
    fetches = []
    for i in range(chunks):
        block = pl.ds(CHUNK * i, CHUNK)
        pair = (
            pltpu.make_async_copy(grads_ref.at[block], grads_held.at[block], sems.at[0, i]),
            pltpu.make_async_copy(errors_ref.at[block], errors_held.at[block], sems.at[1, i]),
        )
        for fetch in pair:
            fetch.start()
        fetches.append(pair)
    prior = prior_ref[...].astype(jnp.bfloat16)
    for i in range(chunks):
        block = pl.ds(CHUNK * i, CHUNK)
        for fetch in fetches[i]:
            fetch.wait()
        merged = (
            grads_held[block].astype(jnp.float32) + errors_held[block].astype(jnp.float32)
        ).astype(jnp.bfloat16)
        merged_ref[block] = merged
        left = lax.dot_general(
            prior, merged, (((1,), (1,)), ((), ())), preferred_element_type=jnp.float32
        )
        keep, give = own_first(core, left[: rank // 2], left[rank // 2 :])
        for down in range(rank // 32):
            for lane in range(CHUNK // 128):
                place = down * (rows // 128) + i * (CHUNK // 128) + lane
                tile = (slice(16 * down, 16 * down + 16), slice(128 * lane, 128 * lane + 128))
                keep_ref[place] = keep[tile]
                give_ref[place] = give[tile]


def merge(core, grads, errors, prior):
    rows, columns = grads.shape
    rank = prior.shape[0]
    tiles = jax.ShapeDtypeStruct((rows // 128 * (rank // 32), 16, 128), jnp.float32)
    return pl.pallas_call(
        merge_kernel,
        in_specs=[SCALAR, IN_HBM, IN_HBM, WHOLE],
        out_specs=[WHOLE, WHOLE, WHOLE],
        out_shape=[jax.ShapeDtypeStruct(grads.shape, jnp.bfloat16), tiles, tiles],
        scratch_shapes=[
            pltpu.VMEM(grads.shape, jnp.bfloat16),
            pltpu.VMEM(grads.shape, jnp.bfloat16),
            pltpu.SemaphoreType.DMA((2, rows // CHUNK)),
        ],
        compiler_params=pltpu.CompilerParams(vmem_limit_bytes=VMEM_LIMIT),
        cost_estimate=pl.CostEstimate(
            flops=2 * rows * columns * rank, bytes_accessed=6 * rows * columns, transcendentals=0
        ),
    )(core, grads, errors, prior)


def inverse_factor(gram):
    rank = gram.shape[0]
    shape = (GROUP, 2 * rank)
    row = lax.broadcasted_iota(jnp.int32, (rank, rank), 0)
    column = lax.broadcasted_iota(jnp.int32, (rank, rank), 1)
    state = jnp.concatenate([gram, jnp.where(row == column, 1.0, 0.0)], axis=1)
    groups = [state[GROUP * g : GROUP * g + GROUP] for g in range(rank // GROUP)]
    place = lax.broadcasted_iota(jnp.int32, shape, 0)
    span = range(GROUP)
    for own in range(rank // GROUP):
        later = range(own, rank // GROUP)
        first = GROUP * own
        columns = [
            {g: jnp.broadcast_to(groups[g][:, first + j : first + j + 1], shape) for g in later}
            for j in span
        ]
        rows = [jnp.broadcast_to(groups[own][j : j + 1], shape) for j in span]
        cross = [
            [jnp.broadcast_to(columns[j][own][i : i + 1], shape) for j in range(i + 1)] for i in span
        ]
        for j in span:
            scale = lax.rsqrt(cross[j][j])
            rows[j] = rows[j] * scale
            for g in later:
                columns[j][g] = columns[j][g] * scale
            for i in range(j + 1, GROUP):
                cross[i][j] = cross[i][j] * scale
            for i in range(j + 1, GROUP):
                rows[i] = rows[i] - cross[i][j] * rows[j]
                for g in later:
                    columns[i][g] = columns[i][g] - columns[j][g] * cross[i][j]
                for l in range(j + 1, i + 1):
                    cross[i][l] = cross[i][l] - cross[i][j] * cross[l][j]
        for g in range(own + 1, rank // GROUP):
            for j in span:
                groups[g] = groups[g] - columns[j][g] * rows[j]
        groups[own] = rows[0]
        for j in range(1, GROUP):
            groups[own] = jnp.where(place == j, rows[j], groups[own])
    return jnp.concatenate(groups)[:, rank:]


def ortho_kernel(core_ref, half_ref, other_ref, merged_ref, ortho_ref, keep_ref, give_ref,
                 left_ref):
    core = core_ref[0]
    rank, rows = left_ref.shape
    across = rows // 128
    for place in range(half_ref.shape[0]):
        low, high = own_first(core, half_ref[place], other_ref[place])
        down = 16 * (place // across)
        lane = pl.ds(128 * (place % across), 128)
        left_ref[pl.ds(down, 16), lane] = low
        left_ref[pl.ds(rank // 2 + down, 16), lane] = high
    left = left_ref[...]
    gram = lax.dot_general(
        left, left, (((1,), (1,)), ((), ())), precision=lax.Precision.HIGHEST,
        preferred_element_type=jnp.float32,
    )
    ortho = jnp.dot(
        inverse_factor(gram), left, precision=lax.Precision.HIGHEST,
        preferred_element_type=jnp.float32,
    ).astype(jnp.bfloat16)
    ortho_ref[...] = ortho
    wide = keep_ref.shape[2]
    count = merged_ref.shape[1] // wide
    for lane in range(count):
        right = jnp.dot(
            ortho, merged_ref[:, wide * lane : wide * lane + wide],
            preferred_element_type=jnp.float32,
        )
        keep, give = own_first(core, right[: rank // 2], right[rank // 2 :])
        for down in range(rank // 16):
            keep_ref[down * count + lane] = keep[8 * down : 8 * down + 8]
            give_ref[down * count + lane] = give[8 * down : 8 * down + 8]


def orthonormal(core, half, other, merged, parts):
    rows, columns = merged.shape
    rank = half.size * 2 // rows
    wide = rank * columns // (8 * parts)
    tiles = jax.ShapeDtypeStruct((parts // 2, 8, wide), jnp.float32)
    return pl.pallas_call(
        ortho_kernel,
        in_specs=[SCALAR, WHOLE, WHOLE, WHOLE],
        out_specs=[WHOLE, WHOLE, WHOLE],
        out_shape=[jax.ShapeDtypeStruct((rank, rows), jnp.bfloat16), tiles, tiles],
        scratch_shapes=[pltpu.VMEM((rank, rows), jnp.float32)],
        compiler_params=pltpu.CompilerParams(vmem_limit_bytes=VMEM_LIMIT),
        cost_estimate=pl.CostEstimate(
            flops=2 * rows * columns * rank, bytes_accessed=2 * rows * columns, transcendentals=0
        ),
    )(core, half, other, merged)


def finish_kernel(core_ref, half_ref, other_ref, ortho_ref, own_ref, merged_ref,
                  update_ref, right_ref, errors_ref, cast_ref, errors_held, sems):
    core = core_ref[0]
    rank = ortho_ref.shape[1]
    wide = half_ref.shape[2]
    count = right_ref.shape[1] // wide
    for lane in range(count):
        pairs = [
            own_first(core, half_ref[down * count + lane], other_ref[down * count + lane])
            for down in range(rank // 16)
        ]
        right = jnp.concatenate([low for low, _ in pairs] + [high for _, high in pairs])
        cast_ref[:, wide * lane : wide * lane + wide] = right.astype(jnp.bfloat16)
        right_ref[:, wide * lane : wide * lane + wide] = right
    cast = cast_ref[...]
    stores = []
    for i in range(merged_ref.shape[0] // CHUNK):
        block = pl.ds(CHUNK * i, CHUNK)
        full_update = jnp.dot(ortho_ref[block], cast, preferred_element_type=jnp.float32)
        errors_held[block] = (
            merged_ref[block].astype(jnp.float32) - full_update
        ).astype(jnp.bfloat16)
        store = pltpu.make_async_copy(errors_held.at[block], errors_ref.at[block], sems.at[i])
        store.start()
        stores.append(store)
    update_ref[...] = jnp.dot(
        own_ref[...], cast, preferred_element_type=jnp.float32
    ).astype(jnp.bfloat16)
    for store in stores:
        store.wait()


def finish(core, half, other, ortho, own, merged):
    rows, columns = merged.shape
    rank = ortho.shape[1]
    return pl.pallas_call(
        finish_kernel,
        in_specs=[SCALAR, WHOLE, WHOLE, WHOLE, WHOLE, WHOLE],
        out_specs=[WHOLE, WHOLE, IN_HBM],
        out_shape=[
            jax.ShapeDtypeStruct((own.shape[0], columns), jnp.bfloat16),
            jax.ShapeDtypeStruct((rank, columns), jnp.float32),
            jax.ShapeDtypeStruct(merged.shape, jnp.bfloat16),
        ],
        scratch_shapes=[
            pltpu.VMEM((rank, columns), jnp.bfloat16),
            pltpu.VMEM(merged.shape, jnp.bfloat16),
            pltpu.SemaphoreType.DMA((rows // CHUNK,)),
        ],
        compiler_params=pltpu.CompilerParams(vmem_limit_bytes=VMEM_LIMIT),
        cost_estimate=pl.CostEstimate(
            flops=2 * rows * columns * rank, bytes_accessed=4 * rows * columns, transcendentals=0
        ),
    )(core, half, other, ortho, own, merged)


def swap_cores(value):
    return lax.ppermute(value, "core", [(0, 1), (1, 0)])


def exchange(value, axes):
    return lax.all_to_all(value, axes, 0, 0)


def spread(value, copies):
    return jnp.broadcast_to(value[None], (copies,) + value.shape)


def per_device(grads, errors, q_prev):
    core = lax.axis_index("core").astype(jnp.int32).reshape(1)
    pairs = lax.axis_size("y") * lax.axis_size("x")
    depth = lax.axis_size("z")
    replicas = 2 * pairs

    merged, keep, give = merge(core, grads[0], errors[0], q_prev.T)
    mine = jnp.sum(exchange(keep + swap_cores(give), YX), axis=0)
    mine = jnp.sum(exchange(spread(mine, depth), "z"), axis=0) / replicas
    half = exchange(spread(mine, pairs), YX)

    ortho, keep, give = orthonormal(core, half, swap_cores(half), merged, replicas)
    mine = jnp.sum(exchange(keep + swap_cores(give), YX), axis=0) / replicas
    half = exchange(spread(mine, pairs), YX)

    ortho = ortho.T
    row_count = grads.shape[1] // replicas
    row_start = lax.axis_index(("y", "x", "core")) * row_count
    own = lax.dynamic_slice_in_dim(ortho, row_start, row_count, 0)
    update, right, new_errors = finish(core, half, swap_cores(half), ortho, own, merged)
    return update, right.T, new_errors[None]


def solution(mesh):
    chips = Mesh(mesh.devices.reshape(4, 4, 2, 8), ("y", "x", "core", "z"))
    dp = ("y", "x", "core")
    placed = (P(dp, None, "z"), P(dp, None, "z"), P("z", None))
    return jax.shard_map(
        per_device,
        mesh=chips,
        in_specs=placed,
        out_specs=(P(dp, "z"), P("z", None), P(dp, None, "z")),
        check_vma=False,
    )
```

time: 90.4 us -> 92 us (1.018)
  local copies, waits for them, and re-layouts: 1.2 us -> 4.98 us
  Pallas kernels: 15.4 us -> 13.2 us
    unnamed x2 -> x6, local copies, waits for them, and re-layouts: 0.99 us -> 4.77 us
    pallas_call x3, Pallas kernels: 15.4 us -> 13.2 us  [the longest x1 5.97 us: merge(): pl.pallas_call(merge_kernel, in_specs=[SCALAR, IN_HBM, IN_HBM, WHOLE], ou...]
where the time goes in v3:
time: 92 us; the launch traced here: 91.6 us
  blocking collectives  57.4 us (62%)
  Pallas kernels  13.2 us (14%)
  starting transfers between devices  11 us (12%)
  local copies, waits for them, and re-layouts  4.98 us (5%)
  waiting for transfers between devices  4.27 us (5%)
    all_to_all x5, blocking collectives, exchange(): return lax.all_to_all(value, axes, 0, 0)  57.4 us
    ppermute x4, starting transfers between devices, swap_cores(): return lax.ppermute(value, 'core', [(0, 1), (1, 0)])  11 us
    pallas_call x1, Pallas kernels, merge(): pl.pallas_call(merge_kernel, in_specs=[SCALAR, IN_HBM, IN_HBM, WHOLE], ou...  5.97 us
    unnamed x6, local copies, waits for them, and re-layouts  4.77 us
    ppermute x4, waiting for transfers between devices, swap_cores(): return lax.ppermute(value, 'core', [(0, 1), (1, 0)])  4.27 us
    pallas_call x1, Pallas kernels, finish(): pl.pallas_call(finish_kernel, in_specs=[SCALAR, WHOLE, WHOLE, WHOLE, WHOL...  3.78 us
    pallas_call x1, Pallas kernels, orthonormal(): pl.pallas_call(ortho_kernel, in_specs=[SCALAR, WHOLE, WHOLE, WHOLE], out_...  3.41 us
  transfers between devices with their start and end apart: 4, of which 4 were waited for; matrix products, arithmetic and copies ran while one was open for 0% of the time, Pallas kernels for 0%

profile of v3, /device:TPU:1, one launch (start us, length us, event | category | flops | bytes accessed | tf_op | source)
XLA Modules:
  0.0 91.6 jit_solution(15880143621281447304)
XLA Ops:
  0.6 0.0 copy-start
  0.6 1.9 %copy-done = bf16[1,1024,1536]{2,1,0:T(8,128)(2,1)S(1)} copy-done((bf16[1,1024,1536]{2,1,0:T(8,128)(2,1)S(1)}, bf16[1,1024,1536]{2,1,0:T(8,128)(2,1)}, u32[]{:S(2)}) %copy-start) | copy-done | bytes 3145752
  2.5 0.0 copy-start.1
  2.5 1.9 %copy-done.1 = bf16[1,1024,1536]{2,1,0:T(8,128)(2,1)S(1)} copy-done((bf16[1,1024,1536]{2,1,0:T(8,128)(2,1)S(1)}, bf16[1,1024,1536]{2,1,0:T(8,128)(2,1)}, u32[]{:S(2)}) %copy-start.1) | copy-done | bytes 3145752
  4.4 0.0 copy-start.2
  4.4 1.0 %copy-done.2 = f32[1536,64]{0,1:T(8,128)S(1)} copy-done((f32[1536,64]{0,1:T(8,128)S(1)}, f32[1536,64]{0,1:T(8,128)}, u32[]{:S(2)}) %copy-start.2) | copy-done | bytes 393240
  5.4 6.0 %shard_map.58 = (bf16[1024,1536]{1,0:T(8,128)(2,1)S(1)}, f32[16,16,128]{2,1,0:T(8,128)S(1)}, f32[16,16,128]{2,1,0:T(8,128)S(1)}) custom-call(s32[1]{0:T(128)} %bitcast.core_ref, bf16[1024,1536]{1,0:T(8,128)(2,1)S(1)} %bitcast.9, bf16[1024,1536]{1,0:T(8,128)(2,1)S(1)} %bitcast.10, f32[64,1536]{1,0:T(8,128)S(1)} %bitcast.12), custom_call_target="tpu_custom_call" | custom-call | flops 201326592 | bytes 9437184 | tf_op jit(solution)/shard_map/pallas_call | solution.py:62
  11.4 3.3 %collective-permute-start = (f32[16,16,128]{2,1,0:T(8,128)S(1)}, f32[16,16,128]{2,1,0:T(8,128)S(1)}, u32[]{:S(2)}, u32[]{:S(2)}) collective-permute-start(f32[16,16,128]{2,1,0:T(8,128)S(1)} %get-tuple-element.13), channel_id=1, source_target_pairs={{0,8},{8,0},{1,9},{9,1},{2,10},{10,2},{3,11},{11,3},{4,12},{12,4},... | collective-permute-start | bytes 393224 | tf_op jit(solution)/shard_map/ppermute | solution.py:230
  14.7 1.0 %collective-permute-done = f32[16,16,128]{2,1,0:T(8,128)S(1)} collective-permute-done((f32[16,16,128]{2,1,0:T(8,128)S(1)}, f32[16,16,128]{2,1,0:T(8,128)S(1)}, u32[]{:S(2)}, u32[]{:S(2)}) %collective-permute-start) | collective-permute-done | bytes 131104 | tf_op jit(solution)/shard_map/ppermute | solution.py:230
  15.7 11.7 %all_to_all.25 = f32[16,16,128]{2,1,0:T(8,128)S(1)} all-to-all(f32[16,16,128]{2,1,0:T(8,128)S(1)} %add.15), channel_id=1, replica_groups=mesh['y'=4,'x'=4,'core'=2,'z'=8] {'y','x'}, dimensions={0} | all-to-all | bytes 262144 | tf_op jit(solution)/shard_map/all_to_all | solution.py:234
  27.4 15.2 %all_to_all.26 = f32[8,16,128]{2,1,0:T(8,128)S(1)} all-to-all(f32[8,16,128]{2,1,0:T(8,128)S(1)} %broadcast_in_dim.8), channel_id=1, replica_groups=mesh['y'=4,'x'=4,'core'=2,'z'=8] {'z'}, dimensions={0} | all-to-all | bytes 131072 | tf_op jit(solution)/shard_map/all_to_all | solution.py:234
  42.7 10.0 %all_to_all.27.half_ref = f32[16,16,128]{2,1,0:T(8,128)S(1)} all-to-all(f32[16,16,128]{2,1,0:T(8,128)S(1)} %broadcast_in_dim.9), channel_id=1, replica_groups=mesh['y'=4,'x'=4,'core'=2,'z'=8] {'y','x'}, dimensions={0} | all-to-all | bytes 262144 | tf_op jit(solution)/shard_map/all_to_all | solution.py:234
  52.7 4.3 %collective-permute-start.1 = (f32[16,16,128]{2,1,0:T(8,128)S(1)}, f32[16,16,128]{2,1,0:T(8,128)S(1)}, u32[]{:S(2)}, u32[]{:S(2)}) collective-permute-start(f32[16,16,128]{2,1,0:T(8,128)S(1)} %all_to_all.27.half_ref), channel_id=1, source_target_pairs={{0,8},{8,0},{1,9},{9,1},{2,10},{10,2},{3,11},{11,3},{4,12},{12,4},... | collective-permute-start | bytes 393224 | tf_op jit(solution)/shard_map/ppermute | solution.py:230
  57.0 1.0 %collective-permute-done.1.other_ref = f32[16,16,128]{2,1,0:T(8,128)S(1)} collective-permute-done((f32[16,16,128]{2,1,0:T(8,128)S(1)}, f32[16,16,128]{2,1,0:T(8,128)S(1)}, u32[]{:S(2)}, u32[]{:S(2)}) %collective-permute-start.1) | collective-permute-done | bytes 131104 | tf_op jit(solution)/shard_map/ppermute | solution.py:230
  58.0 3.4 %shard_map.59 = (bf16[64,1024]{1,0:T(8,128)(2,1)S(1)}, f32[16,8,384]{2,1,0:T(8,128)S(1)}, f32[16,8,384]{2,1,0:T(8,128)S(1)}) custom-call(s32[1]{0:T(128)} %bitcast.core_ref, f32[16,16,128]{2,1,0:T(8,128)S(1)} %all_to_all.27.half_ref, f32[16,16,128]{2,1,0:T(8,128)S(1)} %collective-permute-done.1.other_ref, bf16[1024,1536]{1,0:T(8,128)(2,1)S(1)} %get-tuple-element.14.merged_ref), custom_call_target="tpu_custom_call" | custom-call | flops 201326592 | bytes 3145728 | tf_op jit(solution)/shard_map/pallas_call | solution.py:160
  61.4 0.4 collective-permute-start.2
  61.8 1.1 %collective-permute-done.2 = f32[16,8,384]{2,1,0:T(8,128)S(1)} collective-permute-done((f32[16,8,384]{2,1,0:T(8,128)S(1)}, f32[16,8,384]{2,1,0:T(8,128)S(1)}, u32[]{:S(2)}, u32[]{:S(2)}) %collective-permute-start.2) | collective-permute-done | bytes 196640 | tf_op jit(solution)/shard_map/ppermute | solution.py:230
  62.9 10.0 %all_to_all.28 = f32[16,8,384]{2,1,0:T(8,128)S(1)} all-to-all(f32[16,8,384]{2,1,0:T(8,128)S(1)} %add.16), channel_id=1, replica_groups=mesh['y'=4,'x'=4,'core'=2,'z'=8] {'y','x'}, dimensions={0} | all-to-all | bytes 393216 | tf_op jit(solution)/shard_map/all_to_all | solution.py:234
  73.0 10.5 %all_to_all.29.half_ref = f32[16,8,384]{2,1,0:T(8,128)} all-to-all(f32[16,8,384]{2,1,0:T(8,128)S(1)} %broadcast_in_dim.10), channel_id=1, replica_groups=mesh['y'=4,'x'=4,'core'=2,'z'=8] {'y','x'}, dimensions={0} | all-to-all | bytes 393216 | tf_op jit(solution)/shard_map/all_to_all | solution.py:234
  83.4 2.9 %collective-permute-start.3 = (f32[16,8,384]{2,1,0:T(8,128)}, f32[16,8,384]{2,1,0:T(8,128)}, u32[]{:S(2)}, u32[]{:S(2)}) collective-permute-start(f32[16,8,384]{2,1,0:T(8,128)} %all_to_all.29.half_ref), channel_id=1, source_target_pairs={{0,8},{8,0},{1,9},{9,1},{2,10},{10,2},{3,11},{11,3},{4,12},{12,4},... | collective-permute-start | bytes 589832 | tf_op jit(solution)/shard_map/ppermute | solution.py:230
  86.4 0.2 copy.8
  86.6 1.2 %collective-permute-done.3.other_ref = f32[16,8,384]{2,1,0:T(8,128)} collective-permute-done((f32[16,8,384]{2,1,0:T(8,128)}, f32[16,8,384]{2,1,0:T(8,128)}, u32[]{:S(2)}, u32[]{:S(2)}) %collective-permute-start.3) | collective-permute-done | bytes 196640 | tf_op jit(solution)/shard_map/ppermute | solution.py:230
  87.8 3.8 %shard_map.60 = (bf16[32,1536]{1,0:T(8,128)(2,1)}, f32[64,1536]{1,0:T(8,128)}, bf16[1024,1536]{1,0:T(8,128)(2,1)}) custom-call(s32[1]{0:T(128)} %bitcast.core_ref, f32[16,8,384]{2,1,0:T(8,128)} %all_to_all.29.half_ref, f32[16,8,384]{2,1,0:T(8,128)} %collective-permute-done.3.other_ref, bf16[1024,64]{1,0:T(8,128)(2,1)S(1)} %bitcast.11, ...), custom_call_target="tpu_custom_call" | custom-call | flops 201326592 | bytes 6291456 | tf_op jit(solution)/shard_map/pallas_call | solution.py:208
  (11 shorter events, 0.1 us)
Async XLA Ops:
  0.6 1.9 %copy-start = (bf16[1,1024,1536]{2,1,0:T(8,128)(2,1)S(1)}, bf16[1,1024,1536]{2,1,0:T(8,128)(2,1)}, u32[]{:S(2)}) copy-start(bf16[1,1024,1536]{2,1,0:T(8,128)(2,1)} %param.3) | copy-start | bytes 9437188
  2.5 1.9 %copy-start.1 = (bf16[1,1024,1536]{2,1,0:T(8,128)(2,1)S(1)}, bf16[1,1024,1536]{2,1,0:T(8,128)(2,1)}, u32[]{:S(2)}) copy-start(bf16[1,1024,1536]{2,1,0:T(8,128)(2,1)} %param.4) | copy-start | bytes 9437188
  4.4 1.0 %copy-start.2 = (f32[1536,64]{0,1:T(8,128)S(1)}, f32[1536,64]{0,1:T(8,128)}, u32[]{:S(2)}) copy-start(f32[1536,64]{0,1:T(8,128)} %param.5) | copy-start | bytes 1179652
  11.4 4.3 %collective-permute-start = (f32[16,16,128]{2,1,0:T(8,128)S(1)}, f32[16,16,128]{2,1,0:T(8,128)S(1)}, u32[]{:S(2)}, u32[]{:S(2)}) collective-permute-start(f32[16,16,128]{2,1,0:T(8,128)S(1)} %get-tuple-element.13), channel_id=1, source_target_pairs={{0,8},{8,0},{1,9},{9,1},{2,10},{10,2},{3,11},{11,3},{4,12},{12,4},... | collective-permute-start | bytes 393224 | tf_op jit(solution)/shard_map/ppermute | solution.py:230
  52.7 5.2 %collective-permute-start.1 = (f32[16,16,128]{2,1,0:T(8,128)S(1)}, f32[16,16,128]{2,1,0:T(8,128)S(1)}, u32[]{:S(2)}, u32[]{:S(2)}) collective-permute-start(f32[16,16,128]{2,1,0:T(8,128)S(1)} %all_to_all.27.half_ref), channel_id=1, source_target_pairs={{0,8},{8,0},{1,9},{9,1},{2,10},{10,2},{3,11},{11,3},{4,12},{12,4},... | collective-permute-start | bytes 393224 | tf_op jit(solution)/shard_map/ppermute | solution.py:230
  61.4 1.5 %collective-permute-start.2 = (f32[16,8,384]{2,1,0:T(8,128)S(1)}, f32[16,8,384]{2,1,0:T(8,128)S(1)}, u32[]{:S(2)}, u32[]{:S(2)}) collective-permute-start(f32[16,8,384]{2,1,0:T(8,128)S(1)} %get-tuple-element.16), channel_id=1, source_target_pairs={{0,8},{8,0},{1,9},{9,1},{2,10},{10,2},{3,11},{11,3},{4,12},{12,4},... | collective-permute-start | bytes 589832 | tf_op jit(solution)/shard_map/ppermute | solution.py:230
  83.4 4.3 %collective-permute-start.3 = (f32[16,8,384]{2,1,0:T(8,128)}, f32[16,8,384]{2,1,0:T(8,128)}, u32[]{:S(2)}, u32[]{:S(2)}) collective-permute-start(f32[16,8,384]{2,1,0:T(8,128)} %all_to_all.29.half_ref), channel_id=1, source_target_pairs={{0,8},{8,0},{1,9},{9,1},{2,10},{10,2},{3,11},{11,3},{4,12},{12,4},... | collective-permute-start | bytes 589832 | tf_op jit(solution)/shard_map/ppermute | solution.py:230

commit v4 on v3

--- a/solution.py
+++ b/solution.py
@@ -9,8 +9,9 @@
 VMEM_LIMIT = 32 * 1024 * 1024
 WHOLE = pl.BlockSpec(memory_space=pltpu.VMEM)
 SCALAR = pl.BlockSpec(memory_space=pltpu.SMEM)
-IN_HBM = pl.BlockSpec(memory_space=pltpu.HBM)
-CHUNK = 128
+ANYWHERE = pl.BlockSpec(memory_space=pl.ANY)
+MERGE_CHUNK = 512
+FINISH_CHUNK = 128
 GROUP = 8
 
 
@@ -19,14 +20,16 @@
 
 
 def merge_kernel(core_ref, grads_ref, errors_ref, prior_ref, merged_ref, keep_ref, give_ref,
-                 grads_held, errors_held, sems):
+                 grads_held, errors_held, prior_held, sems, prior_sem):
     core = core_ref[0]
     rank = prior_ref.shape[0]
     rows = merged_ref.shape[0]
-    chunks = rows // CHUNK
+    chunks = rows // MERGE_CHUNK
+    prior_fetch = pltpu.make_async_copy(prior_ref, prior_held, prior_sem)
+    prior_fetch.start()
     fetches = []
     for i in range(chunks):
-        block = pl.ds(CHUNK * i, CHUNK)
+        block = pl.ds(MERGE_CHUNK * i, MERGE_CHUNK)
         pair = (
             pltpu.make_async_copy(grads_ref.at[block], grads_held.at[block], sems.at[0, i]),
             pltpu.make_async_copy(errors_ref.at[block], errors_held.at[block], sems.at[1, i]),
@@ -34,22 +37,25 @@
         for fetch in pair:
             fetch.start()
         fetches.append(pair)
-    prior = prior_ref[...].astype(jnp.bfloat16)
     for i in range(chunks):
-        block = pl.ds(CHUNK * i, CHUNK)
+        block = pl.ds(MERGE_CHUNK * i, MERGE_CHUNK)
         for fetch in fetches[i]:
             fetch.wait()
         merged = (
             grads_held[block].astype(jnp.float32) + errors_held[block].astype(jnp.float32)
         ).astype(jnp.bfloat16)
         merged_ref[block] = merged
+        if i == 0:
+            prior_fetch.wait()
+            prior = prior_held[...].astype(jnp.bfloat16)
         left = lax.dot_general(
             prior, merged, (((1,), (1,)), ((), ())), preferred_element_type=jnp.float32
         )
         keep, give = own_first(core, left[: rank // 2], left[rank // 2 :])
+        lanes = MERGE_CHUNK // 128
         for down in range(rank // 32):
-            for lane in range(CHUNK // 128):
-                place = down * (rows // 128) + i * (CHUNK // 128) + lane
+            for lane in range(lanes):
+                place = down * (rows // 128) + i * lanes + lane
                 tile = (slice(16 * down, 16 * down + 16), slice(128 * lane, 128 * lane + 128))
                 keep_ref[place] = keep[tile]
                 give_ref[place] = give[tile]
@@ -61,19 +67,21 @@
     tiles = jax.ShapeDtypeStruct((rows // 128 * (rank // 32), 16, 128), jnp.float32)
     return pl.pallas_call(
         merge_kernel,
-        in_specs=[SCALAR, IN_HBM, IN_HBM, WHOLE],
+        in_specs=[SCALAR, ANYWHERE, ANYWHERE, ANYWHERE],
         out_specs=[WHOLE, WHOLE, WHOLE],
-        out_shape=[jax.ShapeDtypeStruct(grads.shape, jnp.bfloat16), tiles, tiles],
+        out_shape=[pltpu.VMEM(grads.shape, jnp.bfloat16), tiles, tiles],
         scratch_shapes=[
             pltpu.VMEM(grads.shape, jnp.bfloat16),
             pltpu.VMEM(grads.shape, jnp.bfloat16),
-            pltpu.SemaphoreType.DMA((2, rows // CHUNK)),
+            pltpu.VMEM(prior.shape, jnp.float32),
+            pltpu.SemaphoreType.DMA((2, rows // MERGE_CHUNK)),
+            pltpu.SemaphoreType.DMA,
         ],
         compiler_params=pltpu.CompilerParams(vmem_limit_bytes=VMEM_LIMIT),
         cost_estimate=pl.CostEstimate(
             flops=2 * rows * columns * rank, bytes_accessed=6 * rows * columns, transcendentals=0
         ),
-    )(core, grads, errors, prior)
+    )(core, *[pltpu.with_memory_space_constraint(x, pltpu.HBM) for x in (grads, errors, prior)])
 
 
 def inverse_factor(gram):
@@ -186,8 +194,8 @@
         right_ref[:, wide * lane : wide * lane + wide] = right
     cast = cast_ref[...]
     stores = []
-    for i in range(merged_ref.shape[0] // CHUNK):
-        block = pl.ds(CHUNK * i, CHUNK)
+    for i in range(merged_ref.shape[0] // FINISH_CHUNK):
+        block = pl.ds(FINISH_CHUNK * i, FINISH_CHUNK)
         full_update = jnp.dot(ortho_ref[block], cast, preferred_element_type=jnp.float32)
         errors_held[block] = (
             merged_ref[block].astype(jnp.float32) - full_update
@@ -208,7 +216,7 @@
     return pl.pallas_call(
         finish_kernel,
         in_specs=[SCALAR, WHOLE, WHOLE, WHOLE, WHOLE, WHOLE],
-        out_specs=[WHOLE, WHOLE, IN_HBM],
+        out_specs=[WHOLE, WHOLE, ANYWHERE],
         out_shape=[
             jax.ShapeDtypeStruct((own.shape[0], columns), jnp.bfloat16),
             jax.ShapeDtypeStruct((rank, columns), jnp.float32),
@@ -217,7 +225,7 @@
         scratch_shapes=[
             pltpu.VMEM((rank, columns), jnp.bfloat16),
             pltpu.VMEM(merged.shape, jnp.bfloat16),
-            pltpu.SemaphoreType.DMA((rows // CHUNK,)),
+            pltpu.SemaphoreType.DMA((rows // FINISH_CHUNK,)),
         ],
         compiler_params=pltpu.CompilerParams(vmem_limit_bytes=VMEM_LIMIT),
         cost_estimate=pl.CostEstimate(

time: 92 us -> 84.8 us (0.922)
  local copies, waits for them, and re-layouts: 4.98 us -> 0.21 us
  Pallas kernels: 13.2 us -> 10.9 us
    unnamed x6 -> x0, local copies, waits for them, and re-layouts: 4.77 us -> none
    pallas_call x1, Pallas kernels: 5.97 us -> 3.67 us  [merge(): pl.pallas_call(merge_kernel, in_specs=[SCALAR, ANYWHERE, ANYWHERE, ANYWHE...]
where the time goes in v4:
time: 84.8 us; the launch traced here: 84.5 us
  blocking collectives  57.3 us (68%)
  starting transfers between devices  11 us (13%)
  Pallas kernels  10.9 us (13%)
  waiting for transfers between devices  4.27 us (5%)
    all_to_all x5, blocking collectives, exchange(): return lax.all_to_all(value, axes, 0, 0)  57.3 us
    ppermute x4, starting transfers between devices, swap_cores(): return lax.ppermute(value, 'core', [(0, 1), (1, 0)])  11 us
    ppermute x4, waiting for transfers between devices, swap_cores(): return lax.ppermute(value, 'core', [(0, 1), (1, 0)])  4.27 us
    pallas_call x1, Pallas kernels, finish(): pl.pallas_call(finish_kernel, in_specs=[SCALAR, WHOLE, WHOLE, WHOLE, WHOL...  3.78 us
    pallas_call x1, Pallas kernels, merge(): pl.pallas_call(merge_kernel, in_specs=[SCALAR, ANYWHERE, ANYWHERE, ANYWHE...  3.67 us
    pallas_call x1, Pallas kernels, orthonormal(): pl.pallas_call(ortho_kernel, in_specs=[SCALAR, WHOLE, WHOLE, WHOLE], out_...  3.41 us
  transfers between devices with their start and end apart: 4, of which 4 were waited for; matrix products, arithmetic and copies ran while one was open for 0% of the time, Pallas kernels for 0%

profile of v4, /device:TPU:1, one launch (start us, length us, event | category | flops | bytes accessed | tf_op | source)
XLA Modules:
  0.0 84.5 jit_solution(2366698428160462631)
XLA Ops:
  0.6 3.7 %shard_map.58 = (bf16[1024,1536]{1,0:T(8,128)(2,1)S(1)}, f32[16,16,128]{2,1,0:T(8,128)S(1)}, f32[16,16,128]{2,1,0:T(8,128)S(1)}) custom-call(s32[1]{0:T(128)} %bitcast.core_ref, bf16[1024,1536]{1,0:T(8,128)(2,1)} %bitcast.10, bf16[1024,1536]{1,0:T(8,128)(2,1)} %bitcast.11, f32[64,1536]{1,0:T(8,128)} %bitcast.12), custom_call_target="tpu_custom_call" | custom-call | flops 201326592 | bytes 9437184 | tf_op jit(solution)/shard_map/pallas_call | solution.py:68
  4.3 3.3 %collective-permute-start = (f32[16,16,128]{2,1,0:T(8,128)S(1)}, f32[16,16,128]{2,1,0:T(8,128)S(1)}, u32[]{:S(2)}, u32[]{:S(2)}) collective-permute-start(f32[16,16,128]{2,1,0:T(8,128)S(1)} %get-tuple-element.13), channel_id=1, source_target_pairs={{0,8},{8,0},{1,9},{9,1},{2,10},{10,2},{3,11},{11,3},{4,12},{12,4},... | collective-permute-start | bytes 393224 | tf_op jit(solution)/shard_map/ppermute | solution.py:238
  7.6 1.0 %collective-permute-done = f32[16,16,128]{2,1,0:T(8,128)S(1)} collective-permute-done((f32[16,16,128]{2,1,0:T(8,128)S(1)}, f32[16,16,128]{2,1,0:T(8,128)S(1)}, u32[]{:S(2)}, u32[]{:S(2)}) %collective-permute-start) | collective-permute-done | bytes 131104 | tf_op jit(solution)/shard_map/ppermute | solution.py:238
  8.6 11.7 %all_to_all.25 = f32[16,16,128]{2,1,0:T(8,128)S(1)} all-to-all(f32[16,16,128]{2,1,0:T(8,128)S(1)} %add.15), channel_id=1, replica_groups=mesh['y'=4,'x'=4,'core'=2,'z'=8] {'y','x'}, dimensions={0} | all-to-all | bytes 262144 | tf_op jit(solution)/shard_map/all_to_all | solution.py:242
  20.3 15.2 %all_to_all.26 = f32[8,16,128]{2,1,0:T(8,128)S(1)} all-to-all(f32[8,16,128]{2,1,0:T(8,128)S(1)} %broadcast_in_dim.8), channel_id=1, replica_groups=mesh['y'=4,'x'=4,'core'=2,'z'=8] {'z'}, dimensions={0} | all-to-all | bytes 131072 | tf_op jit(solution)/shard_map/all_to_all | solution.py:242
  35.6 10.0 %all_to_all.27.half_ref = f32[16,16,128]{2,1,0:T(8,128)S(1)} all-to-all(f32[16,16,128]{2,1,0:T(8,128)S(1)} %broadcast_in_dim.9), channel_id=1, replica_groups=mesh['y'=4,'x'=4,'core'=2,'z'=8] {'y','x'}, dimensions={0} | all-to-all | bytes 262144 | tf_op jit(solution)/shard_map/all_to_all | solution.py:242
  45.6 4.3 %collective-permute-start.1 = (f32[16,16,128]{2,1,0:T(8,128)S(1)}, f32[16,16,128]{2,1,0:T(8,128)S(1)}, u32[]{:S(2)}, u32[]{:S(2)}) collective-permute-start(f32[16,16,128]{2,1,0:T(8,128)S(1)} %all_to_all.27.half_ref), channel_id=1, source_target_pairs={{0,8},{8,0},{1,9},{9,1},{2,10},{10,2},{3,11},{11,3},{4,12},{12,4},... | collective-permute-start | bytes 393224 | tf_op jit(solution)/shard_map/ppermute | solution.py:238
  49.9 1.0 %collective-permute-done.1.other_ref = f32[16,16,128]{2,1,0:T(8,128)S(1)} collective-permute-done((f32[16,16,128]{2,1,0:T(8,128)S(1)}, f32[16,16,128]{2,1,0:T(8,128)S(1)}, u32[]{:S(2)}, u32[]{:S(2)}) %collective-permute-start.1) | collective-permute-done | bytes 131104 | tf_op jit(solution)/shard_map/ppermute | solution.py:238
  50.9 3.4 %shard_map.59 = (bf16[64,1024]{1,0:T(8,128)(2,1)S(1)}, f32[16,8,384]{2,1,0:T(8,128)S(1)}, f32[16,8,384]{2,1,0:T(8,128)S(1)}) custom-call(s32[1]{0:T(128)} %bitcast.core_ref, f32[16,16,128]{2,1,0:T(8,128)S(1)} %all_to_all.27.half_ref, f32[16,16,128]{2,1,0:T(8,128)S(1)} %collective-permute-done.1.other_ref, bf16[1024,1536]{1,0:T(8,128)(2,1)S(1)} %get-tuple-element.14.merged_ref), custom_call_target="tpu_custom_call" | custom-call | flops 201326592 | bytes 3145728 | tf_op jit(solution)/shard_map/pallas_call | solution.py:168
  54.3 0.4 collective-permute-start.2
  54.7 1.1 %collective-permute-done.2 = f32[16,8,384]{2,1,0:T(8,128)S(1)} collective-permute-done((f32[16,8,384]{2,1,0:T(8,128)S(1)}, f32[16,8,384]{2,1,0:T(8,128)S(1)}, u32[]{:S(2)}, u32[]{:S(2)}) %collective-permute-start.2) | collective-permute-done | bytes 196640 | tf_op jit(solution)/shard_map/ppermute | solution.py:238
  55.8 10.0 %all_to_all.28 = f32[16,8,384]{2,1,0:T(8,128)S(1)} all-to-all(f32[16,8,384]{2,1,0:T(8,128)S(1)} %add.16), channel_id=1, replica_groups=mesh['y'=4,'x'=4,'core'=2,'z'=8] {'y','x'}, dimensions={0} | all-to-all | bytes 393216 | tf_op jit(solution)/shard_map/all_to_all | solution.py:242
  65.9 10.5 %all_to_all.29.half_ref = f32[16,8,384]{2,1,0:T(8,128)} all-to-all(f32[16,8,384]{2,1,0:T(8,128)S(1)} %broadcast_in_dim.10), channel_id=1, replica_groups=mesh['y'=4,'x'=4,'core'=2,'z'=8] {'y','x'}, dimensions={0} | all-to-all | bytes 393216 | tf_op jit(solution)/shard_map/all_to_all | solution.py:242
  76.4 2.9 %collective-permute-start.3 = (f32[16,8,384]{2,1,0:T(8,128)}, f32[16,8,384]{2,1,0:T(8,128)}, u32[]{:S(2)}, u32[]{:S(2)}) collective-permute-start(f32[16,8,384]{2,1,0:T(8,128)} %all_to_all.29.half_ref), channel_id=1, source_target_pairs={{0,8},{8,0},{1,9},{9,1},{2,10},{10,2},{3,11},{11,3},{4,12},{12,4},... | collective-permute-start | bytes 589832 | tf_op jit(solution)/shard_map/ppermute | solution.py:238
  79.3 0.2 copy.8
  79.5 1.2 %collective-permute-done.3.other_ref = f32[16,8,384]{2,1,0:T(8,128)} collective-permute-done((f32[16,8,384]{2,1,0:T(8,128)}, f32[16,8,384]{2,1,0:T(8,128)}, u32[]{:S(2)}, u32[]{:S(2)}) %collective-permute-start.3) | collective-permute-done | bytes 196640 | tf_op jit(solution)/shard_map/ppermute | solution.py:238
  80.7 3.8 %shard_map.60 = (bf16[32,1536]{1,0:T(8,128)(2,1)}, f32[64,1536]{1,0:T(8,128)}, bf16[1024,1536]{1,0:T(8,128)(2,1)}) custom-call(s32[1]{0:T(128)} %bitcast.core_ref, f32[16,8,384]{2,1,0:T(8,128)} %all_to_all.29.half_ref, f32[16,8,384]{2,1,0:T(8,128)} %collective-permute-done.3.other_ref, bf16[1024,64]{1,0:T(8,128)(2,1)S(1)} %bitcast.9, ...), custom_call_target="tpu_custom_call" | custom-call | flops 201326592 | bytes 6291456 | tf_op jit(solution)/shard_map/pallas_call | solution.py:216
  (11 shorter events, 0.1 us)
Async XLA Ops:
  4.3 4.3 %collective-permute-start = (f32[16,16,128]{2,1,0:T(8,128)S(1)}, f32[16,16,128]{2,1,0:T(8,128)S(1)}, u32[]{:S(2)}, u32[]{:S(2)}) collective-permute-start(f32[16,16,128]{2,1,0:T(8,128)S(1)} %get-tuple-element.13), channel_id=1, source_target_pairs={{0,8},{8,0},{1,9},{9,1},{2,10},{10,2},{3,11},{11,3},{4,12},{12,4},... | collective-permute-start | bytes 393224 | tf_op jit(solution)/shard_map/ppermute | solution.py:238
  45.6 5.2 %collective-permute-start.1 = (f32[16,16,128]{2,1,0:T(8,128)S(1)}, f32[16,16,128]{2,1,0:T(8,128)S(1)}, u32[]{:S(2)}, u32[]{:S(2)}) collective-permute-start(f32[16,16,128]{2,1,0:T(8,128)S(1)} %all_to_all.27.half_ref), channel_id=1, source_target_pairs={{0,8},{8,0},{1,9},{9,1},{2,10},{10,2},{3,11},{11,3},{4,12},{12,4},... | collective-permute-start | bytes 393224 | tf_op jit(solution)/shard_map/ppermute | solution.py:238
  54.3 1.5 %collective-permute-start.2 = (f32[16,8,384]{2,1,0:T(8,128)S(1)}, f32[16,8,384]{2,1,0:T(8,128)S(1)}, u32[]{:S(2)}, u32[]{:S(2)}) collective-permute-start(f32[16,8,384]{2,1,0:T(8,128)S(1)} %get-tuple-element.16), channel_id=1, source_target_pairs={{0,8},{8,0},{1,9},{9,1},{2,10},{10,2},{3,11},{11,3},{4,12},{12,4},... | collective-permute-start | bytes 589832 | tf_op jit(solution)/shard_map/ppermute | solution.py:238
  76.4 4.3 %collective-permute-start.3 = (f32[16,8,384]{2,1,0:T(8,128)}, f32[16,8,384]{2,1,0:T(8,128)}, u32[]{:S(2)}, u32[]{:S(2)}) collective-permute-start(f32[16,8,384]{2,1,0:T(8,128)} %all_to_all.29.half_ref), channel_id=1, source_target_pairs={{0,8},{8,0},{1,9},{9,1},{2,10},{10,2},{3,11},{11,3},{4,12},{12,4},... | collective-permute-start | bytes 589832 | tf_op jit(solution)/shard_map/ppermute | solution.py:238

commit v5 on v4

--- a/solution.py
+++ b/solution.py
@@ -19,9 +19,8 @@
     return jnp.where(core == 0, low, high), jnp.where(core == 0, high, low)
 
 
-def merge_kernel(core_ref, grads_ref, errors_ref, prior_ref, merged_ref, keep_ref, give_ref,
+def merge_kernel(grads_ref, errors_ref, prior_ref, merged_ref, left_ref,
                  grads_held, errors_held, prior_held, sems, prior_sem):
-    core = core_ref[0]
     rank = prior_ref.shape[0]
     rows = merged_ref.shape[0]
     chunks = rows // MERGE_CHUNK
@@ -51,25 +50,24 @@
         left = lax.dot_general(
             prior, merged, (((1,), (1,)), ((), ())), preferred_element_type=jnp.float32
         )
-        keep, give = own_first(core, left[: rank // 2], left[rank // 2 :])
         lanes = MERGE_CHUNK // 128
-        for down in range(rank // 32):
+        for down in range(rank // 16):
+            half, place = divmod(down, rank // 32)
             for lane in range(lanes):
-                place = down * (rows // 128) + i * lanes + lane
-                tile = (slice(16 * down, 16 * down + 16), slice(128 * lane, 128 * lane + 128))
-                keep_ref[place] = keep[tile]
-                give_ref[place] = give[tile]
-
-
-def merge(core, grads, errors, prior):
+                left_ref[place * (rows // 128) + i * lanes + lane, 16 * half : 16 * half + 16] = (
+                    left[16 * down : 16 * down + 16, 128 * lane : 128 * lane + 128]
+                )
+
+
+def merge(grads, errors, prior):
     rows, columns = grads.shape
     rank = prior.shape[0]
-    tiles = jax.ShapeDtypeStruct((rows // 128 * (rank // 32), 16, 128), jnp.float32)
+    tiles = jax.ShapeDtypeStruct((rows // 128 * (rank // 32), 32, 128), jnp.float32)
     return pl.pallas_call(
         merge_kernel,
-        in_specs=[SCALAR, ANYWHERE, ANYWHERE, ANYWHERE],
-        out_specs=[WHOLE, WHOLE, WHOLE],
-        out_shape=[pltpu.VMEM(grads.shape, jnp.bfloat16), tiles, tiles],
+        in_specs=[ANYWHERE, ANYWHERE, ANYWHERE],
+        out_specs=[WHOLE, WHOLE],
+        out_shape=[pltpu.VMEM(grads.shape, jnp.bfloat16), tiles],
         scratch_shapes=[
             pltpu.VMEM(grads.shape, jnp.bfloat16),
             pltpu.VMEM(grads.shape, jnp.bfloat16),
@@ -81,7 +79,7 @@
         cost_estimate=pl.CostEstimate(
             flops=2 * rows * columns * rank, bytes_accessed=6 * rows * columns, transcendentals=0
         ),
-    )(core, *[pltpu.with_memory_space_constraint(x, pltpu.HBM) for x in (grads, errors, prior)])
+    )(*[pltpu.with_memory_space_constraint(x, pltpu.HBM) for x in (grads, errors, prior)])
 
 
 def inverse_factor(gram):
@@ -126,17 +124,17 @@
     return jnp.concatenate(groups)[:, rank:]
 
 
-def ortho_kernel(core_ref, half_ref, other_ref, merged_ref, ortho_ref, keep_ref, give_ref,
+def ortho_kernel(core_ref, own_ref, other_ref, merged_ref, ortho_ref, keep_ref, give_ref,
                  left_ref):
     core = core_ref[0]
     rank, rows = left_ref.shape
     across = rows // 128
-    for place in range(half_ref.shape[0]):
-        low, high = own_first(core, half_ref[place], other_ref[place])
-        down = 16 * (place // across)
+    for place in range(own_ref.shape[0]):
+        tile = jnp.where(core == 1, own_ref[place], other_ref[place])
         lane = pl.ds(128 * (place % across), 128)
-        left_ref[pl.ds(down, 16), lane] = low
-        left_ref[pl.ds(rank // 2 + down, 16), lane] = high
+        for half in range(2):
+            down = rank // 2 * half + 16 * (place // across)
+            left_ref[pl.ds(down, 16), lane] = tile[16 * half : 16 * half + 16]
     left = left_ref[...]
     gram = lax.dot_general(
         left, left, (((1,), (1,)), ((), ())), precision=lax.Precision.HIGHEST,
@@ -160,9 +158,9 @@
             give_ref[down * count + lane] = give[8 * down : 8 * down + 8]
 
 
-def orthonormal(core, half, other, merged, parts):
+def orthonormal(core, own, other, merged, parts):
     rows, columns = merged.shape
-    rank = half.size * 2 // rows
+    rank = own.size // rows
     wide = rank * columns // (8 * parts)
     tiles = jax.ShapeDtypeStruct((parts // 2, 8, wide), jnp.float32)
     return pl.pallas_call(
@@ -175,7 +173,7 @@
         cost_estimate=pl.CostEstimate(
             flops=2 * rows * columns * rank, bytes_accessed=2 * rows * columns, transcendentals=0
         ),
-    )(core, half, other, merged)
+    )(core, own, other, merged)
 
 
 def finish_kernel(core_ref, half_ref, other_ref, ortho_ref, own_ref, merged_ref,
@@ -252,12 +250,15 @@
     depth = lax.axis_size("z")
     replicas = 2 * pairs
 
-    merged, keep, give = merge(core, grads[0], errors[0], q_prev.T)
-    mine = jnp.sum(exchange(keep + swap_cores(give), YX), axis=0)
-    mine = jnp.sum(exchange(spread(mine, depth), "z"), axis=0) / replicas
-    half = exchange(spread(mine, pairs), YX)
-
-    ortho, keep, give = orthonormal(core, half, swap_cores(half), merged, replicas)
+    def reduce_left(total):
+        mine = jnp.sum(exchange(total, YX), axis=0)
+        mine = jnp.sum(exchange(spread(mine, depth), "z"), axis=0) / replicas
+        return exchange(spread(mine, pairs), YX)
+
+    merged, left = merge(grads[0], errors[0], q_prev.T)
+    left = lax.cond(core[0] == 1, reduce_left, lambda total: total, left + swap_cores(left))
+
+    ortho, keep, give = orthonormal(core, left, swap_cores(left), merged, replicas)
     mine = jnp.sum(exchange(keep + swap_cores(give), YX), axis=0) / replicas
     half = exchange(spread(mine, pairs), YX)
 

time: 84.8 us -> 86.5 us (1.020)
  starting transfers between devices: 11 us -> 5.94 us
  blocking collectives: 57.3 us -> 60.1 us
  other arithmetic: 0.1 us -> 1.77 us
  waiting for transfers between devices: 4.27 us -> 5.56 us
  Pallas kernels: 10.9 us -> 11.8 us
    ppermute x4, starting transfers between devices: 11 us -> 5.94 us  [swap_cores(): return lax.ppermute(value, 'core', [(0, 1), (1, 0)])]
    all_to_all x5, blocking collectives: 57.3 us -> 60.1 us  [exchange(): return lax.all_to_all(value, axes, 0, 0)]
    add x1, other arithmetic: 0.02 us -> 1.68 us  [per_device(): left + swap_cores(left)]
    ppermute x4, waiting for transfers between devices: 4.27 us -> 5.56 us  [swap_cores(): return lax.ppermute(value, 'core', [(0, 1), (1, 0)])]
    pallas_call x1, Pallas kernels: 3.41 us -> 4.36 us  [orthonormal(): pl.pallas_call(ortho_kernel, in_specs=[SCALAR, WHOLE, WHOLE, WHOLE], out_...]
where the time goes in v5:
time: 86.5 us; the launch traced here: 86.1 us
  blocking collectives  60.1 us (69%)
  Pallas kernels  11.8 us (14%)
  starting transfers between devices  5.94 us (7%)
  waiting for transfers between devices  5.56 us (6%)
  other arithmetic  1.77 us (2%)
    all_to_all x5, blocking collectives, exchange(): return lax.all_to_all(value, axes, 0, 0)  60.1 us
    ppermute x4, starting transfers between devices, swap_cores(): return lax.ppermute(value, 'core', [(0, 1), (1, 0)])  5.94 us
    ppermute x4, waiting for transfers between devices, swap_cores(): return lax.ppermute(value, 'core', [(0, 1), (1, 0)])  5.56 us
    pallas_call x1, Pallas kernels, orthonormal(): pl.pallas_call(ortho_kernel, in_specs=[SCALAR, WHOLE, WHOLE, WHOLE], out_...  4.36 us
    pallas_call x1, Pallas kernels, finish(): pl.pallas_call(finish_kernel, in_specs=[SCALAR, WHOLE, WHOLE, WHOLE, WHOL...  3.78 us
    pallas_call x1, Pallas kernels, merge(): pl.pallas_call(merge_kernel, in_specs=[ANYWHERE, ANYWHERE, ANYWHERE], out...  3.66 us
  transfers between devices with their start and end apart: 4, of which 4 were waited for; matrix products, arithmetic and copies ran while one was open for 0% of the time, Pallas kernels for 0%

profile of v5, /device:TPU:1, one launch (start us, length us, event | category | flops | bytes accessed | tf_op | source)
XLA Modules:
  0.0 86.1 jit_solution(846936604141756227)
XLA Ops:
  0.6 3.7 %shard_map.58 = (bf16[1024,1536]{1,0:T(8,128)(2,1)S(1)}, f32[16,32,128]{2,1,0:T(8,128)S(1)}) custom-call(bf16[1024,1536]{1,0:T(8,128)(2,1)} %bitcast.10, bf16[1024,1536]{1,0:T(8,128)(2,1)} %bitcast.11, f32[64,1536]{1,0:T(8,128)} %bitcast.12), custom_call_target="tpu_custom_call" | custom-call | flops 201326592 | bytes 9437184 | tf_op jit(solution)/shard_map/pallas_call | solution.py:66
  4.3 3.3 %collective-permute-start = (f32[16,32,128]{2,1,0:T(8,128)S(1)}, f32[16,32,128]{2,1,0:T(8,128)}, u32[]{:S(2)}, u32[]{:S(2)}) collective-permute-start(f32[16,32,128]{2,1,0:T(8,128)S(1)} %get-tuple-element.16), channel_id=1, source_target_pairs={{0,8},{8,0},{1,9},{9,1},{2,10},{10,2},{3,11},{11,3},{4,12},{12,4},... | collective-permute-start | bytes 786440 | tf_op jit(solution)/shard_map/ppermute | solution.py:236
  7.6 1.3 %collective-permute-done = f32[16,32,128]{2,1,0:T(8,128)} collective-permute-done((f32[16,32,128]{2,1,0:T(8,128)S(1)}, f32[16,32,128]{2,1,0:T(8,128)}, u32[]{:S(2)}, u32[]{:S(2)}) %collective-permute-start) | collective-permute-done | bytes 262176 | tf_op jit(solution)/shard_map/ppermute | solution.py:236
  8.9 1.7 %add.21 = f32[16,32,128]{2,1,0:T(8,128)} add(f32[16,32,128]{2,1,0:T(8,128)S(1)} %get-tuple-element.16, f32[16,32,128]{2,1,0:T(8,128)} %collective-permute-done) | non-fusion elementwise | flops 65536 | bytes 786432 | tf_op jit(solution)/shard_map/add | solution.py:259
  10.6 39.4 %conditional.1 = (f32[16,32,128]{2,1,0:T(8,128)}) conditional(s32[]{:T(128)} %convert_element_type.3, f32[16,32,128]{2,1,0:T(8,128)} %add.21, f32[16,32,128]{2,1,0:T(8,128)} %add.21), branch_computations={%region_0.0_spmd, %region_1.0_spmd} | conditional | flops 94208 | bytes 2195472 | solution.py:259
  10.6 12.6 %all_to_all.22 = f32[16,32,128]{2,1,0:T(8,128)S(1)} all-to-all(f32[16,32,128]{2,1,0:T(8,128)} %param.1), channel_id=1, replica_groups=mesh['y'=4,'x'=4,'core'=2,'z'=8] {'y','x'}, dimensions={0} | all-to-all | bytes 524288 | tf_op jit(solution)/shard_map/cond/branch_1_fun/all_to_all | solution.py:240
  23.2 15.9 %all_to_all.23 = f32[8,32,128]{2,1,0:T(8,128)S(1)} all-to-all(f32[8,32,128]{2,1,0:T(8,128)S(1)} %broadcast_in_dim.0), channel_id=1, replica_groups=mesh['y'=4,'x'=4,'core'=2,'z'=8] {'z'}, dimensions={0} | all-to-all | bytes 262144 | tf_op jit(solution)/shard_map/cond/branch_1_fun/all_to_all | solution.py:240
  39.2 10.8 %all_to_all.24 = f32[16,32,128]{2,1,0:T(8,128)} all-to-all(f32[16,32,128]{2,1,0:T(8,128)S(1)} %broadcast_in_dim.1), channel_id=1, replica_groups=mesh['y'=4,'x'=4,'core'=2,'z'=8] {'y','x'}, dimensions={0} | all-to-all | bytes 524288 | tf_op jit(solution)/shard_map/cond/branch_1_fun/all_to_all | solution.py:240
  50.0 0.0 collective-permute-start.1
  50.0 1.7 %collective-permute-done.1.other_ref = f32[16,32,128]{2,1,0:T(8,128)S(1)} collective-permute-done((f32[16,32,128]{2,1,0:T(8,128)}, f32[16,32,128]{2,1,0:T(8,128)S(1)}, u32[]{:S(2)}, u32[]{:S(2)}) %collective-permute-start.1) | collective-permute-done | bytes 262176 | tf_op jit(solution)/shard_map/ppermute | solution.py:236
  51.7 4.4 %shard_map.59 = (bf16[64,1024]{1,0:T(8,128)(2,1)S(1)}, f32[16,8,384]{2,1,0:T(8,128)S(1)}, f32[16,8,384]{2,1,0:T(8,128)S(1)}) custom-call(s32[1]{0:T(128)} %bitcast.core_ref, f32[16,32,128]{2,1,0:T(8,128)} %get-tuple-element.24.own_ref, f32[16,32,128]{2,1,0:T(8,128)S(1)} %collective-permute-done.1.other_ref, bf16[1024,1536]{1,0:T(8,128)(2,1)S(1)} %get-tuple-element.17.merged_ref), custom_call_target="tpu_custom_call" | custom-call | flops 201326592 | bytes 3145728 | tf_op jit(solution)/shard_map/pallas_call | solution.py:166
  56.1 0.2 collective-permute-start.2
  56.3 1.3 %collective-permute-done.2 = f32[16,8,384]{2,1,0:T(8,128)S(1)} collective-permute-done((f32[16,8,384]{2,1,0:T(8,128)S(1)}, f32[16,8,384]{2,1,0:T(8,128)S(1)}, u32[]{:S(2)}, u32[]{:S(2)}) %collective-permute-start.2) | collective-permute-done | bytes 196640 | tf_op jit(solution)/shard_map/ppermute | solution.py:236
  57.7 10.3 %all_to_all.25 = f32[16,8,384]{2,1,0:T(8,128)S(1)} all-to-all(f32[16,8,384]{2,1,0:T(8,128)S(1)} %add.22), channel_id=1, replica_groups=mesh['y'=4,'x'=4,'core'=2,'z'=8] {'y','x'}, dimensions={0} | all-to-all | bytes 393216 | tf_op jit(solution)/shard_map/all_to_all | solution.py:240
  68.0 10.5 %all_to_all.26.half_ref = f32[16,8,384]{2,1,0:T(8,128)} all-to-all(f32[16,8,384]{2,1,0:T(8,128)S(1)} %broadcast_in_dim.16), channel_id=1, replica_groups=mesh['y'=4,'x'=4,'core'=2,'z'=8] {'y','x'}, dimensions={0} | all-to-all | bytes 393216 | tf_op jit(solution)/shard_map/all_to_all | solution.py:240
  78.5 2.4 %collective-permute-start.3 = (f32[16,8,384]{2,1,0:T(8,128)}, f32[16,8,384]{2,1,0:T(8,128)}, u32[]{:S(2)}, u32[]{:S(2)}) collective-permute-start(f32[16,8,384]{2,1,0:T(8,128)} %all_to_all.26.half_ref), channel_id=1, source_target_pairs={{0,8},{8,0},{1,9},{9,1},{2,10},{10,2},{3,11},{11,3},{4,12},{12,4},... | collective-permute-start | bytes 589832 | tf_op jit(solution)/shard_map/ppermute | solution.py:236
  80.9 0.2 copy.8
  81.1 1.2 %collective-permute-done.3.other_ref = f32[16,8,384]{2,1,0:T(8,128)} collective-permute-done((f32[16,8,384]{2,1,0:T(8,128)}, f32[16,8,384]{2,1,0:T(8,128)}, u32[]{:S(2)}, u32[]{:S(2)}) %collective-permute-start.3) | collective-permute-done | bytes 196640 | tf_op jit(solution)/shard_map/ppermute | solution.py:236
  82.3 3.8 %shard_map.60 = (bf16[32,1536]{1,0:T(8,128)(2,1)}, f32[64,1536]{1,0:T(8,128)}, bf16[1024,1536]{1,0:T(8,128)(2,1)}) custom-call(s32[1]{0:T(128)} %bitcast.core_ref, f32[16,8,384]{2,1,0:T(8,128)} %all_to_all.26.half_ref, f32[16,8,384]{2,1,0:T(8,128)} %collective-permute-done.3.other_ref, bf16[1024,64]{1,0:T(8,128)(2,1)S(1)} %bitcast.9, ...), custom_call_target="tpu_custom_call" | custom-call | flops 201326592 | bytes 6291456 | tf_op jit(solution)/shard_map/pallas_call | solution.py:214
  (10 shorter events, 0.1 us)
Async XLA Ops:
  4.3 4.6 %collective-permute-start = (f32[16,32,128]{2,1,0:T(8,128)S(1)}, f32[16,32,128]{2,1,0:T(8,128)}, u32[]{:S(2)}, u32[]{:S(2)}) collective-permute-start(f32[16,32,128]{2,1,0:T(8,128)S(1)} %get-tuple-element.16), channel_id=1, source_target_pairs={{0,8},{8,0},{1,9},{9,1},{2,10},{10,2},{3,11},{11,3},{4,12},{12,4},... | collective-permute-start | bytes 786440 | tf_op jit(solution)/shard_map/ppermute | solution.py:236
  50.0 1.7 %collective-permute-start.1 = (f32[16,32,128]{2,1,0:T(8,128)}, f32[16,32,128]{2,1,0:T(8,128)S(1)}, u32[]{:S(2)}, u32[]{:S(2)}) collective-permute-start(f32[16,32,128]{2,1,0:T(8,128)} %get-tuple-element.24.own_ref), channel_id=1, source_target_pairs={{0,8},{8,0},{1,9},{9,1},{2,10},{10,2},{3,11},{11,3},{4,12},{12,4},... | collective-permute-start | bytes 786440 | tf_op jit(solution)/shard_map/ppermute | solution.py:236
  56.1 1.5 %collective-permute-start.2 = (f32[16,8,384]{2,1,0:T(8,128)S(1)}, f32[16,8,384]{2,1,0:T(8,128)S(1)}, u32[]{:S(2)}, u32[]{:S(2)}) collective-permute-start(f32[16,8,384]{2,1,0:T(8,128)S(1)} %get-tuple-element.19), channel_id=1, source_target_pairs={{0,8},{8,0},{1,9},{9,1},{2,10},{10,2},{3,11},{11,3},{4,12},{12,4},... | collective-permute-start | bytes 589832 | tf_op jit(solution)/shard_map/ppermute | solution.py:236
  78.5 3.8 %collective-permute-start.3 = (f32[16,8,384]{2,1,0:T(8,128)}, f32[16,8,384]{2,1,0:T(8,128)}, u32[]{:S(2)}, u32[]{:S(2)}) collective-permute-start(f32[16,8,384]{2,1,0:T(8,128)} %all_to_all.26.half_ref), channel_id=1, source_target_pairs={{0,8},{8,0},{1,9},{9,1},{2,10},{10,2},{3,11},{11,3},{4,12},{12,4},... | collective-permute-start | bytes 589832 | tf_op jit(solution)/shard_map/ppermute | solution.py:236

commit v6 on v4

--- a/solution.py
+++ b/solution.py
@@ -13,6 +13,10 @@
 MERGE_CHUNK = 512
 FINISH_CHUNK = 128
 GROUP = 8
+
+
+def in_vmem(value):
+    return pltpu.with_memory_space_constraint(value, pltpu.VMEM)
 
 
 def own_first(core, low, high):
@@ -179,7 +183,8 @@
 
 
 def finish_kernel(core_ref, half_ref, other_ref, ortho_ref, own_ref, merged_ref,
-                  update_ref, right_ref, errors_ref, cast_ref, errors_held, sems):
+                  update_ref, right_ref, errors_ref,
+                  cast_ref, update_held, right_held, errors_held, small_sems, sems):
     core = core_ref[0]
     rank = ortho_ref.shape[1]
     wide = half_ref.shape[2]
@@ -191,7 +196,7 @@
         ]
         right = jnp.concatenate([low for low, _ in pairs] + [high for _, high in pairs])
         cast_ref[:, wide * lane : wide * lane + wide] = right.astype(jnp.bfloat16)
-        right_ref[:, wide * lane : wide * lane + wide] = right
+        right_held[:, wide * lane : wide * lane + wide] = right
     cast = cast_ref[...]
     stores = []
     for i in range(merged_ref.shape[0] // FINISH_CHUNK):
@@ -200,12 +205,18 @@
         errors_held[block] = (
             merged_ref[block].astype(jnp.float32) - full_update
         ).astype(jnp.bfloat16)
-        store = pltpu.make_async_copy(errors_held.at[block], errors_ref.at[block], sems.at[i])
-        store.start()
-        stores.append(store)
-    update_ref[...] = jnp.dot(
-        own_ref[...], cast, preferred_element_type=jnp.float32
-    ).astype(jnp.bfloat16)
+        stores.append(
+            pltpu.make_async_copy(errors_held.at[block], errors_ref.at[block], sems.at[i])
+        )
+        stores[-1].start()
+        if i == 0:
+            stores.append(pltpu.make_async_copy(right_held, right_ref, small_sems.at[0]))
+            stores[-1].start()
+            update_held[...] = jnp.dot(
+                own_ref[...], cast, preferred_element_type=jnp.float32
+            ).astype(jnp.bfloat16)
+            stores.append(pltpu.make_async_copy(update_held, update_ref, small_sems.at[1]))
+            stores[-1].start()
     for store in stores:
         store.wait()
 
@@ -213,25 +224,29 @@
 def finish(core, half, other, ortho, own, merged):
     rows, columns = merged.shape
     rank = ortho.shape[1]
+    small = (own.shape[0], columns), (rank, columns)
     return pl.pallas_call(
         finish_kernel,
         in_specs=[SCALAR, WHOLE, WHOLE, WHOLE, WHOLE, WHOLE],
-        out_specs=[WHOLE, WHOLE, ANYWHERE],
+        out_specs=[ANYWHERE, ANYWHERE, ANYWHERE],
         out_shape=[
-            jax.ShapeDtypeStruct((own.shape[0], columns), jnp.bfloat16),
-            jax.ShapeDtypeStruct((rank, columns), jnp.float32),
-            jax.ShapeDtypeStruct(merged.shape, jnp.bfloat16),
+            pltpu.HBM(small[0], jnp.bfloat16),
+            pltpu.HBM(small[1], jnp.float32),
+            pltpu.HBM(merged.shape, jnp.bfloat16),
         ],
         scratch_shapes=[
-            pltpu.VMEM((rank, columns), jnp.bfloat16),
+            pltpu.VMEM(small[1], jnp.bfloat16),
+            pltpu.VMEM(small[0], jnp.bfloat16),
+            pltpu.VMEM(small[1], jnp.float32),
             pltpu.VMEM(merged.shape, jnp.bfloat16),
+            pltpu.SemaphoreType.DMA((2,)),
             pltpu.SemaphoreType.DMA((rows // FINISH_CHUNK,)),
         ],
         compiler_params=pltpu.CompilerParams(vmem_limit_bytes=VMEM_LIMIT),
         cost_estimate=pl.CostEstimate(
             flops=2 * rows * columns * rank, bytes_accessed=4 * rows * columns, transcendentals=0
         ),
-    )(core, half, other, ortho, own, merged)
+    )(core, in_vmem(half), in_vmem(other), ortho, own, merged)
 
 
 def swap_cores(value):

time: 84.8 us -> 84 us (level)
  no operation moved by 1% of the time
where the time goes in v6:
time: 84 us; the launch traced here: 83.7 us
  blocking collectives  57.3 us (68%)
  starting transfers between devices  11 us (13%)
  Pallas kernels  10.1 us (12%)
  waiting for transfers between devices  4.27 us (5%)
    all_to_all x5, blocking collectives, exchange(): return lax.all_to_all(value, axes, 0, 0)  57.3 us
    ppermute x4, starting transfers between devices, swap_cores(): return lax.ppermute(value, 'core', [(0, 1), (1, 0)])  11 us
    ppermute x4, waiting for transfers between devices, swap_cores(): return lax.ppermute(value, 'core', [(0, 1), (1, 0)])  4.27 us
    pallas_call x1, Pallas kernels, merge(): pl.pallas_call(merge_kernel, in_specs=[SCALAR, ANYWHERE, ANYWHERE, ANYWHE...  3.67 us
    pallas_call x1, Pallas kernels, orthonormal(): pl.pallas_call(ortho_kernel, in_specs=[SCALAR, WHOLE, WHOLE, WHOLE], out_...  3.41 us
    pallas_call x1, Pallas kernels, finish(): pl.pallas_call(finish_kernel, in_specs=[SCALAR, WHOLE, WHOLE, WHOLE, WHOL...  3.05 us
  transfers between devices with their start and end apart: 4, of which 4 were waited for; matrix products, arithmetic and copies ran while one was open for 0% of the time, Pallas kernels for 0%

profile of v6, /device:TPU:1, one launch (start us, length us, event | category | flops | bytes accessed | tf_op | source)
XLA Modules:
  0.0 83.7 jit_solution(296104260452083288)
XLA Ops:
  0.6 3.7 %shard_map.58 = (bf16[1024,1536]{1,0:T(8,128)(2,1)S(1)}, f32[16,16,128]{2,1,0:T(8,128)S(1)}, f32[16,16,128]{2,1,0:T(8,128)S(1)}) custom-call(s32[1]{0:T(128)} %bitcast.core_ref, bf16[1024,1536]{1,0:T(8,128)(2,1)} %bitcast.10, bf16[1024,1536]{1,0:T(8,128)(2,1)} %bitcast.11, f32[64,1536]{1,0:T(8,128)} %bitcast.12), custom_call_target="tpu_custom_call" | custom-call | flops 201326592 | bytes 9437184 | tf_op jit(solution)/shard_map/pallas_call | solution.py:72
  4.3 3.3 %collective-permute-start = (f32[16,16,128]{2,1,0:T(8,128)S(1)}, f32[16,16,128]{2,1,0:T(8,128)S(1)}, u32[]{:S(2)}, u32[]{:S(2)}) collective-permute-start(f32[16,16,128]{2,1,0:T(8,128)S(1)} %get-tuple-element.13), channel_id=1, source_target_pairs={{0,8},{8,0},{1,9},{9,1},{2,10},{10,2},{3,11},{11,3},{4,12},{12,4},... | collective-permute-start | bytes 393224 | tf_op jit(solution)/shard_map/ppermute | solution.py:253
  7.6 1.0 %collective-permute-done = f32[16,16,128]{2,1,0:T(8,128)S(1)} collective-permute-done((f32[16,16,128]{2,1,0:T(8,128)S(1)}, f32[16,16,128]{2,1,0:T(8,128)S(1)}, u32[]{:S(2)}, u32[]{:S(2)}) %collective-permute-start) | collective-permute-done | bytes 131104 | tf_op jit(solution)/shard_map/ppermute | solution.py:253
  8.6 11.7 %all_to_all.25 = f32[16,16,128]{2,1,0:T(8,128)S(1)} all-to-all(f32[16,16,128]{2,1,0:T(8,128)S(1)} %add.15), channel_id=1, replica_groups=mesh['y'=4,'x'=4,'core'=2,'z'=8] {'y','x'}, dimensions={0} | all-to-all | bytes 262144 | tf_op jit(solution)/shard_map/all_to_all | solution.py:257
  20.3 15.2 %all_to_all.26 = f32[8,16,128]{2,1,0:T(8,128)S(1)} all-to-all(f32[8,16,128]{2,1,0:T(8,128)S(1)} %broadcast_in_dim.8), channel_id=1, replica_groups=mesh['y'=4,'x'=4,'core'=2,'z'=8] {'z'}, dimensions={0} | all-to-all | bytes 131072 | tf_op jit(solution)/shard_map/all_to_all | solution.py:257
  35.6 10.0 %all_to_all.27.half_ref = f32[16,16,128]{2,1,0:T(8,128)S(1)} all-to-all(f32[16,16,128]{2,1,0:T(8,128)S(1)} %broadcast_in_dim.9), channel_id=1, replica_groups=mesh['y'=4,'x'=4,'core'=2,'z'=8] {'y','x'}, dimensions={0} | all-to-all | bytes 262144 | tf_op jit(solution)/shard_map/all_to_all | solution.py:257
  45.6 4.3 %collective-permute-start.1 = (f32[16,16,128]{2,1,0:T(8,128)S(1)}, f32[16,16,128]{2,1,0:T(8,128)S(1)}, u32[]{:S(2)}, u32[]{:S(2)}) collective-permute-start(f32[16,16,128]{2,1,0:T(8,128)S(1)} %all_to_all.27.half_ref), channel_id=1, source_target_pairs={{0,8},{8,0},{1,9},{9,1},{2,10},{10,2},{3,11},{11,3},{4,12},{12,4},... | collective-permute-start | bytes 393224 | tf_op jit(solution)/shard_map/ppermute | solution.py:253
  49.9 1.0 %collective-permute-done.1.other_ref = f32[16,16,128]{2,1,0:T(8,128)S(1)} collective-permute-done((f32[16,16,128]{2,1,0:T(8,128)S(1)}, f32[16,16,128]{2,1,0:T(8,128)S(1)}, u32[]{:S(2)}, u32[]{:S(2)}) %collective-permute-start.1) | collective-permute-done | bytes 131104 | tf_op jit(solution)/shard_map/ppermute | solution.py:253
  50.9 3.4 %shard_map.59 = (bf16[64,1024]{1,0:T(8,128)(2,1)S(1)}, f32[16,8,384]{2,1,0:T(8,128)S(1)}, f32[16,8,384]{2,1,0:T(8,128)S(1)}) custom-call(s32[1]{0:T(128)} %bitcast.core_ref, f32[16,16,128]{2,1,0:T(8,128)S(1)} %all_to_all.27.half_ref, f32[16,16,128]{2,1,0:T(8,128)S(1)} %collective-permute-done.1.other_ref, bf16[1024,1536]{1,0:T(8,128)(2,1)S(1)} %get-tuple-element.14.merged_ref), custom_call_target="tpu_custom_call" | custom-call | flops 201326592 | bytes 3145728 | tf_op jit(solution)/shard_map/pallas_call | solution.py:172
  54.3 0.4 collective-permute-start.2
  54.7 1.1 %collective-permute-done.2 = f32[16,8,384]{2,1,0:T(8,128)S(1)} collective-permute-done((f32[16,8,384]{2,1,0:T(8,128)S(1)}, f32[16,8,384]{2,1,0:T(8,128)S(1)}, u32[]{:S(2)}, u32[]{:S(2)}) %collective-permute-start.2) | collective-permute-done | bytes 196640 | tf_op jit(solution)/shard_map/ppermute | solution.py:253
  55.8 10.0 %all_to_all.28 = f32[16,8,384]{2,1,0:T(8,128)S(1)} all-to-all(f32[16,8,384]{2,1,0:T(8,128)S(1)} %add.16), channel_id=1, replica_groups=mesh['y'=4,'x'=4,'core'=2,'z'=8] {'y','x'}, dimensions={0} | all-to-all | bytes 393216 | tf_op jit(solution)/shard_map/all_to_all | solution.py:257
  65.9 10.5 %all_to_all.29.half_ref = f32[16,8,384]{2,1,0:T(8,128)} all-to-all(f32[16,8,384]{2,1,0:T(8,128)S(1)} %broadcast_in_dim.10), channel_id=1, replica_groups=mesh['y'=4,'x'=4,'core'=2,'z'=8] {'y','x'}, dimensions={0} | all-to-all | bytes 393216 | tf_op jit(solution)/shard_map/all_to_all | solution.py:257
  76.4 2.9 %collective-permute-start.3 = (f32[16,8,384]{2,1,0:T(8,128)}, f32[16,8,384]{2,1,0:T(8,128)}, u32[]{:S(2)}, u32[]{:S(2)}) collective-permute-start(f32[16,8,384]{2,1,0:T(8,128)} %all_to_all.29.half_ref), channel_id=1, source_target_pairs={{0,8},{8,0},{1,9},{9,1},{2,10},{10,2},{3,11},{11,3},{4,12},{12,4},... | collective-permute-start | bytes 589832 | tf_op jit(solution)/shard_map/ppermute | solution.py:253
  79.3 0.2 copy.8
  79.5 1.2 %collective-permute-done.3.other_ref = f32[16,8,384]{2,1,0:T(8,128)} collective-permute-done((f32[16,8,384]{2,1,0:T(8,128)}, f32[16,8,384]{2,1,0:T(8,128)}, u32[]{:S(2)}, u32[]{:S(2)}) %collective-permute-start.3) | collective-permute-done | bytes 196640 | tf_op jit(solution)/shard_map/ppermute | solution.py:253
  80.7 3.0 %shard_map.60 = (bf16[32,1536]{1,0:T(8,128)(2,1)}, f32[64,1536]{1,0:T(8,128)}, bf16[1024,1536]{1,0:T(8,128)(2,1)}) custom-call(s32[1]{0:T(128)} %bitcast.core_ref, f32[16,8,384]{2,1,0:T(8,128)} %all_to_all.29.half_ref, f32[16,8,384]{2,1,0:T(8,128)} %collective-permute-done.3.other_ref, bf16[1024,64]{1,0:T(8,128)(2,1)S(1)} %bitcast.9, ...), custom_call_target="tpu_custom_call" | custom-call | flops 201326592 | bytes 6291456 | tf_op jit(solution)/shard_map/pallas_call | solution.py:228
  (11 shorter events, 0.1 us)
Async XLA Ops:
  4.3 4.3 %collective-permute-start = (f32[16,16,128]{2,1,0:T(8,128)S(1)}, f32[16,16,128]{2,1,0:T(8,128)S(1)}, u32[]{:S(2)}, u32[]{:S(2)}) collective-permute-start(f32[16,16,128]{2,1,0:T(8,128)S(1)} %get-tuple-element.13), channel_id=1, source_target_pairs={{0,8},{8,0},{1,9},{9,1},{2,10},{10,2},{3,11},{11,3},{4,12},{12,4},... | collective-permute-start | bytes 393224 | tf_op jit(solution)/shard_map/ppermute | solution.py:253
  45.6 5.2 %collective-permute-start.1 = (f32[16,16,128]{2,1,0:T(8,128)S(1)}, f32[16,16,128]{2,1,0:T(8,128)S(1)}, u32[]{:S(2)}, u32[]{:S(2)}) collective-permute-start(f32[16,16,128]{2,1,0:T(8,128)S(1)} %all_to_all.27.half_ref), channel_id=1, source_target_pairs={{0,8},{8,0},{1,9},{9,1},{2,10},{10,2},{3,11},{11,3},{4,12},{12,4},... | collective-permute-start | bytes 393224 | tf_op jit(solution)/shard_map/ppermute | solution.py:253
  54.3 1.5 %collective-permute-start.2 = (f32[16,8,384]{2,1,0:T(8,128)S(1)}, f32[16,8,384]{2,1,0:T(8,128)S(1)}, u32[]{:S(2)}, u32[]{:S(2)}) collective-permute-start(f32[16,8,384]{2,1,0:T(8,128)S(1)} %get-tuple-element.16), channel_id=1, source_target_pairs={{0,8},{8,0},{1,9},{9,1},{2,10},{10,2},{3,11},{11,3},{4,12},{12,4},... | collective-permute-start | bytes 589832 | tf_op jit(solution)/shard_map/ppermute | solution.py:253
  76.4 4.3 %collective-permute-start.3 = (f32[16,8,384]{2,1,0:T(8,128)}, f32[16,8,384]{2,1,0:T(8,128)}, u32[]{:S(2)}, u32[]{:S(2)}) collective-permute-start(f32[16,8,384]{2,1,0:T(8,128)} %all_to_all.29.half_ref), channel_id=1, source_target_pairs={{0,8},{8,0},{1,9},{9,1},{2,10},{10,2},{3,11},{11,3},{4,12},{12,4},... | collective-permute-start | bytes 589832 | tf_op jit(solution)/shard_map/ppermute | solution.py:253

commit v7 on v6

--- a/solution.py
+++ b/solution.py
@@ -13,10 +13,6 @@
 MERGE_CHUNK = 512
 FINISH_CHUNK = 128
 GROUP = 8
-
-
-def in_vmem(value):
-    return pltpu.with_memory_space_constraint(value, pltpu.VMEM)
 
 
 def own_first(core, low, high):
@@ -150,7 +146,7 @@
         inverse_factor(gram), left, precision=lax.Precision.HIGHEST,
         preferred_element_type=jnp.float32,
     ).astype(jnp.bfloat16)
-    ortho_ref[...] = ortho
+    ortho_ref[...] = ortho.T
     wide = keep_ref.shape[2]
     count = merged_ref.shape[1] // wide
     for lane in range(count):
@@ -173,7 +169,7 @@
         ortho_kernel,
         in_specs=[SCALAR, WHOLE, WHOLE, WHOLE],
         out_specs=[WHOLE, WHOLE, WHOLE],
-        out_shape=[jax.ShapeDtypeStruct((rank, rows), jnp.bfloat16), tiles, tiles],
+        out_shape=[pltpu.VMEM((rows, rank), jnp.bfloat16), tiles, tiles],
         scratch_shapes=[pltpu.VMEM((rank, rows), jnp.float32)],
         compiler_params=pltpu.CompilerParams(vmem_limit_bytes=VMEM_LIMIT),
         cost_estimate=pl.CostEstimate(
@@ -182,11 +178,12 @@
     )(core, half, other, merged)
 
 
-def finish_kernel(core_ref, half_ref, other_ref, ortho_ref, own_ref, merged_ref,
+def finish_kernel(core_ref, slot_ref, half_ref, other_ref, ortho_ref, merged_ref,
                   update_ref, right_ref, errors_ref,
                   cast_ref, update_held, right_held, errors_held, small_sems, sems):
     core = core_ref[0]
     rank = ortho_ref.shape[1]
+    own_rows = update_held.shape[0]
     wide = half_ref.shape[2]
     count = right_ref.shape[1] // wide
     for lane in range(count):
@@ -212,8 +209,9 @@
         if i == 0:
             stores.append(pltpu.make_async_copy(right_held, right_ref, small_sems.at[0]))
             stores[-1].start()
+            own = ortho_ref[pl.ds(pl.multiple_of(slot_ref[0] * own_rows, own_rows), own_rows)]
             update_held[...] = jnp.dot(
-                own_ref[...], cast, preferred_element_type=jnp.float32
+                own, cast, preferred_element_type=jnp.float32
             ).astype(jnp.bfloat16)
             stores.append(pltpu.make_async_copy(update_held, update_ref, small_sems.at[1]))
             stores[-1].start()
@@ -221,13 +219,13 @@
         store.wait()
 
 
-def finish(core, half, other, ortho, own, merged):
+def finish(core, slot, half, other, ortho, merged, parts):
     rows, columns = merged.shape
     rank = ortho.shape[1]
-    small = (own.shape[0], columns), (rank, columns)
+    small = (rows // parts, columns), (rank, columns)
     return pl.pallas_call(
         finish_kernel,
-        in_specs=[SCALAR, WHOLE, WHOLE, WHOLE, WHOLE, WHOLE],
+        in_specs=[SCALAR, SCALAR, WHOLE, WHOLE, WHOLE, WHOLE],
         out_specs=[ANYWHERE, ANYWHERE, ANYWHERE],
         out_shape=[
             pltpu.HBM(small[0], jnp.bfloat16),
@@ -246,7 +244,7 @@
         cost_estimate=pl.CostEstimate(
             flops=2 * rows * columns * rank, bytes_accessed=4 * rows * columns, transcendentals=0
         ),
-    )(core, in_vmem(half), in_vmem(other), ortho, own, merged)
+    )(core, slot, half, other, ortho, merged)
 
 
 def swap_cores(value):
@@ -257,30 +255,37 @@
     return lax.all_to_all(value, axes, 0, 0)
 
 
+def added(parts):
+    terms = [parts[i] for i in range(parts.shape[0])]
+    while len(terms) > 1:
+        terms = [a + b for a, b in zip(terms[::2], terms[1::2], strict=True)]
+    return terms[0]
+
+
 def spread(value, copies):
     return jnp.broadcast_to(value[None], (copies,) + value.shape)
 
 
 def per_device(grads, errors, q_prev):
     core = lax.axis_index("core").astype(jnp.int32).reshape(1)
+    slot = lax.axis_index(("y", "x", "core")).astype(jnp.int32).reshape(1)
     pairs = lax.axis_size("y") * lax.axis_size("x")
     depth = lax.axis_size("z")
     replicas = 2 * pairs
 
-    merged, keep, give = merge(core, grads[0], errors[0], q_prev.T)
-    mine = jnp.sum(exchange(keep + swap_cores(give), YX), axis=0)
-    mine = jnp.sum(exchange(spread(mine, depth), "z"), axis=0) / replicas
+    core, slot, prior = lax.optimization_barrier((core, slot, q_prev.T))
+    merged, keep, give = merge(core, grads[0], errors[0], prior)
+    mine = added(exchange(keep + swap_cores(give), YX))
+    mine = added(exchange(spread(mine, depth), "z")) / replicas
     half = exchange(spread(mine, pairs), YX)
 
     ortho, keep, give = orthonormal(core, half, swap_cores(half), merged, replicas)
-    mine = jnp.sum(exchange(keep + swap_cores(give), YX), axis=0) / replicas
+    mine = added(exchange(keep + swap_cores(give), YX)) / replicas
     half = exchange(spread(mine, pairs), YX)
 
-    ortho = ortho.T
-    row_count = grads.shape[1] // replicas
-    row_start = lax.axis_index(("y", "x", "core")) * row_count
-    own = lax.dynamic_slice_in_dim(ortho, row_start, row_count, 0)
-    update, right, new_errors = finish(core, half, swap_cores(half), ortho, own, merged)
+    update, right, new_errors = finish(
+        core, slot, half, swap_cores(half), ortho, merged, replicas
+    )
     return update, right.T, new_errors[None]
 
 

time: 84 us -> 82.5 us (0.982)
  Pallas kernels: 10.1 us -> 9.25 us
    pallas_call x1, Pallas kernels: 3.05 us -> 2.16 us  [finish(): pl.pallas_call(finish_kernel, in_specs=[SCALAR, SCALAR, WHOLE, WHOLE, WHO...]
where the time goes in v7:
time: 82.5 us; the launch traced here: 82.2 us
  blocking collectives  57.1 us (69%)
  starting transfers between devices  11 us (13%)
  Pallas kernels  9.25 us (11%)
  waiting for transfers between devices  4.12 us (5%)
    all_to_all x5, blocking collectives, exchange(): return lax.all_to_all(value, axes, 0, 0)  57.1 us
    ppermute x4, starting transfers between devices, swap_cores(): return lax.ppermute(value, 'core', [(0, 1), (1, 0)])  11 us
    ppermute x4, waiting for transfers between devices, swap_cores(): return lax.ppermute(value, 'core', [(0, 1), (1, 0)])  4.12 us
    pallas_call x1, Pallas kernels, merge(): pl.pallas_call(merge_kernel, in_specs=[SCALAR, ANYWHERE, ANYWHERE, ANYWHE...  3.67 us
    pallas_call x1, Pallas kernels, orthonormal(): pl.pallas_call(ortho_kernel, in_specs=[SCALAR, WHOLE, WHOLE, WHOLE], out_...  3.42 us
    pallas_call x1, Pallas kernels, finish(): pl.pallas_call(finish_kernel, in_specs=[SCALAR, SCALAR, WHOLE, WHOLE, WHO...  2.16 us
  transfers between devices with their start and end apart: 4, of which 4 were waited for; matrix products, arithmetic and copies ran while one was open for 0% of the time, Pallas kernels for 0%

profile of v7, /device:TPU:1, one launch (start us, length us, event | category | flops | bytes accessed | tf_op | source)
XLA Modules:
  0.0 82.2 jit_solution(6528745835879206125)
XLA Ops:
  0.6 3.7 %shard_map.58 = (bf16[1024,1536]{1,0:T(8,128)(2,1)S(1)}, f32[16,16,128]{2,1,0:T(8,128)S(1)}, f32[16,16,128]{2,1,0:T(8,128)S(1)}) custom-call(s32[1]{0:T(128)} %bitcast.core_ref, bf16[1024,1536]{1,0:T(8,128)(2,1)} %bitcast.13, bf16[1024,1536]{1,0:T(8,128)(2,1)} %bitcast.14, f32[64,1536]{1,0:T(8,128)} %bitcast.15), custom_call_target="tpu_custom_call" | custom-call | flops 201326592 | bytes 9437184 | tf_op jit(solution)/shard_map/pallas_call | solution.py:68
  4.3 3.3 %collective-permute-start = (f32[16,16,128]{2,1,0:T(8,128)S(1)}, f32[16,16,128]{2,1,0:T(8,128)S(1)}, u32[]{:S(2)}, u32[]{:S(2)}) collective-permute-start(f32[16,16,128]{2,1,0:T(8,128)S(1)} %get-tuple-element.19), channel_id=1, source_target_pairs={{0,8},{8,0},{1,9},{9,1},{2,10},{10,2},{3,11},{11,3},{4,12},{12,4},... | collective-permute-start | bytes 393224 | tf_op jit(solution)/shard_map/ppermute | solution.py:251
  7.6 1.0 %collective-permute-done = f32[16,16,128]{2,1,0:T(8,128)S(1)} collective-permute-done((f32[16,16,128]{2,1,0:T(8,128)S(1)}, f32[16,16,128]{2,1,0:T(8,128)S(1)}, u32[]{:S(2)}, u32[]{:S(2)}) %collective-permute-start) | collective-permute-done | bytes 131104 | tf_op jit(solution)/shard_map/ppermute | solution.py:251
  8.6 11.7 %all_to_all.25 = f32[16,16,128]{2,1,0:T(8,128)S(1)} all-to-all(f32[16,16,128]{2,1,0:T(8,128)S(1)} %add.162), channel_id=1, replica_groups=mesh['y'=4,'x'=4,'core'=2,'z'=8] {'y','x'}, dimensions={0} | all-to-all | bytes 262144 | tf_op jit(solution)/shard_map/all_to_all | solution.py:255
  20.3 15.2 %all_to_all.26 = f32[8,16,128]{2,1,0:T(8,128)S(1)} all-to-all(f32[8,16,128]{2,1,0:T(8,128)S(1)} %broadcast_in_dim.28), channel_id=1, replica_groups=mesh['y'=4,'x'=4,'core'=2,'z'=8] {'z'}, dimensions={0} | all-to-all | bytes 131072 | tf_op jit(solution)/shard_map/all_to_all | solution.py:255
  35.6 10.0 %all_to_all.27.half_ref = f32[16,16,128]{2,1,0:T(8,128)S(1)} all-to-all(f32[16,16,128]{2,1,0:T(8,128)S(1)} %broadcast_in_dim.30), channel_id=1, replica_groups=mesh['y'=4,'x'=4,'core'=2,'z'=8] {'y','x'}, dimensions={0} | all-to-all | bytes 262144 | tf_op jit(solution)/shard_map/all_to_all | solution.py:255
  45.6 4.3 %collective-permute-start.1 = (f32[16,16,128]{2,1,0:T(8,128)S(1)}, f32[16,16,128]{2,1,0:T(8,128)S(1)}, u32[]{:S(2)}, u32[]{:S(2)}) collective-permute-start(f32[16,16,128]{2,1,0:T(8,128)S(1)} %all_to_all.27.half_ref), channel_id=1, source_target_pairs={{0,8},{8,0},{1,9},{9,1},{2,10},{10,2},{3,11},{11,3},{4,12},{12,4},... | collective-permute-start | bytes 393224 | tf_op jit(solution)/shard_map/ppermute | solution.py:251
  49.9 1.0 %collective-permute-done.1.other_ref = f32[16,16,128]{2,1,0:T(8,128)S(1)} collective-permute-done((f32[16,16,128]{2,1,0:T(8,128)S(1)}, f32[16,16,128]{2,1,0:T(8,128)S(1)}, u32[]{:S(2)}, u32[]{:S(2)}) %collective-permute-start.1) | collective-permute-done | bytes 131104 | tf_op jit(solution)/shard_map/ppermute | solution.py:251
  50.8 3.4 %shard_map.59 = (bf16[1024,64]{1,0:T(8,128)(2,1)S(1)}, f32[16,8,384]{2,1,0:T(8,128)S(1)}, f32[16,8,384]{2,1,0:T(8,128)S(1)}) custom-call(s32[1]{0:T(128)} %bitcast.core_ref, f32[16,16,128]{2,1,0:T(8,128)S(1)} %all_to_all.27.half_ref, f32[16,16,128]{2,1,0:T(8,128)S(1)} %collective-permute-done.1.other_ref, bf16[1024,1536]{1,0:T(8,128)(2,1)S(1)} %get-tuple-element.20.merged_ref), custom_call_target="tpu_custom_call" | custom-call | flops 201326592 | bytes 3145728 | tf_op jit(solution)/shard_map/pallas_call | solution.py:168
  54.3 0.4 collective-permute-start.2
  54.7 1.1 %collective-permute-done.2 = f32[16,8,384]{2,1,0:T(8,128)S(1)} collective-permute-done((f32[16,8,384]{2,1,0:T(8,128)S(1)}, f32[16,8,384]{2,1,0:T(8,128)S(1)}, u32[]{:S(2)}, u32[]{:S(2)}) %collective-permute-start.2) | collective-permute-done | bytes 196640 | tf_op jit(solution)/shard_map/ppermute | solution.py:251
  55.8 10.0 %all_to_all.28 = f32[16,8,384]{2,1,0:T(8,128)S(1)} all-to-all(f32[16,8,384]{2,1,0:T(8,128)S(1)} %add.185), channel_id=1, replica_groups=mesh['y'=4,'x'=4,'core'=2,'z'=8] {'y','x'}, dimensions={0} | all-to-all | bytes 393216 | tf_op jit(solution)/shard_map/all_to_all | solution.py:255
  65.9 10.2 %all_to_all.29.half_ref = f32[16,8,384]{2,1,0:T(8,128)S(1)} all-to-all(f32[16,8,384]{2,1,0:T(8,128)S(1)} %broadcast_in_dim.32), channel_id=1, replica_groups=mesh['y'=4,'x'=4,'core'=2,'z'=8] {'y','x'}, dimensions={0} | all-to-all | bytes 393216 | tf_op jit(solution)/shard_map/all_to_all | solution.py:255
  76.0 2.9 %collective-permute-start.3 = (f32[16,8,384]{2,1,0:T(8,128)S(1)}, f32[16,8,384]{2,1,0:T(8,128)S(1)}, u32[]{:S(2)}, u32[]{:S(2)}) collective-permute-start(f32[16,8,384]{2,1,0:T(8,128)S(1)} %all_to_all.29.half_ref), channel_id=1, source_target_pairs={{0,8},{8,0},{1,9},{9,1},{2,10},{10,2},{3,11},{11,3},{4,12},{12,4},... | collective-permute-start | bytes 589832 | tf_op jit(solution)/shard_map/ppermute | solution.py:251
  79.0 1.1 %collective-permute-done.3.other_ref = f32[16,8,384]{2,1,0:T(8,128)S(1)} collective-permute-done((f32[16,8,384]{2,1,0:T(8,128)S(1)}, f32[16,8,384]{2,1,0:T(8,128)S(1)}, u32[]{:S(2)}, u32[]{:S(2)}) %collective-permute-start.3) | collective-permute-done | bytes 196640 | tf_op jit(solution)/shard_map/ppermute | solution.py:251
  80.0 2.2 %shard_map.60 = (bf16[32,1536]{1,0:T(8,128)(2,1)}, f32[64,1536]{1,0:T(8,128)}, bf16[1024,1536]{1,0:T(8,128)(2,1)}) custom-call(s32[1]{0:T(128)} %bitcast.core_ref, s32[1]{0:T(128)} %bitcast.1.slot_ref, f32[16,8,384]{2,1,0:T(8,128)S(1)} %all_to_all.29.half_ref, f32[16,8,384]{2,1,0:T(8,128)S(1)} %collective-permute-done.3.other_ref, ...), custom_call_target="tpu_custom_call" | custom-call | flops 201326592 | bytes 6291456 | tf_op jit(solution)/shard_map/pallas_call | solution.py:226
  (8 shorter events, 0.1 us)
Async XLA Ops:
  4.3 4.3 %collective-permute-start = (f32[16,16,128]{2,1,0:T(8,128)S(1)}, f32[16,16,128]{2,1,0:T(8,128)S(1)}, u32[]{:S(2)}, u32[]{:S(2)}) collective-permute-start(f32[16,16,128]{2,1,0:T(8,128)S(1)} %get-tuple-element.19), channel_id=1, source_target_pairs={{0,8},{8,0},{1,9},{9,1},{2,10},{10,2},{3,11},{11,3},{4,12},{12,4},... | collective-permute-start | bytes 393224 | tf_op jit(solution)/shard_map/ppermute | solution.py:251
  45.6 5.2 %collective-permute-start.1 = (f32[16,16,128]{2,1,0:T(8,128)S(1)}, f32[16,16,128]{2,1,0:T(8,128)S(1)}, u32[]{:S(2)}, u32[]{:S(2)}) collective-permute-start(f32[16,16,128]{2,1,0:T(8,128)S(1)} %all_to_all.27.half_ref), channel_id=1, source_target_pairs={{0,8},{8,0},{1,9},{9,1},{2,10},{10,2},{3,11},{11,3},{4,12},{12,4},... | collective-permute-start | bytes 393224 | tf_op jit(solution)/shard_map/ppermute | solution.py:251
  54.3 1.5 %collective-permute-start.2 = (f32[16,8,384]{2,1,0:T(8,128)S(1)}, f32[16,8,384]{2,1,0:T(8,128)S(1)}, u32[]{:S(2)}, u32[]{:S(2)}) collective-permute-start(f32[16,8,384]{2,1,0:T(8,128)S(1)} %get-tuple-element.22), channel_id=1, source_target_pairs={{0,8},{8,0},{1,9},{9,1},{2,10},{10,2},{3,11},{11,3},{4,12},{12,4},... | collective-permute-start | bytes 589832 | tf_op jit(solution)/shard_map/ppermute | solution.py:251
  76.0 4.0 %collective-permute-start.3 = (f32[16,8,384]{2,1,0:T(8,128)S(1)}, f32[16,8,384]{2,1,0:T(8,128)S(1)}, u32[]{:S(2)}, u32[]{:S(2)}) collective-permute-start(f32[16,8,384]{2,1,0:T(8,128)S(1)} %all_to_all.29.half_ref), channel_id=1, source_target_pairs={{0,8},{8,0},{1,9},{9,1},{2,10},{10,2},{3,11},{11,3},{4,12},{12,4},... | collective-permute-start | bytes 589832 | tf_op jit(solution)/shard_map/ppermute | solution.py:251

commit v8 on v7

--- a/solution.py
+++ b/solution.py
@@ -1,3 +1,5 @@
+import functools
+
 import jax
 import jax.numpy as jnp
 from jax import lax
@@ -7,6 +9,7 @@
 
 YX = ("y", "x")
 VMEM_LIMIT = 32 * 1024 * 1024
+SMALL_LIMIT = 16 * 1024 * 1024
 WHOLE = pl.BlockSpec(memory_space=pltpu.VMEM)
 SCALAR = pl.BlockSpec(memory_space=pltpu.SMEM)
 ANYWHERE = pl.BlockSpec(memory_space=pl.ANY)
@@ -126,8 +129,19 @@
     return jnp.concatenate(groups)[:, rank:]
 
 
-def ortho_kernel(core_ref, half_ref, other_ref, merged_ref, ortho_ref, keep_ref, give_ref,
-                 left_ref):
+def right_tiles(ortho, merged_ref, half, tiles_ref):
+    wide = tiles_ref.shape[2]
+    count = merged_ref.shape[1] // (2 * wide)
+    for lane in range(count):
+        start = pl.multiple_of(half * (count * wide), 128) + lane * wide
+        right = jnp.dot(
+            ortho, merged_ref[:, pl.ds(start, wide)], preferred_element_type=jnp.float32
+        )
+        for down in range(ortho.shape[0] // 8):
+            tiles_ref[down * count + lane] = right[8 * down : 8 * down + 8]
+
+
+def ortho_kernel(core_ref, half_ref, other_ref, merged_ref, ortho_ref, give_ref, left_ref):
     core = core_ref[0]
     rank, rows = left_ref.shape
     across = rows // 128
@@ -146,18 +160,14 @@
         inverse_factor(gram), left, precision=lax.Precision.HIGHEST,
         preferred_element_type=jnp.float32,
     ).astype(jnp.bfloat16)
-    ortho_ref[...] = ortho.T
-    wide = keep_ref.shape[2]
-    count = merged_ref.shape[1] // wide
-    for lane in range(count):
-        right = jnp.dot(
-            ortho, merged_ref[:, wide * lane : wide * lane + wide],
-            preferred_element_type=jnp.float32,
-        )
-        keep, give = own_first(core, right[: rank // 2], right[rank // 2 :])
-        for down in range(rank // 16):
-            keep_ref[down * count + lane] = keep[8 * down : 8 * down + 8]
-            give_ref[down * count + lane] = give[8 * down : 8 * down + 8]
+    ortho_ref[...] = ortho
+    right_tiles(ortho, merged_ref, 1 - core, give_ref)
+
+
+def keep_kernel(core_ref, ortho_ref, merged_ref, keep_ref, turned_ref):
+    ortho = ortho_ref[...]
+    right_tiles(ortho, merged_ref, core_ref[0], keep_ref)
+    turned_ref[...] = ortho.T
 
 
 def orthonormal(core, half, other, merged, parts):
@@ -168,8 +178,8 @@
     return pl.pallas_call(
         ortho_kernel,
         in_specs=[SCALAR, WHOLE, WHOLE, WHOLE],
-        out_specs=[WHOLE, WHOLE, WHOLE],
-        out_shape=[pltpu.VMEM((rows, rank), jnp.bfloat16), tiles, tiles],
+        out_specs=[WHOLE, WHOLE],
+        out_shape=[pltpu.VMEM((rank, rows), jnp.bfloat16), tiles],
         scratch_shapes=[pltpu.VMEM((rank, rows), jnp.float32)],
         compiler_params=pltpu.CompilerParams(vmem_limit_bytes=VMEM_LIMIT),
         cost_estimate=pl.CostEstimate(
@@ -178,20 +188,33 @@
     )(core, half, other, merged)
 
 
-def finish_kernel(core_ref, slot_ref, half_ref, other_ref, ortho_ref, merged_ref,
-                  update_ref, right_ref, errors_ref,
-                  cast_ref, update_held, right_held, errors_held, small_sems, sems):
-    core = core_ref[0]
-    rank = ortho_ref.shape[1]
+def kept_right(core, ortho, merged, parts):
+    rank, rows = ortho.shape
+    columns = merged.shape[1]
+    tiles = jax.ShapeDtypeStruct((parts // 2, 8, rank * columns // (8 * parts)), jnp.float32)
+    return pl.pallas_call(
+        keep_kernel,
+        in_specs=[SCALAR, WHOLE, WHOLE],
+        out_specs=[WHOLE, WHOLE],
+        out_shape=[tiles, pltpu.VMEM((rows, rank), jnp.bfloat16)],
+        compiler_params=pltpu.CompilerParams(vmem_limit_bytes=SMALL_LIMIT),
+        cost_estimate=pl.CostEstimate(
+            flops=rows * columns * rank, bytes_accessed=rows * columns, transcendentals=0
+        ),
+    )(core, ortho, merged)
+
+
+def finish_kernel(flip, core_ref, slot_ref, tiles_ref, ortho_ref, merged_ref, *refs):
+    update_ref, right_ref, errors_ref = refs[-9:-6]
+    cast_ref, update_held, right_held, errors_held, small_sems, sems = refs[-6:]
+    half = 1 - core_ref[0] if flip else core_ref[0]
     own_rows = update_held.shape[0]
-    wide = half_ref.shape[2]
-    count = right_ref.shape[1] // wide
+    rank, columns = right_held.shape
+    wide = tiles_ref.shape[2]
+    count = columns // wide
+    lanes = pl.ds(pl.multiple_of(half * columns, 128), columns)
     for lane in range(count):
-        pairs = [
-            own_first(core, half_ref[down * count + lane], other_ref[down * count + lane])
-            for down in range(rank // 16)
-        ]
-        right = jnp.concatenate([low for low, _ in pairs] + [high for _, high in pairs])
+        right = jnp.concatenate([tiles_ref[down * count + lane] for down in range(rank // 8)])
         cast_ref[:, wide * lane : wide * lane + wide] = right.astype(jnp.bfloat16)
         right_held[:, wide * lane : wide * lane + wide] = right
     cast = cast_ref[...]
@@ -200,51 +223,56 @@
         block = pl.ds(FINISH_CHUNK * i, FINISH_CHUNK)
         full_update = jnp.dot(ortho_ref[block], cast, preferred_element_type=jnp.float32)
         errors_held[block] = (
-            merged_ref[block].astype(jnp.float32) - full_update
+            merged_ref[block, lanes].astype(jnp.float32) - full_update
         ).astype(jnp.bfloat16)
         stores.append(
-            pltpu.make_async_copy(errors_held.at[block], errors_ref.at[block], sems.at[i])
+            pltpu.make_async_copy(errors_held.at[block], errors_ref.at[block, lanes], sems.at[i])
         )
         stores[-1].start()
         if i == 0:
-            stores.append(pltpu.make_async_copy(right_held, right_ref, small_sems.at[0]))
+            stores.append(
+                pltpu.make_async_copy(right_held, right_ref.at[:, lanes], small_sems.at[0])
+            )
             stores[-1].start()
             own = ortho_ref[pl.ds(pl.multiple_of(slot_ref[0] * own_rows, own_rows), own_rows)]
             update_held[...] = jnp.dot(
                 own, cast, preferred_element_type=jnp.float32
             ).astype(jnp.bfloat16)
-            stores.append(pltpu.make_async_copy(update_held, update_ref, small_sems.at[1]))
+            stores.append(
+                pltpu.make_async_copy(update_held, update_ref.at[:, lanes], small_sems.at[1])
+            )
             stores[-1].start()
     for store in stores:
         store.wait()
 
 
-def finish(core, slot, half, other, ortho, merged, parts):
+def finish(core, slot, tiles, ortho, merged, parts, begun=()):
     rows, columns = merged.shape
     rank = ortho.shape[1]
-    small = (rows // parts, columns), (rank, columns)
+    half = columns // 2
     return pl.pallas_call(
-        finish_kernel,
-        in_specs=[SCALAR, SCALAR, WHOLE, WHOLE, WHOLE, WHOLE],
+        functools.partial(finish_kernel, bool(begun)),
+        in_specs=[SCALAR, SCALAR, WHOLE, WHOLE, WHOLE] + [ANYWHERE] * len(begun),
         out_specs=[ANYWHERE, ANYWHERE, ANYWHERE],
         out_shape=[
-            pltpu.HBM(small[0], jnp.bfloat16),
-            pltpu.HBM(small[1], jnp.float32),
+            pltpu.HBM((rows // parts, columns), jnp.bfloat16),
+            pltpu.HBM((rank, columns), jnp.float32),
             pltpu.HBM(merged.shape, jnp.bfloat16),
         ],
+        input_output_aliases={5 + i: i for i in range(len(begun))},
         scratch_shapes=[
-            pltpu.VMEM(small[1], jnp.bfloat16),
-            pltpu.VMEM(small[0], jnp.bfloat16),
-            pltpu.VMEM(small[1], jnp.float32),
-            pltpu.VMEM(merged.shape, jnp.bfloat16),
+            pltpu.VMEM((rank, half), jnp.bfloat16),
+            pltpu.VMEM((rows // parts, half), jnp.bfloat16),
+            pltpu.VMEM((rank, half), jnp.float32),
+            pltpu.VMEM((rows, half), jnp.bfloat16),
             pltpu.SemaphoreType.DMA((2,)),
             pltpu.SemaphoreType.DMA((rows // FINISH_CHUNK,)),
         ],
-        compiler_params=pltpu.CompilerParams(vmem_limit_bytes=VMEM_LIMIT),
+        compiler_params=pltpu.CompilerParams(vmem_limit_bytes=SMALL_LIMIT),
         cost_estimate=pl.CostEstimate(
-            flops=2 * rows * columns * rank, bytes_accessed=4 * rows * columns, transcendentals=0
+            flops=rows * columns * rank, bytes_accessed=2 * rows * columns, transcendentals=0
         ),
-    )(core, slot, half, other, ortho, merged)
+    )(core, slot, tiles, ortho, merged, *begun)
 
 
 def swap_cores(value):
@@ -279,13 +307,15 @@
     mine = added(exchange(spread(mine, depth), "z")) / replicas
     half = exchange(spread(mine, pairs), YX)
 
-    ortho, keep, give = orthonormal(core, half, swap_cores(half), merged, replicas)
-    mine = added(exchange(keep + swap_cores(give), YX)) / replicas
+    ortho, give = orthonormal(core, half, swap_cores(half), merged, replicas)
+    given = swap_cores(give)
+    keep, ortho = kept_right(core, ortho, merged, replicas)
+    mine = added(exchange(keep + given, YX)) / replicas
     half = exchange(spread(mine, pairs), YX)
 
-    update, right, new_errors = finish(
-        core, slot, half, swap_cores(half), ortho, merged, replicas
-    )
+    other = swap_cores(half)
+    begun = finish(core, slot, half, ortho, merged, replicas)
+    update, right, new_errors = finish(core, slot, other, ortho, merged, replicas, begun)
     return update, right.T, new_errors[None]
 
 

time: 82.5 us -> 82.1 us (level)
  waiting for transfers between devices: 4.12 us -> 2.67 us
  Pallas kernels: 9.25 us -> 10.3 us
    ppermute x4, waiting for transfers between devices: 4.12 us -> 2.67 us  [swap_cores(): return lax.ppermute(value, 'core', [(0, 1), (1, 0)])]
    pallas_call x1 -> x3, Pallas kernels: 2.16 us -> 3.43 us  [the longest x2 3.06 us: finish(): pl.pallas_call(functools.partial(finish_kernel, bool(begun)), in_specs=[S...]
  transfers between devices with their start and end apart: 4 -> 4, of which waited for: 4 -> 3; matrix products, arithmetic and copies ran while one was open for 0% -> 0% of each run, Pallas kernels for 0% -> 2%
where the time goes in v8:
time: 82.1 us; the launch traced here: 81.8 us
  blocking collectives  57.1 us (70%)
  starting transfers between devices  11 us (13%)
  Pallas kernels  10.3 us (13%)
  waiting for transfers between devices  2.67 us (3%)
    all_to_all x5, blocking collectives, exchange(): return lax.all_to_all(value, axes, 0, 0)  57.1 us
    ppermute x4, starting transfers between devices, swap_cores(): return lax.ppermute(value, 'core', [(0, 1), (1, 0)])  11 us
    pallas_call x1, Pallas kernels, merge(): pl.pallas_call(merge_kernel, in_specs=[SCALAR, ANYWHERE, ANYWHERE, ANYWHE...  3.67 us
    pallas_call x1, Pallas kernels, orthonormal(): pl.pallas_call(ortho_kernel, in_specs=[SCALAR, WHOLE, WHOLE, WHOLE], out_...  3.19 us
    pallas_call x2, Pallas kernels, finish(): pl.pallas_call(functools.partial(finish_kernel, bool(begun)), in_specs=[S...  3.06 us
    ppermute x4, waiting for transfers between devices, swap_cores(): return lax.ppermute(value, 'core', [(0, 1), (1, 0)])  2.67 us
  transfers between devices with their start and end apart: 4, of which 3 were waited for; matrix products, arithmetic and copies ran while one was open for 0% of the time, Pallas kernels for 2%

profile of v8, /device:TPU:1, one launch (start us, length us, event | category | flops | bytes accessed | tf_op | source)
XLA Modules:
  0.0 81.8 jit_solution(7561537409569633391)
XLA Ops:
  0.6 3.7 %shard_map.58 = (bf16[1024,1536]{1,0:T(8,128)(2,1)S(1)}, f32[16,16,128]{2,1,0:T(8,128)S(1)}, f32[16,16,128]{2,1,0:T(8,128)S(1)}) custom-call(s32[1]{0:T(128)} %bitcast.core_ref, bf16[1024,1536]{1,0:T(8,128)(2,1)} %bitcast.13, bf16[1024,1536]{1,0:T(8,128)(2,1)} %bitcast.14, f32[64,1536]{1,0:T(8,128)} %bitcast.16), custom_call_target="tpu_custom_call" | custom-call | flops 201326592 | bytes 9437184 | tf_op jit(solution)/shard_map/pallas_call | solution.py:71
  4.3 3.3 %collective-permute-start = (f32[16,16,128]{2,1,0:T(8,128)S(1)}, f32[16,16,128]{2,1,0:T(8,128)S(1)}, u32[]{:S(2)}, u32[]{:S(2)}) collective-permute-start(f32[16,16,128]{2,1,0:T(8,128)S(1)} %get-tuple-element.23), channel_id=1, source_target_pairs={{0,8},{8,0},{1,9},{9,1},{2,10},{10,2},{3,11},{11,3},{4,12},{12,4},... | collective-permute-start | bytes 393224 | tf_op jit(solution)/shard_map/ppermute | solution.py:279
  7.6 1.0 %collective-permute-done = f32[16,16,128]{2,1,0:T(8,128)S(1)} collective-permute-done((f32[16,16,128]{2,1,0:T(8,128)S(1)}, f32[16,16,128]{2,1,0:T(8,128)S(1)}, u32[]{:S(2)}, u32[]{:S(2)}) %collective-permute-start) | collective-permute-done | bytes 131104 | tf_op jit(solution)/shard_map/ppermute | solution.py:279
  8.6 11.7 %all_to_all.25 = f32[16,16,128]{2,1,0:T(8,128)S(1)} all-to-all(f32[16,16,128]{2,1,0:T(8,128)S(1)} %add.162), channel_id=1, replica_groups=mesh['y'=4,'x'=4,'core'=2,'z'=8] {'y','x'}, dimensions={0} | all-to-all | bytes 262144 | tf_op jit(solution)/shard_map/all_to_all | solution.py:283
  20.3 15.2 %all_to_all.26 = f32[8,16,128]{2,1,0:T(8,128)S(1)} all-to-all(f32[8,16,128]{2,1,0:T(8,128)S(1)} %broadcast_in_dim.28), channel_id=1, replica_groups=mesh['y'=4,'x'=4,'core'=2,'z'=8] {'z'}, dimensions={0} | all-to-all | bytes 131072 | tf_op jit(solution)/shard_map/all_to_all | solution.py:283
  35.6 10.0 %all_to_all.27.half_ref = f32[16,16,128]{2,1,0:T(8,128)S(1)} all-to-all(f32[16,16,128]{2,1,0:T(8,128)S(1)} %broadcast_in_dim.30), channel_id=1, replica_groups=mesh['y'=4,'x'=4,'core'=2,'z'=8] {'y','x'}, dimensions={0} | all-to-all | bytes 262144 | tf_op jit(solution)/shard_map/all_to_all | solution.py:283
  45.6 4.3 %collective-permute-start.1 = (f32[16,16,128]{2,1,0:T(8,128)S(1)}, f32[16,16,128]{2,1,0:T(8,128)S(1)}, u32[]{:S(2)}, u32[]{:S(2)}) collective-permute-start(f32[16,16,128]{2,1,0:T(8,128)S(1)} %all_to_all.27.half_ref), channel_id=1, source_target_pairs={{0,8},{8,0},{1,9},{9,1},{2,10},{10,2},{3,11},{11,3},{4,12},{12,4},... | collective-permute-start | bytes 393224 | tf_op jit(solution)/shard_map/ppermute | solution.py:279
  49.9 1.0 %collective-permute-done.1.other_ref = f32[16,16,128]{2,1,0:T(8,128)S(1)} collective-permute-done((f32[16,16,128]{2,1,0:T(8,128)S(1)}, f32[16,16,128]{2,1,0:T(8,128)S(1)}, u32[]{:S(2)}, u32[]{:S(2)}) %collective-permute-start.1) | collective-permute-done | bytes 131104 | tf_op jit(solution)/shard_map/ppermute | solution.py:279
  50.8 3.2 %shard_map.59 = (bf16[64,1024]{1,0:T(8,128)(2,1)S(1)}, f32[16,8,384]{2,1,0:T(8,128)S(1)}) custom-call(s32[1]{0:T(128)} %bitcast.core_ref, f32[16,16,128]{2,1,0:T(8,128)S(1)} %all_to_all.27.half_ref, f32[16,16,128]{2,1,0:T(8,128)S(1)} %collective-permute-done.1.other_ref, bf16[1024,1536]{1,0:T(8,128)(2,1)S(1)} %get-tuple-element.24.merged_ref), custom_call_target="tpu_custom_call" | custom-call | flops 201326592 | bytes 3145728 | tf_op jit(solution)/shard_map/pallas_call | solution.py:178
  54.0 0.4 collective-permute-start.2
  54.5 0.4 shard_map.60
  54.9 0.7 collective-permute-done.2
  55.6 10.0 %all_to_all.28 = f32[16,8,384]{2,1,0:T(8,128)S(1)} all-to-all(f32[16,8,384]{2,1,0:T(8,128)S(1)} %add.185), channel_id=1, replica_groups=mesh['y'=4,'x'=4,'core'=2,'z'=8] {'y','x'}, dimensions={0} | all-to-all | bytes 393216 | tf_op jit(solution)/shard_map/all_to_all | solution.py:283
  65.6 10.2 %all_to_all.29.tiles_ref = f32[16,8,384]{2,1,0:T(8,128)S(1)} all-to-all(f32[16,8,384]{2,1,0:T(8,128)S(1)} %broadcast_in_dim.32), channel_id=1, replica_groups=mesh['y'=4,'x'=4,'core'=2,'z'=8] {'y','x'}, dimensions={0} | all-to-all | bytes 393216 | tf_op jit(solution)/shard_map/all_to_all | solution.py:283
  75.8 2.9 %collective-permute-start.3 = (f32[16,8,384]{2,1,0:T(8,128)S(1)}, f32[16,8,384]{2,1,0:T(8,128)S(1)}, u32[]{:S(2)}, u32[]{:S(2)}) collective-permute-start(f32[16,8,384]{2,1,0:T(8,128)S(1)} %all_to_all.29.tiles_ref), channel_id=1, source_target_pairs={{0,8},{8,0},{1,9},{9,1},{2,10},{10,2},{3,11},{11,3},{4,12},{12,4},... | collective-permute-start | bytes 589832 | tf_op jit(solution)/shard_map/ppermute | solution.py:279
  78.7 1.5 %shard_map.61 = (bf16[32,1536]{1,0:T(8,128)(2,1)}, f32[64,1536]{1,0:T(8,128)}, bf16[1024,1536]{1,0:T(8,128)(2,1)}) custom-call(s32[1]{0:T(128)} %bitcast.core_ref, s32[1]{0:T(128)} %bitcast.1.slot_ref, f32[16,8,384]{2,1,0:T(8,128)S(1)} %all_to_all.29.tiles_ref, bf16[1024,64]{1,0:T(8,128)(2,1)S(1)} %get-tuple-element.28.ortho_ref, ...), custom_call_target="tpu_custom_call" | custom-call | flops 100663296 | bytes 3145728 | tf_op jit(solution)/shard_map/pallas_call | solution.py:253
  80.3 0.0 collective-permute-done.3.tiles_ref
  80.3 1.5 %shard_map.62 = (bf16[32,1536]{1,0:T(8,128)(2,1)}, f32[64,1536]{1,0:T(8,128)}, bf16[1024,1536]{1,0:T(8,128)(2,1)}) custom-call(s32[1]{0:T(128)} %bitcast.core_ref, s32[1]{0:T(128)} %bitcast.1.slot_ref, f32[16,8,384]{2,1,0:T(8,128)S(1)} %collective-permute-done.3.tiles_ref, ...), custom_call_target="tpu_custom_call", output_to_operand_aliasing={{0}: (5, {}), {1}: (6, {}), {2}: (7, {})} | custom-call | flops 100663296 | bytes 3145728 | tf_op jit(solution)/shard_map/pallas_call | solution.py:253
  (8 shorter events, 0.1 us)
Async XLA Ops:
  4.3 4.3 %collective-permute-start = (f32[16,16,128]{2,1,0:T(8,128)S(1)}, f32[16,16,128]{2,1,0:T(8,128)S(1)}, u32[]{:S(2)}, u32[]{:S(2)}) collective-permute-start(f32[16,16,128]{2,1,0:T(8,128)S(1)} %get-tuple-element.23), channel_id=1, source_target_pairs={{0,8},{8,0},{1,9},{9,1},{2,10},{10,2},{3,11},{11,3},{4,12},{12,4},... | collective-permute-start | bytes 393224 | tf_op jit(solution)/shard_map/ppermute | solution.py:279
  45.6 5.2 %collective-permute-start.1 = (f32[16,16,128]{2,1,0:T(8,128)S(1)}, f32[16,16,128]{2,1,0:T(8,128)S(1)}, u32[]{:S(2)}, u32[]{:S(2)}) collective-permute-start(f32[16,16,128]{2,1,0:T(8,128)S(1)} %all_to_all.27.half_ref), channel_id=1, source_target_pairs={{0,8},{8,0},{1,9},{9,1},{2,10},{10,2},{3,11},{11,3},{4,12},{12,4},... | collective-permute-start | bytes 393224 | tf_op jit(solution)/shard_map/ppermute | solution.py:279
  54.0 1.5 %collective-permute-start.2 = (f32[16,8,384]{2,1,0:T(8,128)S(1)}, f32[16,8,384]{2,1,0:T(8,128)S(1)}, u32[]{:S(2)}, u32[]{:S(2)}) collective-permute-start(f32[16,8,384]{2,1,0:T(8,128)S(1)} %get-tuple-element.27), channel_id=1, source_target_pairs={{0,8},{8,0},{1,9},{9,1},{2,10},{10,2},{3,11},{11,3},{4,12},{12,4},... | collective-permute-start | bytes 589832 | tf_op jit(solution)/shard_map/ppermute | solution.py:279
  75.8 4.5 %collective-permute-start.3 = (f32[16,8,384]{2,1,0:T(8,128)S(1)}, f32[16,8,384]{2,1,0:T(8,128)S(1)}, u32[]{:S(2)}, u32[]{:S(2)}) collective-permute-start(f32[16,8,384]{2,1,0:T(8,128)S(1)} %all_to_all.29.tiles_ref), channel_id=1, source_target_pairs={{0,8},{8,0},{1,9},{9,1},{2,10},{10,2},{3,11},{11,3},{4,12},{12,4},... | collective-permute-start | bytes 589832 | tf_op jit(solution)/shard_map/ppermute | solution.py:279

commit v9 on v8

--- a/solution.py
+++ b/solution.py
@@ -8,6 +8,7 @@
 from jax.sharding import Mesh, PartitionSpec as P
 
 YX = ("y", "x")
+DP = ("y", "x", "core")
 VMEM_LIMIT = 32 * 1024 * 1024
 SMALL_LIMIT = 16 * 1024 * 1024
 WHOLE = pl.BlockSpec(memory_space=pltpu.VMEM)
@@ -18,13 +19,8 @@
 GROUP = 8
 
 
-def own_first(core, low, high):
-    return jnp.where(core == 0, low, high), jnp.where(core == 0, high, low)
-
-
-def merge_kernel(core_ref, grads_ref, errors_ref, prior_ref, merged_ref, keep_ref, give_ref,
+def merge_kernel(grads_ref, errors_ref, prior_ref, merged_ref, left_ref,
                  grads_held, errors_held, prior_held, sems, prior_sem):
-    core = core_ref[0]
     rank = prior_ref.shape[0]
     rows = merged_ref.shape[0]
     chunks = rows // MERGE_CHUNK
@@ -54,25 +50,23 @@
         left = lax.dot_general(
             prior, merged, (((1,), (1,)), ((), ())), preferred_element_type=jnp.float32
         )
-        keep, give = own_first(core, left[: rank // 2], left[rank // 2 :])
         lanes = MERGE_CHUNK // 128
-        for down in range(rank // 32):
+        for down in range(rank // 16):
             for lane in range(lanes):
-                place = down * (rows // 128) + i * lanes + lane
-                tile = (slice(16 * down, 16 * down + 16), slice(128 * lane, 128 * lane + 128))
-                keep_ref[place] = keep[tile]
-                give_ref[place] = give[tile]
-
-
-def merge(core, grads, errors, prior):
+                left_ref[down * (rows // 128) + i * lanes + lane] = (
+                    left[16 * down : 16 * down + 16, 128 * lane : 128 * lane + 128]
+                )
+
+
+def merge(grads, errors, prior):
     rows, columns = grads.shape
     rank = prior.shape[0]
-    tiles = jax.ShapeDtypeStruct((rows // 128 * (rank // 32), 16, 128), jnp.float32)
+    tiles = jax.ShapeDtypeStruct((rows // 128 * (rank // 16), 16, 128), jnp.float32)
     return pl.pallas_call(
         merge_kernel,
-        in_specs=[SCALAR, ANYWHERE, ANYWHERE, ANYWHERE],
-        out_specs=[WHOLE, WHOLE, WHOLE],
-        out_shape=[pltpu.VMEM(grads.shape, jnp.bfloat16), tiles, tiles],
+        in_specs=[ANYWHERE, ANYWHERE, ANYWHERE],
+        out_specs=[WHOLE, WHOLE],
+        out_shape=[pltpu.VMEM(grads.shape, jnp.bfloat16), tiles],
         scratch_shapes=[
             pltpu.VMEM(grads.shape, jnp.bfloat16),
             pltpu.VMEM(grads.shape, jnp.bfloat16),
@@ -84,7 +78,7 @@
         cost_estimate=pl.CostEstimate(
             flops=2 * rows * columns * rank, bytes_accessed=6 * rows * columns, transcendentals=0
         ),
-    )(core, *[pltpu.with_memory_space_constraint(x, pltpu.HBM) for x in (grads, errors, prior)])
+    )(*[pltpu.with_memory_space_constraint(x, pltpu.HBM) for x in (grads, errors, prior)])
 
 
 def inverse_factor(gram):
@@ -141,16 +135,13 @@
             tiles_ref[down * count + lane] = right[8 * down : 8 * down + 8]
 
 
-def ortho_kernel(core_ref, half_ref, other_ref, merged_ref, ortho_ref, give_ref, left_ref):
+def ortho_kernel(core_ref, tiles_ref, merged_ref, ortho_ref, give_ref, left_ref):
     core = core_ref[0]
     rank, rows = left_ref.shape
     across = rows // 128
-    for place in range(half_ref.shape[0]):
-        low, high = own_first(core, half_ref[place], other_ref[place])
-        down = 16 * (place // across)
-        lane = pl.ds(128 * (place % across), 128)
-        left_ref[pl.ds(down, 16), lane] = low
-        left_ref[pl.ds(rank // 2 + down, 16), lane] = high
+    for place in range(tiles_ref.shape[0]):
+        down, lane = divmod(place, across)
+        left_ref[16 * down : 16 * down + 16, 128 * lane : 128 * lane + 128] = tiles_ref[place]
     left = left_ref[...]
     gram = lax.dot_general(
         left, left, (((1,), (1,)), ((), ())), precision=lax.Precision.HIGHEST,
@@ -170,14 +161,14 @@
     turned_ref[...] = ortho.T
 
 
-def orthonormal(core, half, other, merged, parts):
+def orthonormal(core, left, merged, parts):
     rows, columns = merged.shape
-    rank = half.size * 2 // rows
+    rank = left.size // rows
     wide = rank * columns // (8 * parts)
     tiles = jax.ShapeDtypeStruct((parts // 2, 8, wide), jnp.float32)
     return pl.pallas_call(
         ortho_kernel,
-        in_specs=[SCALAR, WHOLE, WHOLE, WHOLE],
+        in_specs=[SCALAR, WHOLE, WHOLE],
         out_specs=[WHOLE, WHOLE],
         out_shape=[pltpu.VMEM((rank, rows), jnp.bfloat16), tiles],
         scratch_shapes=[pltpu.VMEM((rank, rows), jnp.float32)],
@@ -185,7 +176,7 @@
         cost_estimate=pl.CostEstimate(
             flops=2 * rows * columns * rank, bytes_accessed=2 * rows * columns, transcendentals=0
         ),
-    )(core, half, other, merged)
+    )(core, left, merged)
 
 
 def kept_right(core, ortho, merged, parts):
@@ -204,75 +195,69 @@
     )(core, ortho, merged)
 
 
-def finish_kernel(flip, core_ref, slot_ref, tiles_ref, ortho_ref, merged_ref, *refs):
-    update_ref, right_ref, errors_ref = refs[-9:-6]
-    cast_ref, update_held, right_held, errors_held, small_sems, sems = refs[-6:]
-    half = 1 - core_ref[0] if flip else core_ref[0]
+def finish_kernel(slot_ref, tiles_ref, ortho_ref, merged_ref, update_ref, right_ref, errors_ref,
+                  cast_ref, update_held, right_held, errors_held, small_sems, sems):
     own_rows = update_held.shape[0]
     rank, columns = right_held.shape
     wide = tiles_ref.shape[2]
-    count = columns // wide
-    lanes = pl.ds(pl.multiple_of(half * columns, 128), columns)
-    for lane in range(count):
-        right = jnp.concatenate([tiles_ref[down * count + lane] for down in range(rank // 8)])
-        cast_ref[:, wide * lane : wide * lane + wide] = right.astype(jnp.bfloat16)
-        right_held[:, wide * lane : wide * lane + wide] = right
+    count = columns // (2 * wide)
+    for place in range(tiles_ref.shape[0]):
+        spot, half = divmod(place, 2)
+        down, lane = spot // count, half * count + spot % count
+        right_held[8 * down : 8 * down + 8, wide * lane : wide * lane + wide] = (
+            tiles_ref[place].astype(jnp.float32)
+        )
+    cast_ref[...] = right_held[...].astype(jnp.bfloat16)
     cast = cast_ref[...]
     stores = []
     for i in range(merged_ref.shape[0] // FINISH_CHUNK):
         block = pl.ds(FINISH_CHUNK * i, FINISH_CHUNK)
         full_update = jnp.dot(ortho_ref[block], cast, preferred_element_type=jnp.float32)
         errors_held[block] = (
-            merged_ref[block, lanes].astype(jnp.float32) - full_update
+            merged_ref[block].astype(jnp.float32) - full_update
         ).astype(jnp.bfloat16)
         stores.append(
-            pltpu.make_async_copy(errors_held.at[block], errors_ref.at[block, lanes], sems.at[i])
+            pltpu.make_async_copy(errors_held.at[block], errors_ref.at[block], sems.at[i])
         )
         stores[-1].start()
         if i == 0:
-            stores.append(
-                pltpu.make_async_copy(right_held, right_ref.at[:, lanes], small_sems.at[0])
-            )
+            stores.append(pltpu.make_async_copy(right_held, right_ref, small_sems.at[0]))
             stores[-1].start()
             own = ortho_ref[pl.ds(pl.multiple_of(slot_ref[0] * own_rows, own_rows), own_rows)]
             update_held[...] = jnp.dot(
                 own, cast, preferred_element_type=jnp.float32
             ).astype(jnp.bfloat16)
-            stores.append(
-                pltpu.make_async_copy(update_held, update_ref.at[:, lanes], small_sems.at[1])
-            )
+            stores.append(pltpu.make_async_copy(update_held, update_ref, small_sems.at[1]))
             stores[-1].start()
     for store in stores:
         store.wait()
 
 
-def finish(core, slot, tiles, ortho, merged, parts, begun=()):
+def finish(slot, tiles, ortho, merged, parts):
     rows, columns = merged.shape
     rank = ortho.shape[1]
-    half = columns // 2
     return pl.pallas_call(
-        functools.partial(finish_kernel, bool(begun)),
-        in_specs=[SCALAR, SCALAR, WHOLE, WHOLE, WHOLE] + [ANYWHERE] * len(begun),
+        finish_kernel,
+        in_specs=[SCALAR, WHOLE, WHOLE, WHOLE],
         out_specs=[ANYWHERE, ANYWHERE, ANYWHERE],
         out_shape=[
             pltpu.HBM((rows // parts, columns), jnp.bfloat16),
             pltpu.HBM((rank, columns), jnp.float32),
             pltpu.HBM(merged.shape, jnp.bfloat16),
         ],
-        input_output_aliases={5 + i: i for i in range(len(begun))},
         scratch_shapes=[
-            pltpu.VMEM((rank, half), jnp.bfloat16),
-            pltpu.VMEM((rows // parts, half), jnp.bfloat16),
-            pltpu.VMEM((rank, half), jnp.float32),
-            pltpu.VMEM((rows, half), jnp.bfloat16),
+            pltpu.VMEM((rank, columns), jnp.bfloat16),
+            pltpu.VMEM((rows // parts, columns), jnp.bfloat16),
+            pltpu.VMEM((rank, columns), jnp.float32),
+            pltpu.VMEM((rows, columns), jnp.bfloat16),
             pltpu.SemaphoreType.DMA((2,)),
             pltpu.SemaphoreType.DMA((rows // FINISH_CHUNK,)),
         ],
         compiler_params=pltpu.CompilerParams(vmem_limit_bytes=SMALL_LIMIT),
         cost_estimate=pl.CostEstimate(
-            flops=rows * columns * rank, bytes_accessed=2 * rows * columns, transcendentals=0
+            flops=2 * rows * columns * rank, bytes_accessed=4 * rows * columns, transcendentals=0
         ),
-    )(core, slot, tiles, ortho, merged, *begun)
+    )(slot, tiles, ortho, merged)
 
 
 def swap_cores(value):
@@ -296,37 +281,33 @@
 
 def per_device(grads, errors, q_prev):
     core = lax.axis_index("core").astype(jnp.int32).reshape(1)
-    slot = lax.axis_index(("y", "x", "core")).astype(jnp.int32).reshape(1)
+    slot = lax.axis_index(DP).astype(jnp.int32).reshape(1)
     pairs = lax.axis_size("y") * lax.axis_size("x")
     depth = lax.axis_size("z")
     replicas = 2 * pairs
 
     core, slot, prior = lax.optimization_barrier((core, slot, q_prev.T))
-    merged, keep, give = merge(core, grads[0], errors[0], prior)
-    mine = added(exchange(keep + swap_cores(give), YX))
+    merged, left = merge(grads[0], errors[0], prior)
+    mine = added(exchange(left, DP))
     mine = added(exchange(spread(mine, depth), "z")) / replicas
-    half = exchange(spread(mine, pairs), YX)
-
-    ortho, give = orthonormal(core, half, swap_cores(half), merged, replicas)
+    left = exchange(spread(mine, replicas), DP)
+
+    ortho, give = orthonormal(core, left, merged, replicas)
     given = swap_cores(give)
     keep, ortho = kept_right(core, ortho, merged, replicas)
     mine = added(exchange(keep + given, YX)) / replicas
-    half = exchange(spread(mine, pairs), YX)
-
-    other = swap_cores(half)
-    begun = finish(core, slot, half, ortho, merged, replicas)
-    update, right, new_errors = finish(core, slot, other, ortho, merged, replicas, begun)
+    right = exchange(spread(mine.astype(jnp.bfloat16), replicas), DP)
+    update, right, new_errors = finish(slot, right, ortho, merged, replicas)
     return update, right.T, new_errors[None]
 
 
 def solution(mesh):
     chips = Mesh(mesh.devices.reshape(4, 4, 2, 8), ("y", "x", "core", "z"))
-    dp = ("y", "x", "core")
-    placed = (P(dp, None, "z"), P(dp, None, "z"), P("z", None))
+    placed = (P(DP, None, "z"), P(DP, None, "z"), P("z", None))
     return jax.shard_map(
         per_device,
         mesh=chips,
         in_specs=placed,
-        out_specs=(P(dp, "z"), P("z", None), P(dp, None, "z")),
+        out_specs=(P(DP, "z"), P("z", None), P(DP, None, "z")),
         check_vma=False,
     )

time: 82.1 us -> 81 us (0.987)
  blocking collectives: 57.1 us -> 69.5 us
  starting transfers between devices: 11 us -> 0.32 us
  waiting for transfers between devices: 2.67 us -> 0.82 us
  Pallas kernels: 10.3 us -> 9.25 us
    all_to_all x5, blocking collectives: 57.1 us -> 69.5 us  [exchange(): return lax.all_to_all(value, axes, 0, 0)]
    ppermute x4 -> x1, starting transfers between devices: 11 us -> 0.32 us  [swap_cores(): return lax.ppermute(value, 'core', [(0, 1), (1, 0)])]
    ppermute x4 -> x1, waiting for transfers between devices: 2.67 us -> 0.82 us  [swap_cores(): return lax.ppermute(value, 'core', [(0, 1), (1, 0)])]
    pallas_call x4 -> x3, Pallas kernels: 9.92 us -> 8.87 us  [the longest x1 3.67 us: merge(): pl.pallas_call(merge_kernel, in_specs=[ANYWHERE, ANYWHERE, ANYWHERE], out...]
  transfers between devices with their start and end apart: 4 -> 1, of which waited for: 3 -> 1; matrix products, arithmetic and copies ran while one was open for 0% -> 0% of each run, Pallas kernels for 2% -> 0%
where the time goes in v9:
time: 81 us; the launch traced here: 80.7 us
  blocking collectives  69.5 us (86%)
  Pallas kernels  9.25 us (11%)
  waiting for transfers between devices  0.82 us (1%)
    all_to_all x5, blocking collectives, exchange(): return lax.all_to_all(value, axes, 0, 0)  69.5 us
    pallas_call x1, Pallas kernels, merge(): pl.pallas_call(merge_kernel, in_specs=[ANYWHERE, ANYWHERE, ANYWHERE], out...  3.67 us
    pallas_call x1, Pallas kernels, orthonormal(): pl.pallas_call(ortho_kernel, in_specs=[SCALAR, WHOLE, WHOLE], out_specs=[...  3.19 us
    pallas_call x1, Pallas kernels, finish(): pl.pallas_call(finish_kernel, in_specs=[SCALAR, WHOLE, WHOLE, WHOLE], out...  2.01 us
  transfers between devices with their start and end apart: 1, of which 1 were waited for; matrix products, arithmetic and copies ran while one was open for 0% of the time, Pallas kernels for 0%

profile of v9, /device:TPU:1, one launch (start us, length us, event | category | flops | bytes accessed | tf_op | source)
XLA Modules:
  0.0 80.7 jit_solution(14988236380836603730)
XLA Ops:
  0.6 3.7 %shard_map.58 = (bf16[1024,1536]{1,0:T(8,128)(2,1)S(1)}, f32[32,16,128]{2,1,0:T(8,128)S(1)}) custom-call(bf16[1024,1536]{1,0:T(8,128)(2,1)} %bitcast.13, bf16[1024,1536]{1,0:T(8,128)(2,1)} %bitcast.14, f32[64,1536]{1,0:T(8,128)} %bitcast.15), custom_call_target="tpu_custom_call" | custom-call | flops 201326592 | bytes 9437184 | tf_op jit(solution)/shard_map/pallas_call | solution.py:65
  4.3 17.3 %all_to_all.25 = f32[32,16,128]{2,1,0:T(8,128)S(1)} all-to-all(f32[32,16,128]{2,1,0:T(8,128)S(1)} %get-tuple-element.18), channel_id=1, replica_groups=mesh['y'=4,'x'=4,'core'=2,'z'=8] {'y','x','core'}, dimensions={0} | all-to-all | bytes 524288 | tf_op jit(solution)/shard_map/all_to_all | solution.py:268
  21.6 15.2 %all_to_all.26 = f32[8,16,128]{2,1,0:T(8,128)S(1)} all-to-all(f32[8,16,128]{2,1,0:T(8,128)S(1)} %broadcast_in_dim.28), channel_id=1, replica_groups=mesh['y'=4,'x'=4,'core'=2,'z'=8] {'z'}, dimensions={0} | all-to-all | bytes 131072 | tf_op jit(solution)/shard_map/all_to_all | solution.py:268
  36.9 13.9 %all_to_all.27.tiles_ref = f32[32,16,128]{2,1,0:T(8,128)S(1)} all-to-all(f32[32,16,128]{2,1,0:T(8,128)S(1)} %broadcast_in_dim.30), channel_id=1, replica_groups=mesh['y'=4,'x'=4,'core'=2,'z'=8] {'y','x','core'}, dimensions={0} | all-to-all | bytes 524288 | tf_op jit(solution)/shard_map/all_to_all | solution.py:268
  50.8 3.2 %shard_map.59 = (bf16[64,1024]{1,0:T(8,128)(2,1)S(1)}, f32[16,8,384]{2,1,0:T(8,128)S(1)}) custom-call(s32[1]{0:T(128)} %bitcast.core_ref, f32[32,16,128]{2,1,0:T(8,128)S(1)} %all_to_all.27.tiles_ref, bf16[1024,1536]{1,0:T(8,128)(2,1)S(1)} %get-tuple-element.19.merged_ref), custom_call_target="tpu_custom_call" | custom-call | flops 201326592 | bytes 3145728 | tf_op jit(solution)/shard_map/pallas_call | solution.py:169
  54.0 0.3 collective-permute-start
  54.3 0.4 shard_map.60
  54.7 0.8 %collective-permute-done = f32[16,8,384]{2,1,0:T(8,128)S(1)} collective-permute-done((f32[16,8,384]{2,1,0:T(8,128)S(1)}, f32[16,8,384]{2,1,0:T(8,128)S(1)}, u32[]{:S(2)}, u32[]{:S(2)}) %collective-permute-start) | collective-permute-done | bytes 196640 | tf_op jit(solution)/shard_map/ppermute | solution.py:264
  55.5 10.4 %all_to_all.28 = f32[16,8,384]{2,1,0:T(8,128)S(1)} all-to-all(f32[16,8,384]{2,1,0:T(8,128)S(1)} %add.261), channel_id=1, replica_groups=mesh['y'=4,'x'=4,'core'=2,'z'=8] {'y','x'}, dimensions={0} | all-to-all | bytes 393216 | tf_op jit(solution)/shard_map/all_to_all | solution.py:268
  66.0 12.7 %all_to_all.29.tiles_ref = bf16[32,8,384]{2,1,0:T(8,128)(2,1)S(1)} all-to-all(bf16[32,8,384]{2,1,0:T(8,128)(2,1)S(1)} %broadcast_in_dim.32), channel_id=1, replica_groups=mesh['y'=4,'x'=4,'core'=2,'z'=8] {'y','x','core'}, dimensions={0} | all-to-all | bytes 393216 | tf_op jit(solution)/shard_map/all_to_all | solution.py:268
  78.7 2.0 %shard_map.61 = (bf16[32,1536]{1,0:T(8,128)(2,1)}, f32[64,1536]{1,0:T(8,128)}, bf16[1024,1536]{1,0:T(8,128)(2,1)}) custom-call(s32[1]{0:T(128)} %bitcast.1.slot_ref, bf16[32,8,384]{2,1,0:T(8,128)(2,1)S(1)} %all_to_all.29.tiles_ref, bf16[1024,64]{1,0:T(8,128)(2,1)S(1)} %get-tuple-element.23.ortho_ref, bf16[1024,1536]{1,0:T(8,128)(2,1)S(1)} %get-tuple-element.19.merged_ref), custom_call_target="tpu_custom_call" | custom-call | flops 201326592 | bytes 6291456 | tf_op jit(solution)/shard_map/pallas_call | solution.py:239
  (7 shorter events, 0.1 us)
Async XLA Ops:
  54.0 1.5 %collective-permute-start = (f32[16,8,384]{2,1,0:T(8,128)S(1)}, f32[16,8,384]{2,1,0:T(8,128)S(1)}, u32[]{:S(2)}, u32[]{:S(2)}) collective-permute-start(f32[16,8,384]{2,1,0:T(8,128)S(1)} %get-tuple-element.22), channel_id=1, source_target_pairs={{0,8},{8,0},{1,9},{9,1},{2,10},{10,2},{3,11},{11,3},{4,12},{12,4},... | collective-permute-start | bytes 589832 | tf_op jit(solution)/shard_map/ppermute | solution.py:264

commit v10 on v9

--- a/solution.py
+++ b/solution.py
@@ -12,7 +12,6 @@
 VMEM_LIMIT = 32 * 1024 * 1024
 SMALL_LIMIT = 16 * 1024 * 1024
 WHOLE = pl.BlockSpec(memory_space=pltpu.VMEM)
-SCALAR = pl.BlockSpec(memory_space=pltpu.SMEM)
 ANYWHERE = pl.BlockSpec(memory_space=pl.ANY)
 MERGE_CHUNK = 512
 FINISH_CHUNK = 128
@@ -120,7 +119,9 @@
         groups[own] = rows[0]
         for j in range(1, GROUP):
             groups[own] = jnp.where(place == j, rows[j], groups[own])
-    return jnp.concatenate(groups)[:, rank:]
+        half = rank // GROUP // 2
+        if (own + 1) % half == 0:
+            yield jnp.concatenate(groups[own + 1 - half : own + 1])[:, rank:]
 
 
 def right_tiles(ortho, merged_ref, half, tiles_ref):
@@ -135,8 +136,7 @@
             tiles_ref[down * count + lane] = right[8 * down : 8 * down + 8]
 
 
-def ortho_kernel(core_ref, tiles_ref, merged_ref, ortho_ref, give_ref, left_ref):
-    core = core_ref[0]
+def ortho_kernel(tiles_ref, merged_ref, ortho_ref, give_ref, left_ref):
     rank, rows = left_ref.shape
     across = rows // 128
     for place in range(tiles_ref.shape[0]):
@@ -147,28 +147,30 @@
         left, left, (((1,), (1,)), ((), ())), precision=lax.Precision.HIGHEST,
         preferred_element_type=jnp.float32,
     )
-    ortho = jnp.dot(
-        inverse_factor(gram), left, precision=lax.Precision.HIGHEST,
-        preferred_element_type=jnp.float32,
-    ).astype(jnp.bfloat16)
+    ortho = jnp.concatenate([
+        jnp.dot(
+            inverse, left, precision=lax.Precision.HIGHEST, preferred_element_type=jnp.float32
+        ).astype(jnp.bfloat16)
+        for inverse in inverse_factor(gram)
+    ])
     ortho_ref[...] = ortho
-    right_tiles(ortho, merged_ref, 1 - core, give_ref)
-
-
-def keep_kernel(core_ref, ortho_ref, merged_ref, keep_ref, turned_ref):
+    right_tiles(ortho, merged_ref, 1 - lax.axis_index("core"), give_ref)
+
+
+def keep_kernel(ortho_ref, merged_ref, keep_ref, turned_ref):
     ortho = ortho_ref[...]
-    right_tiles(ortho, merged_ref, core_ref[0], keep_ref)
+    right_tiles(ortho, merged_ref, lax.axis_index("core"), keep_ref)
     turned_ref[...] = ortho.T
 
 
-def orthonormal(core, left, merged, parts):
+def orthonormal(left, merged, parts):
     rows, columns = merged.shape
     rank = left.size // rows
     wide = rank * columns // (8 * parts)
     tiles = jax.ShapeDtypeStruct((parts // 2, 8, wide), jnp.float32)
     return pl.pallas_call(
         ortho_kernel,
-        in_specs=[SCALAR, WHOLE, WHOLE],
+        in_specs=[WHOLE, WHOLE],
         out_specs=[WHOLE, WHOLE],
         out_shape=[pltpu.VMEM((rank, rows), jnp.bfloat16), tiles],
         scratch_shapes=[pltpu.VMEM((rank, rows), jnp.float32)],
@@ -176,26 +178,26 @@
         cost_estimate=pl.CostEstimate(
             flops=2 * rows * columns * rank, bytes_accessed=2 * rows * columns, transcendentals=0
         ),
-    )(core, left, merged)
-
-
-def kept_right(core, ortho, merged, parts):
+    )(left, merged)
+
+
+def kept_right(ortho, merged, parts):
     rank, rows = ortho.shape
     columns = merged.shape[1]
     tiles = jax.ShapeDtypeStruct((parts // 2, 8, rank * columns // (8 * parts)), jnp.float32)
     return pl.pallas_call(
         keep_kernel,
-        in_specs=[SCALAR, WHOLE, WHOLE],
+        in_specs=[WHOLE, WHOLE],
         out_specs=[WHOLE, WHOLE],
         out_shape=[tiles, pltpu.VMEM((rows, rank), jnp.bfloat16)],
         compiler_params=pltpu.CompilerParams(vmem_limit_bytes=SMALL_LIMIT),
         cost_estimate=pl.CostEstimate(
             flops=rows * columns * rank, bytes_accessed=rows * columns, transcendentals=0
         ),
-    )(core, ortho, merged)
-
-
-def finish_kernel(slot_ref, tiles_ref, ortho_ref, merged_ref, update_ref, right_ref, errors_ref,
+    )(ortho, merged)
+
+
+def finish_kernel(tiles_ref, ortho_ref, merged_ref, update_ref, right_ref, errors_ref,
                   cast_ref, update_held, right_held, errors_held, small_sems, sems):
     own_rows = update_held.shape[0]
     rank, columns = right_held.shape
@@ -223,7 +225,7 @@
         if i == 0:
             stores.append(pltpu.make_async_copy(right_held, right_ref, small_sems.at[0]))
             stores[-1].start()
-            own = ortho_ref[pl.ds(pl.multiple_of(slot_ref[0] * own_rows, own_rows), own_rows)]
+            own = ortho_ref[pl.ds(pl.multiple_of(lax.axis_index(DP) * own_rows, own_rows), own_rows)]
             update_held[...] = jnp.dot(
                 own, cast, preferred_element_type=jnp.float32
             ).astype(jnp.bfloat16)
@@ -233,12 +235,12 @@
         store.wait()
 
 
-def finish(slot, tiles, ortho, merged, parts):
+def finish(tiles, ortho, merged, parts):
     rows, columns = merged.shape
     rank = ortho.shape[1]
     return pl.pallas_call(
         finish_kernel,
-        in_specs=[SCALAR, WHOLE, WHOLE, WHOLE],
+        in_specs=[WHOLE, WHOLE, WHOLE],
         out_specs=[ANYWHERE, ANYWHERE, ANYWHERE],
         out_shape=[
             pltpu.HBM((rows // parts, columns), jnp.bfloat16),
@@ -257,7 +259,7 @@
         cost_estimate=pl.CostEstimate(
             flops=2 * rows * columns * rank, bytes_accessed=4 * rows * columns, transcendentals=0
         ),
-    )(slot, tiles, ortho, merged)
+    )(tiles, ortho, merged)
 
 
 def swap_cores(value):
@@ -280,24 +282,21 @@
 
 
 def per_device(grads, errors, q_prev):
-    core = lax.axis_index("core").astype(jnp.int32).reshape(1)
-    slot = lax.axis_index(DP).astype(jnp.int32).reshape(1)
     pairs = lax.axis_size("y") * lax.axis_size("x")
     depth = lax.axis_size("z")
     replicas = 2 * pairs
 
-    core, slot, prior = lax.optimization_barrier((core, slot, q_prev.T))
-    merged, left = merge(grads[0], errors[0], prior)
+    merged, left = merge(grads[0], errors[0], q_prev.T)
     mine = added(exchange(left, DP))
     mine = added(exchange(spread(mine, depth), "z")) / replicas
     left = exchange(spread(mine, replicas), DP)
 
-    ortho, give = orthonormal(core, left, merged, replicas)
+    ortho, give = orthonormal(left, merged, replicas)
     given = swap_cores(give)
-    keep, ortho = kept_right(core, ortho, merged, replicas)
+    keep, ortho = kept_right(ortho, merged, replicas)
     mine = added(exchange(keep + given, YX)) / replicas
     right = exchange(spread(mine.astype(jnp.bfloat16), replicas), DP)
-    update, right, new_errors = finish(slot, right, ortho, merged, replicas)
+    update, right, new_errors = finish(right, ortho, merged, replicas)
     return update, right.T, new_errors[None]
 
 

time: 81 us -> 80.8 us (level)
  no operation moved by 1% of the time
where the time goes in v10:
time: 80.8 us; the launch traced here: 80.5 us
  blocking collectives  69.6 us (86%)
  Pallas kernels  9.05 us (11%)
  waiting for transfers between devices  0.81 us (1%)
    all_to_all x5, blocking collectives, exchange(): return lax.all_to_all(value, axes, 0, 0)  69.6 us
    pallas_call x1, Pallas kernels, merge(): pl.pallas_call(merge_kernel, in_specs=[ANYWHERE, ANYWHERE, ANYWHERE], out...  3.66 us
    pallas_call x1, Pallas kernels, orthonormal(): pl.pallas_call(ortho_kernel, in_specs=[WHOLE, WHOLE], out_specs=[WHOLE, W...  2.99 us
    pallas_call x1, Pallas kernels, finish(): pl.pallas_call(finish_kernel, in_specs=[WHOLE, WHOLE, WHOLE], out_specs=[...  2.02 us
  transfers between devices with their start and end apart: 1, of which 1 were waited for; matrix products, arithmetic and copies ran while one was open for 0% of the time, Pallas kernels for 0%

profile of v10, /device:TPU:1, one launch (start us, length us, event | category | flops | bytes accessed | tf_op | source)
XLA Modules:
  0.0 80.5 jit_solution(4189485979558495214)
XLA Ops:
  0.6 3.7 %shard_map.58 = (bf16[1024,1536]{1,0:T(8,128)(2,1)S(1)}, f32[32,16,128]{2,1,0:T(8,128)S(1)}) custom-call(bf16[1024,1536]{1,0:T(8,128)(2,1)} %bitcast.11, bf16[1024,1536]{1,0:T(8,128)(2,1)} %bitcast.12, f32[64,1536]{1,0:T(8,128)} %bitcast.13), custom_call_target="tpu_custom_call" | custom-call | flops 201326592 | bytes 9437184 | tf_op jit(solution)/shard_map/pallas_call | solution.py:64
  4.3 17.3 %all_to_all.25 = f32[32,16,128]{2,1,0:T(8,128)S(1)} all-to-all(f32[32,16,128]{2,1,0:T(8,128)S(1)} %get-tuple-element.12), channel_id=1, replica_groups=mesh['y'=4,'x'=4,'core'=2,'z'=8] {'y','x','core'}, dimensions={0} | all-to-all | bytes 524288 | tf_op jit(solution)/shard_map/all_to_all | solution.py:270
  21.6 15.2 %all_to_all.26 = f32[8,16,128]{2,1,0:T(8,128)S(1)} all-to-all(f32[8,16,128]{2,1,0:T(8,128)S(1)} %broadcast_in_dim.28), channel_id=1, replica_groups=mesh['y'=4,'x'=4,'core'=2,'z'=8] {'z'}, dimensions={0} | all-to-all | bytes 131072 | tf_op jit(solution)/shard_map/all_to_all | solution.py:270
  36.9 13.9 %all_to_all.27.tiles_ref = f32[32,16,128]{2,1,0:T(8,128)S(1)} all-to-all(f32[32,16,128]{2,1,0:T(8,128)S(1)} %broadcast_in_dim.30), channel_id=1, replica_groups=mesh['y'=4,'x'=4,'core'=2,'z'=8] {'y','x','core'}, dimensions={0} | all-to-all | bytes 524288 | tf_op jit(solution)/shard_map/all_to_all | solution.py:270
  50.8 3.0 %shard_map.59 = (bf16[64,1024]{1,0:T(8,128)(2,1)S(1)}, f32[16,8,384]{2,1,0:T(8,128)S(1)}) custom-call(f32[32,16,128]{2,1,0:T(8,128)S(1)} %all_to_all.27.tiles_ref, bf16[1024,1536]{1,0:T(8,128)(2,1)S(1)} %get-tuple-element.13.merged_ref), custom_call_target="tpu_custom_call" | custom-call | flops 201326592 | bytes 3145728 | tf_op jit(solution)/shard_map/pallas_call | solution.py:171
  53.8 0.3 collective-permute-start
  54.1 0.4 shard_map.60
  54.5 0.8 %collective-permute-done = f32[16,8,384]{2,1,0:T(8,128)S(1)} collective-permute-done((f32[16,8,384]{2,1,0:T(8,128)S(1)}, f32[16,8,384]{2,1,0:T(8,128)S(1)}, u32[]{:S(2)}, u32[]{:S(2)}) %collective-permute-start) | collective-permute-done | bytes 196640 | tf_op jit(solution)/shard_map/ppermute | solution.py:266
  55.3 10.4 %all_to_all.28 = f32[16,8,384]{2,1,0:T(8,128)S(1)} all-to-all(f32[16,8,384]{2,1,0:T(8,128)S(1)} %add.253), channel_id=1, replica_groups=mesh['y'=4,'x'=4,'core'=2,'z'=8] {'y','x'}, dimensions={0} | all-to-all | bytes 393216 | tf_op jit(solution)/shard_map/all_to_all | solution.py:270
  65.8 12.7 %all_to_all.29.tiles_ref = bf16[32,8,384]{2,1,0:T(8,128)(2,1)S(1)} all-to-all(bf16[32,8,384]{2,1,0:T(8,128)(2,1)S(1)} %broadcast_in_dim.32), channel_id=1, replica_groups=mesh['y'=4,'x'=4,'core'=2,'z'=8] {'y','x','core'}, dimensions={0} | all-to-all | bytes 393216 | tf_op jit(solution)/shard_map/all_to_all | solution.py:270
  78.5 2.0 %shard_map.61 = (bf16[32,1536]{1,0:T(8,128)(2,1)}, f32[64,1536]{1,0:T(8,128)}, bf16[1024,1536]{1,0:T(8,128)(2,1)}) custom-call(bf16[32,8,384]{2,1,0:T(8,128)(2,1)S(1)} %all_to_all.29.tiles_ref, bf16[1024,64]{1,0:T(8,128)(2,1)S(1)} %get-tuple-element.17.ortho_ref, bf16[1024,1536]{1,0:T(8,128)(2,1)S(1)} %get-tuple-element.13.merged_ref), custom_call_target="tpu_custom_call" | custom-call | flops 201326592 | bytes 6291456 | tf_op jit(solution)/shard_map/pallas_call | solution.py:241
  (7 shorter events, 0.1 us)
Async XLA Ops:
  53.8 1.5 %collective-permute-start = (f32[16,8,384]{2,1,0:T(8,128)S(1)}, f32[16,8,384]{2,1,0:T(8,128)S(1)}, u32[]{:S(2)}, u32[]{:S(2)}) collective-permute-start(f32[16,8,384]{2,1,0:T(8,128)S(1)} %get-tuple-element.16), channel_id=1, source_target_pairs={{0,8},{8,0},{1,9},{9,1},{2,10},{10,2},{3,11},{11,3},{4,12},{12,4},... | collective-permute-start | bytes 589832 | tf_op jit(solution)/shard_map/ppermute | solution.py:266

commit v11 on v10

--- a/solution.py
+++ b/solution.py
@@ -9,6 +9,7 @@
 
 YX = ("y", "x")
 DP = ("y", "x", "core")
+ALL = ("core", "y", "x")
 VMEM_LIMIT = 32 * 1024 * 1024
 SMALL_LIMIT = 16 * 1024 * 1024
 WHOLE = pl.BlockSpec(memory_space=pltpu.VMEM)
@@ -204,7 +205,7 @@
     wide = tiles_ref.shape[2]
     count = columns // (2 * wide)
     for place in range(tiles_ref.shape[0]):
-        spot, half = divmod(place, 2)
+        half, spot = divmod(place, tiles_ref.shape[0] // 2)
         down, lane = spot // count, half * count + spot % count
         right_held[8 * down : 8 * down + 8, wide * lane : wide * lane + wide] = (
             tiles_ref[place].astype(jnp.float32)
@@ -287,15 +288,15 @@
     replicas = 2 * pairs
 
     merged, left = merge(grads[0], errors[0], q_prev.T)
-    mine = added(exchange(left, DP))
+    mine = added(exchange(left, ALL))
     mine = added(exchange(spread(mine, depth), "z")) / replicas
-    left = exchange(spread(mine, replicas), DP)
+    left = exchange(spread(mine, replicas), ALL)
 
     ortho, give = orthonormal(left, merged, replicas)
     given = swap_cores(give)
     keep, ortho = kept_right(ortho, merged, replicas)
     mine = added(exchange(keep + given, YX)) / replicas
-    right = exchange(spread(mine.astype(jnp.bfloat16), replicas), DP)
+    right = exchange(spread(mine.astype(jnp.bfloat16), replicas), ALL)
     update, right, new_errors = finish(right, ortho, merged, replicas)
     return update, right.T, new_errors[None]
 

time: 80.8 us -> 80.5 us (level)
  blocking collectives: 69.6 us -> 68.6 us
  starting transfers between devices: 0.33 us -> 1.18 us
    all_to_all x5, blocking collectives: 69.6 us -> 68.6 us  [exchange(): return lax.all_to_all(value, axes, 0, 0)]
    ppermute x1, starting transfers between devices: 0.33 us -> 1.18 us  [swap_cores(): return lax.ppermute(value, 'core', [(0, 1), (1, 0)])]
where the time goes in v11:
time: 80.5 us; the launch traced here: 80.3 us
  blocking collectives  68.6 us (85%)
  Pallas kernels  9.05 us (11%)
  starting transfers between devices  1.18 us (1%)
    all_to_all x5, blocking collectives, exchange(): return lax.all_to_all(value, axes, 0, 0)  68.6 us
    pallas_call x1, Pallas kernels, merge(): pl.pallas_call(merge_kernel, in_specs=[ANYWHERE, ANYWHERE, ANYWHERE], out...  3.66 us
    pallas_call x1, Pallas kernels, orthonormal(): pl.pallas_call(ortho_kernel, in_specs=[WHOLE, WHOLE], out_specs=[WHOLE, W...  2.99 us
    pallas_call x1, Pallas kernels, finish(): pl.pallas_call(finish_kernel, in_specs=[WHOLE, WHOLE, WHOLE], out_specs=[...  2.02 us
  transfers between devices with their start and end apart: 1, of which 1 were waited for; matrix products, arithmetic and copies ran while one was open for 0% of the time, Pallas kernels for 0%

profile of v11, /device:TPU:1, one launch (start us, length us, event | category | flops | bytes accessed | tf_op | source)
XLA Modules:
  0.0 80.3 jit_solution(10272880512661941755)
XLA Ops:
  0.6 3.7 %shard_map.58 = (bf16[1024,1536]{1,0:T(8,128)(2,1)S(1)}, f32[32,16,128]{2,1,0:T(8,128)S(1)}) custom-call(bf16[1024,1536]{1,0:T(8,128)(2,1)} %bitcast.11, bf16[1024,1536]{1,0:T(8,128)(2,1)} %bitcast.12, f32[64,1536]{1,0:T(8,128)} %bitcast.13), custom_call_target="tpu_custom_call" | custom-call | flops 201326592 | bytes 9437184 | tf_op jit(solution)/shard_map/pallas_call | solution.py:65
  4.3 16.7 %all_to_all.25 = f32[32,16,128]{2,1,0:T(8,128)S(1)} all-to-all(f32[32,16,128]{2,1,0:T(8,128)S(1)} %get-tuple-element.12), channel_id=1, replica_groups=mesh['y'=4,'x'=4,'core'=2,'z'=8] {'core','y','x'}, dimensions={0} | all-to-all | bytes 524288 | tf_op jit(solution)/shard_map/all_to_all | solution.py:271
  21.0 15.2 %all_to_all.26 = f32[8,16,128]{2,1,0:T(8,128)S(1)} all-to-all(f32[8,16,128]{2,1,0:T(8,128)S(1)} %broadcast_in_dim.28), channel_id=1, replica_groups=mesh['y'=4,'x'=4,'core'=2,'z'=8] {'z'}, dimensions={0} | all-to-all | bytes 131072 | tf_op jit(solution)/shard_map/all_to_all | solution.py:271
  36.3 13.8 %all_to_all.27.tiles_ref = f32[32,16,128]{2,1,0:T(8,128)S(1)} all-to-all(f32[32,16,128]{2,1,0:T(8,128)S(1)} %broadcast_in_dim.30), channel_id=1, replica_groups=mesh['y'=4,'x'=4,'core'=2,'z'=8] {'core','y','x'}, dimensions={0} | all-to-all | bytes 524288 | tf_op jit(solution)/shard_map/all_to_all | solution.py:271
  50.1 3.0 %shard_map.59 = (bf16[64,1024]{1,0:T(8,128)(2,1)S(1)}, f32[16,8,384]{2,1,0:T(8,128)S(1)}) custom-call(f32[32,16,128]{2,1,0:T(8,128)S(1)} %all_to_all.27.tiles_ref, bf16[1024,1536]{1,0:T(8,128)(2,1)S(1)} %get-tuple-element.13.merged_ref), custom_call_target="tpu_custom_call" | custom-call | flops 201326592 | bytes 3145728 | tf_op jit(solution)/shard_map/pallas_call | solution.py:172
  53.1 1.2 %collective-permute-start = (f32[16,8,384]{2,1,0:T(8,128)S(1)}, f32[16,8,384]{2,1,0:T(8,128)S(1)}, u32[]{:S(2)}, u32[]{:S(2)}) collective-permute-start(f32[16,8,384]{2,1,0:T(8,128)S(1)} %get-tuple-element.16), channel_id=1, source_target_pairs={{0,8},{8,0},{1,9},{9,1},{2,10},{10,2},{3,11},{11,3},{4,12},{12,4},... | collective-permute-start | bytes 589832 | tf_op jit(solution)/shard_map/ppermute | solution.py:267
  54.3 0.4 shard_map.60
  54.7 0.7 collective-permute-done
  55.4 9.9 %all_to_all.28 = f32[16,8,384]{2,1,0:T(8,128)S(1)} all-to-all(f32[16,8,384]{2,1,0:T(8,128)S(1)} %add.253), channel_id=1, replica_groups=mesh['y'=4,'x'=4,'core'=2,'z'=8] {'y','x'}, dimensions={0} | all-to-all | bytes 393216 | tf_op jit(solution)/shard_map/all_to_all | solution.py:271
  65.3 12.9 %all_to_all.29.tiles_ref = bf16[32,8,384]{2,1,0:T(8,128)(2,1)S(1)} all-to-all(bf16[32,8,384]{2,1,0:T(8,128)(2,1)S(1)} %broadcast_in_dim.32), channel_id=1, replica_groups=mesh['y'=4,'x'=4,'core'=2,'z'=8] {'core','y','x'}, dimensions={0} | all-to-all | bytes 393216 | tf_op jit(solution)/shard_map/all_to_all | solution.py:271
  78.2 2.0 %shard_map.61 = (bf16[32,1536]{1,0:T(8,128)(2,1)}, f32[64,1536]{1,0:T(8,128)}, bf16[1024,1536]{1,0:T(8,128)(2,1)}) custom-call(bf16[32,8,384]{2,1,0:T(8,128)(2,1)S(1)} %all_to_all.29.tiles_ref, bf16[1024,64]{1,0:T(8,128)(2,1)S(1)} %get-tuple-element.17.ortho_ref, bf16[1024,1536]{1,0:T(8,128)(2,1)S(1)} %get-tuple-element.13.merged_ref), custom_call_target="tpu_custom_call" | custom-call | flops 201326592 | bytes 6291456 | tf_op jit(solution)/shard_map/pallas_call | solution.py:242
  (7 shorter events, 0.1 us)
Async XLA Ops:
  53.1 2.3 %collective-permute-start = (f32[16,8,384]{2,1,0:T(8,128)S(1)}, f32[16,8,384]{2,1,0:T(8,128)S(1)}, u32[]{:S(2)}, u32[]{:S(2)}) collective-permute-start(f32[16,8,384]{2,1,0:T(8,128)S(1)} %get-tuple-element.16), channel_id=1, source_target_pairs={{0,8},{8,0},{1,9},{9,1},{2,10},{10,2},{3,11},{11,3},{4,12},{12,4},... | collective-permute-start | bytes 589832 | tf_op jit(solution)/shard_map/ppermute | solution.py:267

commit v12 on v11

--- a/solution.py
+++ b/solution.py
@@ -120,9 +120,9 @@
         groups[own] = rows[0]
         for j in range(1, GROUP):
             groups[own] = jnp.where(place == j, rows[j], groups[own])
-        half = rank // GROUP // 2
-        if (own + 1) % half == 0:
-            yield jnp.concatenate(groups[own + 1 - half : own + 1])[:, rank:]
+        part = rank // GROUP // 4
+        if (own + 1) % part == 0:
+            yield jnp.concatenate(groups[own + 1 - part : own + 1])[:, rank:]
 
 
 def right_tiles(ortho, merged_ref, half, tiles_ref):

time: 80.5 us -> 80.4 us (level)
  no operation moved by 1% of the time
where the time goes in v12:
time: 80.4 us; the launch traced here: 80.2 us
  blocking collectives  68.6 us (85%)
  Pallas kernels  8.98 us (11%)
  starting transfers between devices  1.17 us (1%)
    all_to_all x5, blocking collectives, exchange(): return lax.all_to_all(value, axes, 0, 0)  68.6 us
    pallas_call x1, Pallas kernels, merge(): pl.pallas_call(merge_kernel, in_specs=[ANYWHERE, ANYWHERE, ANYWHERE], out...  3.66 us
    pallas_call x1, Pallas kernels, orthonormal(): pl.pallas_call(ortho_kernel, in_specs=[WHOLE, WHOLE], out_specs=[WHOLE, W...  2.92 us
    pallas_call x1, Pallas kernels, finish(): pl.pallas_call(finish_kernel, in_specs=[WHOLE, WHOLE, WHOLE], out_specs=[...  2.01 us
  transfers between devices with their start and end apart: 1, of which 1 were waited for; matrix products, arithmetic and copies ran while one was open for 0% of the time, Pallas kernels for 0%

profile of v12, /device:TPU:1, one launch (start us, length us, event | category | flops | bytes accessed | tf_op | source)
XLA Modules:
  0.0 80.2 jit_solution(2083813921239170197)
XLA Ops:
  0.6 3.7 %shard_map.58 = (bf16[1024,1536]{1,0:T(8,128)(2,1)S(1)}, f32[32,16,128]{2,1,0:T(8,128)S(1)}) custom-call(bf16[1024,1536]{1,0:T(8,128)(2,1)} %bitcast.11, bf16[1024,1536]{1,0:T(8,128)(2,1)} %bitcast.12, f32[64,1536]{1,0:T(8,128)} %bitcast.13), custom_call_target="tpu_custom_call" | custom-call | flops 201326592 | bytes 9437184 | tf_op jit(solution)/shard_map/pallas_call | solution.py:65
  4.3 16.7 %all_to_all.25 = f32[32,16,128]{2,1,0:T(8,128)S(1)} all-to-all(f32[32,16,128]{2,1,0:T(8,128)S(1)} %get-tuple-element.12), channel_id=1, replica_groups=mesh['y'=4,'x'=4,'core'=2,'z'=8] {'core','y','x'}, dimensions={0} | all-to-all | bytes 524288 | tf_op jit(solution)/shard_map/all_to_all | solution.py:271
  21.0 15.2 %all_to_all.26 = f32[8,16,128]{2,1,0:T(8,128)S(1)} all-to-all(f32[8,16,128]{2,1,0:T(8,128)S(1)} %broadcast_in_dim.28), channel_id=1, replica_groups=mesh['y'=4,'x'=4,'core'=2,'z'=8] {'z'}, dimensions={0} | all-to-all | bytes 131072 | tf_op jit(solution)/shard_map/all_to_all | solution.py:271
  36.3 13.8 %all_to_all.27.tiles_ref = f32[32,16,128]{2,1,0:T(8,128)S(1)} all-to-all(f32[32,16,128]{2,1,0:T(8,128)S(1)} %broadcast_in_dim.30), channel_id=1, replica_groups=mesh['y'=4,'x'=4,'core'=2,'z'=8] {'core','y','x'}, dimensions={0} | all-to-all | bytes 524288 | tf_op jit(solution)/shard_map/all_to_all | solution.py:271
  50.1 2.9 %shard_map.59 = (bf16[64,1024]{1,0:T(8,128)(2,1)S(1)}, f32[16,8,384]{2,1,0:T(8,128)S(1)}) custom-call(f32[32,16,128]{2,1,0:T(8,128)S(1)} %all_to_all.27.tiles_ref, bf16[1024,1536]{1,0:T(8,128)(2,1)S(1)} %get-tuple-element.13.merged_ref), custom_call_target="tpu_custom_call" | custom-call | flops 201326592 | bytes 3145728 | tf_op jit(solution)/shard_map/pallas_call | solution.py:172
  53.0 1.2 %collective-permute-start = (f32[16,8,384]{2,1,0:T(8,128)S(1)}, f32[16,8,384]{2,1,0:T(8,128)S(1)}, u32[]{:S(2)}, u32[]{:S(2)}) collective-permute-start(f32[16,8,384]{2,1,0:T(8,128)S(1)} %get-tuple-element.16), channel_id=1, source_target_pairs={{0,8},{8,0},{1,9},{9,1},{2,10},{10,2},{3,11},{11,3},{4,12},{12,4},... | collective-permute-start | bytes 589832 | tf_op jit(solution)/shard_map/ppermute | solution.py:267
  54.2 0.4 shard_map.60
  54.6 0.7 collective-permute-done
  55.3 10.2 %all_to_all.28 = f32[16,8,384]{2,1,0:T(8,128)S(1)} all-to-all(f32[16,8,384]{2,1,0:T(8,128)S(1)} %add.253), channel_id=1, replica_groups=mesh['y'=4,'x'=4,'core'=2,'z'=8] {'y','x'}, dimensions={0} | all-to-all | bytes 393216 | tf_op jit(solution)/shard_map/all_to_all | solution.py:271
  65.6 12.6 %all_to_all.29.tiles_ref = bf16[32,8,384]{2,1,0:T(8,128)(2,1)S(1)} all-to-all(bf16[32,8,384]{2,1,0:T(8,128)(2,1)S(1)} %broadcast_in_dim.32), channel_id=1, replica_groups=mesh['y'=4,'x'=4,'core'=2,'z'=8] {'core','y','x'}, dimensions={0} | all-to-all | bytes 393216 | tf_op jit(solution)/shard_map/all_to_all | solution.py:271
  78.2 2.0 %shard_map.61 = (bf16[32,1536]{1,0:T(8,128)(2,1)}, f32[64,1536]{1,0:T(8,128)}, bf16[1024,1536]{1,0:T(8,128)(2,1)}) custom-call(bf16[32,8,384]{2,1,0:T(8,128)(2,1)S(1)} %all_to_all.29.tiles_ref, bf16[1024,64]{1,0:T(8,128)(2,1)S(1)} %get-tuple-element.17.ortho_ref, bf16[1024,1536]{1,0:T(8,128)(2,1)S(1)} %get-tuple-element.13.merged_ref), custom_call_target="tpu_custom_call" | custom-call | flops 201326592 | bytes 6291456 | tf_op jit(solution)/shard_map/pallas_call | solution.py:242
  (7 shorter events, 0.1 us)
Async XLA Ops:
  53.0 2.2 %collective-permute-start = (f32[16,8,384]{2,1,0:T(8,128)S(1)}, f32[16,8,384]{2,1,0:T(8,128)S(1)}, u32[]{:S(2)}, u32[]{:S(2)}) collective-permute-start(f32[16,8,384]{2,1,0:T(8,128)S(1)} %get-tuple-element.16), channel_id=1, source_target_pairs={{0,8},{8,0},{1,9},{9,1},{2,10},{10,2},{3,11},{11,3},{4,12},{12,4},... | collective-permute-start | bytes 589832 | tf_op jit(solution)/shard_map/ppermute | solution.py:267
